TPU v7x, 32 devices: a whole 2x2x4 slice. The times are simulated.
32 devices in a mesh: section: 2 (over x), wide: 8 (over z, y), tp: 2 (over core).
Axes of the slice: x: 2, y: 2, z: 4, core: 2. Of those that a mesh axis runs over, the one named last changes fastest.
Arguments:
- tokens: bfloat16 [2, 4096, 2048], P(None, ('wide', 'tp')), may hold values from -6 to 6
- out_grad: bfloat16 [2, 4096, 2048], P(None, ('wide', 'tp')), may hold values from -6 to 6
- attn_gain: bfloat16 [2, 2048], P('section', 'wide'), may hold values from 0.25 to 1.75
- w_query: bfloat16 [2, 2048, 2048], P('section', 'wide', 'tp'), may hold values from -0.125 to 0.125
- w_key: bfloat16 [2, 2048, 256], P('section', 'wide', 'tp'), may hold values from -0.125 to 0.125
- w_value: bfloat16 [2, 2048, 256], P('section', 'wide', 'tp'), may hold values from -0.125 to 0.125
- w_out: bfloat16 [2, 2048, 2048], P('section', 'tp', 'wide'), may hold values from -2 to 2
- ffn_gain: bfloat16 [2, 2048], P('section', 'wide'), may hold values from 0.25 to 1.75
- w_gate: bfloat16 [2, 2048, 5632], P('section', 'wide', 'tp'), may hold values from -0.125 to 0.125
- w_up: bfloat16 [2, 2048, 5632], P('section', 'wide', 'tp'), may hold values from -0.125 to 0.125
- w_down: bfloat16 [2, 5632, 2048], P('section', 'tp', 'wide'), may hold values from -0.078125 to 0.078125
Outputs:
- section_out: bfloat16 [2, 2, 4096, 2048], P('section', None, ('wide', 'tp'))
- input_grads: bfloat16 [2, 2, 4096, 2048], P('section', None, ('wide', 'tp'))
- grad_attn_gain: float32 [2, 2048], P('section', 'wide')
- grad_w_query: float32 [2, 2048, 2048], P('section', 'wide', 'tp')
- grad_w_key: float32 [2, 2048, 256], P('section', 'wide', 'tp')
- grad_w_value: float32 [2, 2048, 256], P('section', 'wide', 'tp')
- grad_w_out: float32 [2, 2048, 2048], P('section', 'tp', 'wide')
- grad_ffn_gain: float32 [2, 2048], P('section', 'wide')
- grad_w_gate: float32 [2, 2048, 5632], P('section', 'wide', 'tp')
- grad_w_up: float32 [2, 2048, 5632], P('section', 'wide', 'tp')
- grad_w_down: float32 [2, 5632, 2048], P('section', 'tp', 'wide')
All inputs are finite; a program needn't handle non-finite values.
Results may differ from a plain program's by a relative error of at most 0.03.
Values may be sent and summed in bfloat16 or wider, within the bound.
A program may use at most 512 MiB of HBM per device.

v0:
```python
import math

import jax
import jax.numpy as jnp
from jax import lax
from jax.sharding import PartitionSpec as P

HD = 64


EPSILON = 1e-05


def from_behind(x, axis, by):
    peers = lax.axis_size(axis)
    pairs = [(i, i + by) for i in range(peers) if 0 <= i + by < peers]
    return lax.ppermute(x, axis, pairs)


def cross(left, right):
    return lax.dot_general(
        left, right, (((0,), (0,)), ((), ())), preferred_element_type=jnp.float32
    )


def against(left, right):
    return lax.dot_general(
        left, right, (((1,), (1,)), ((), ())), preferred_element_type=jnp.float32
    )


def rope_tables(query_places):
    inverse = 1.0 / 10000.0 ** (jnp.arange(0, HD, 2).astype(jnp.float32) / HD)
    angle = query_places.astype(jnp.float32)[:, None] * inverse[None, :]
    return (jnp.cos(angle), jnp.sin(angle))


def rotate(heads, cosine, sine_part):
    half = heads.shape[-1] // 2
    first = heads[..., :half]
    second = heads[..., half:]
    cos_rows = cosine[:, None, :]
    sin_rows = sine_part[:, None, :]
    return jnp.concatenate(
        [first * cos_rows - second * sin_rows, second * cos_rows + first * sin_rows], axis=-1
    )


def spread_rows(values):
    return lax.all_gather(values, "tp", axis=0, tiled=True)


def fold_rows(values):
    return lax.psum_scatter(
        values.astype(jnp.bfloat16), "tp", scatter_dimension=0, tiled=True
    ).astype(jnp.float32)


def spread_grads(values):
    return lax.all_gather(values, "tp", axis=0, tiled=True)


def fold_grads(values):
    return lax.psum_scatter(
        values.astype(jnp.bfloat16), "tp", scatter_dimension=0, tiled=True
    ).astype(jnp.float32)


def group_layout(queries, keys_all, values_all, kv_local):
    span_rows = queries.shape[0]
    group = queries.shape[1] // kv_local
    query_groups = queries.reshape(span_rows, kv_local, group, HD).transpose(1, 2, 0, 3)
    key_groups = keys_all.reshape(-1, kv_local, HD).transpose(1, 0, 2)
    value_groups = values_all.reshape(-1, kv_local, HD).transpose(1, 0, 2)
    return (query_groups, key_groups, value_groups)


def attend(queries, keys_all, values_all, query_places, kv_local):
    span_rows = queries.shape[0]
    softmax_scale = 1.0 / math.sqrt(HD)
    query_groups, key_groups, value_groups = group_layout(queries, keys_all, values_all, kv_local)
    visible = jnp.arange(keys_all.shape[0])[None, :] <= query_places[:, None]

    def per_group(operands):
        query_group, key_group, value_group = operands
        scores = (
            jnp.einsum("gcd,td->gct", query_group, key_group, preferred_element_type=jnp.float32)
            * softmax_scale
        )
        scores = jnp.where(visible, scores, -1e30)
        maxima = jnp.max(scores, axis=-1, keepdims=True)
        exponent_terms = jnp.exp(scores - maxima)
        totals = jnp.sum(exponent_terms, axis=-1, keepdims=True)
        probs_low = (exponent_terms / totals).astype(jnp.bfloat16)
        attended = jnp.einsum(
            "gct,td->gcd", probs_low, value_group, preferred_element_type=jnp.float32
        )
        return (attended.astype(jnp.bfloat16), (maxima + jnp.log(totals))[..., 0])

    attended, log_totals = lax.map(per_group, (query_groups, key_groups, value_groups))
    return (attended.transpose(2, 0, 1, 3).reshape(span_rows, -1), log_totals)


def attend_back(queries, keys_all, values_all, grad_attended, log_totals, query_places, kv_local):
    span_rows = queries.shape[0]
    softmax_scale = 1.0 / math.sqrt(HD)
    query_groups, key_groups, value_groups = group_layout(queries, keys_all, values_all, kv_local)
    grad_groups = grad_attended.reshape(span_rows, kv_local, -1, HD).transpose(1, 2, 0, 3)
    visible = jnp.arange(keys_all.shape[0])[None, :] <= query_places[:, None]

    def per_group(operands):
        query_group, key_group, value_group, grad_group, log_group = operands
        scores = (
            jnp.einsum("gcd,td->gct", query_group, key_group, preferred_element_type=jnp.float32)
            * softmax_scale
        )
        scores = jnp.where(visible, scores, -1e30)
        probs = jnp.exp(scores - log_group[..., None])
        grad_probs = jnp.einsum(
            "gcd,td->gct", grad_group, value_group, preferred_element_type=jnp.float32
        )
        row_dot = jnp.sum(grad_probs * probs, axis=-1, keepdims=True)
        grad_scores = (probs * (grad_probs - row_dot) * softmax_scale).astype(jnp.bfloat16)
        grad_query = jnp.einsum(
            "gct,td->gcd", grad_scores, key_group, preferred_element_type=jnp.float32
        )
        grad_key = jnp.einsum(
            "gct,gcd->td", grad_scores, query_group, preferred_element_type=jnp.float32
        )
        grad_value = jnp.einsum(
            "gct,gcd->td",
            probs.astype(jnp.bfloat16),
            grad_group,
            preferred_element_type=jnp.float32,
        )
        return (grad_query, grad_key, grad_value)

    grad_query, grad_key, grad_value = lax.map(
        per_group, (query_groups, key_groups, value_groups, grad_groups, log_totals)
    )
    grad_query = grad_query.transpose(2, 0, 1, 3).reshape(span_rows, -1, HD)
    grad_key = grad_key.transpose(1, 0, 2).reshape(keys_all.shape[0], -1)
    grad_value = grad_value.transpose(1, 0, 2).reshape(keys_all.shape[0], -1)
    return (grad_query, grad_key, grad_value)


def layer_forward(inputs, weights, rotary, query_places, kv_local):
    gain_first, w_query, w_key, w_value, w_out, gain_second, w_gate, w_up, w_down = weights
    cosine, sine_part = rotary
    first_scale = lax.rsqrt(jnp.mean(inputs * inputs, axis=-1, keepdims=True) + EPSILON)
    normed_rows = spread_rows(
        (inputs * first_scale * gain_first.astype(jnp.float32)).astype(jnp.bfloat16)
    )
    span_rows = normed_rows.shape[0]
    query_lin = jnp.dot(normed_rows, w_query, preferred_element_type=jnp.float32).reshape(
        span_rows, -1, HD
    )
    queries = rotate(query_lin, cosine, sine_part).astype(jnp.bfloat16)
    key_lin = jnp.dot(normed_rows, w_key, preferred_element_type=jnp.float32).reshape(
        span_rows, kv_local, HD
    )
    keys_local = (
        rotate(key_lin, cosine, sine_part).astype(jnp.bfloat16).reshape(span_rows, kv_local * HD)
    )
    values_local = jnp.dot(normed_rows, w_value, preferred_element_type=jnp.float32).astype(
        jnp.bfloat16
    )
    keys_all, values_all = (
        lax.all_gather(keys_local, "wide", axis=0, tiled=True),
        lax.all_gather(values_local, "wide", axis=0, tiled=True),
    )
    attended, log_totals = attend(queries, keys_all, values_all, query_places, kv_local)
    middle = inputs + fold_rows(jnp.dot(attended, w_out, preferred_element_type=jnp.float32))
    second_scale = lax.rsqrt(jnp.mean(middle * middle, axis=-1, keepdims=True) + EPSILON)
    normed_ffn = spread_rows(
        (middle * second_scale * gain_second.astype(jnp.float32)).astype(jnp.bfloat16)
    )
    gate_pre = jnp.dot(normed_ffn, w_gate, preferred_element_type=jnp.float32)
    up_proj = jnp.dot(normed_ffn, w_up, preferred_element_type=jnp.float32)
    hidden = (jax.nn.silu(gate_pre) * up_proj).astype(jnp.bfloat16)
    result = middle + fold_rows(jnp.dot(hidden, w_down, preferred_element_type=jnp.float32))
    saved = (
        inputs,
        first_scale,
        normed_rows,
        queries,
        keys_all,
        values_all,
        attended,
        log_totals,
        middle,
        second_scale,
        normed_ffn,
        gate_pre,
        up_proj,
        hidden,
    )
    return (result, saved)


def backward_inputs(upstream, saved, weights, rotary, query_places, kv_local):
    gain_first, w_query, w_key, w_value, w_out, gain_second, w_gate, w_up, w_down = weights
    (
        inputs,
        first_scale,
        normed_rows,
        queries,
        keys_all,
        values_all,
        attended,
        log_totals,
        middle,
        second_scale,
        normed_ffn,
        gate_pre,
        up_proj,
        hidden,
    ) = saved
    cosine, sine_part = rotary
    span_rows = normed_rows.shape[0]
    grad_full2 = spread_grads(upstream.astype(jnp.bfloat16))
    grad_hidden = against(grad_full2, w_down)
    sigma = jax.nn.sigmoid(gate_pre)
    grad_gate = (grad_hidden * up_proj * sigma * (1.0 + gate_pre * (1.0 - sigma))).astype(
        jnp.bfloat16
    )
    grad_up = (grad_hidden * gate_pre * sigma).astype(jnp.bfloat16)
    grad_normed_ffn = fold_grads(against(grad_gate, w_gate) + against(grad_up, w_up))
    second_norm = middle * second_scale
    gain_second_term = jnp.sum(grad_normed_ffn * second_norm, axis=0)
    second_scaled = grad_normed_ffn * gain_second.astype(jnp.float32)
    grad_middle = upstream + second_scale * (
        second_scaled - second_norm * jnp.mean(second_scaled * second_norm, axis=-1, keepdims=True)
    )
    grad_full1 = spread_grads(grad_middle.astype(jnp.bfloat16))
    grad_attended = against(grad_full1, w_out).astype(jnp.bfloat16)
    grad_query, grad_key_part, grad_value_part = attend_back(
        queries, keys_all, values_all, grad_attended, log_totals, query_places, kv_local
    )
    grad_key, grad_value = (
        lax.psum_scatter(
            grad_key_part.astype(jnp.bfloat16), "wide", scatter_dimension=0, tiled=True
        ).astype(jnp.float32),
        lax.psum_scatter(
            grad_value_part.astype(jnp.bfloat16), "wide", scatter_dimension=0, tiled=True
        ).astype(jnp.float32),
    )
    grad_qlin = rotate(grad_query, cosine, -sine_part).astype(jnp.bfloat16).reshape(span_rows, -1)
    grad_klin = (
        rotate(grad_key.reshape(span_rows, kv_local, HD), cosine, -sine_part)
        .astype(jnp.bfloat16)
        .reshape(span_rows, -1)
    )
    grad_vlin = grad_value.astype(jnp.bfloat16)
    grad_normed = fold_grads(
        against(grad_qlin, w_query) + against(grad_klin, w_key) + against(grad_vlin, w_value)
    )
    first_norm = inputs * first_scale
    gain_first_term = jnp.sum(grad_normed * first_norm, axis=0)
    first_scaled = grad_normed * gain_first.astype(jnp.float32)
    grad_inputs = grad_middle + first_scale * (
        first_scaled - first_norm * jnp.mean(first_scaled * first_norm, axis=-1, keepdims=True)
    )
    pieces = (
        gain_first_term,
        grad_qlin,
        grad_klin,
        grad_vlin,
        grad_full1,
        gain_second_term,
        grad_gate,
        grad_up,
        grad_full2,
    )
    return (grad_inputs, pieces)


def weight_terms(normed_rows, attended, normed_ffn, hidden, pieces):
    (
        gain_first_term,
        grad_qlin,
        grad_klin,
        grad_vlin,
        grad_full1,
        gain_second_term,
        grad_gate,
        grad_up,
        grad_full2,
    ) = pieces
    return (
        gain_first_term,
        cross(normed_rows, grad_qlin),
        cross(normed_rows, grad_klin),
        cross(normed_rows, grad_vlin),
        cross(attended, grad_full1),
        gain_second_term,
        cross(normed_ffn, grad_gate),
        cross(normed_ffn, grad_up),
        cross(hidden, grad_full2),
    )


def put_slot(buffer, element, where_slot, active):
    return jnp.where(
        active, lax.dynamic_update_index_in_dim(buffer, element, where_slot, 0), buffer
    )


def shards(
    tokens, out_grad, attn_gain, w_query, w_key, w_value, w_out, ffn_gain, w_gate, w_up, w_down
):
    section_index = lax.axis_index("section")
    micro_count = tokens.shape[0]
    row_count = tokens.shape[1]
    model_width = tokens.shape[2]
    kv_local = w_key.shape[2] // HD
    span_rows = row_count * lax.axis_size("tp")
    query_places = lax.axis_index("wide") * span_rows + jnp.arange(span_rows)
    rotary = rope_tables(query_places)
    weights = (
        lax.all_gather(attn_gain[0], "wide", axis=0, tiled=True),
        lax.all_gather(w_query[0], "wide", axis=0, tiled=True),
        lax.all_gather(w_key[0], "wide", axis=0, tiled=True),
        lax.all_gather(w_value[0], "wide", axis=0, tiled=True),
        lax.all_gather(w_out[0], "wide", axis=1, tiled=True),
        lax.all_gather(ffn_gain[0], "wide", axis=0, tiled=True),
        lax.all_gather(w_gate[0], "wide", axis=0, tiled=True),
        lax.all_gather(w_up[0], "wide", axis=0, tiled=True),
        lax.all_gather(w_down[0], "wide", axis=1, tiled=True),
    )
    incoming = jnp.zeros((row_count, model_width), jnp.bfloat16)
    outputs = jnp.zeros((micro_count, row_count, model_width), jnp.bfloat16)
    storage = None
    for moment in range(micro_count + 1):
        micro_slot = moment - section_index
        active = (micro_slot >= 0) & (micro_slot < micro_count)
        where_slot = jnp.clip(micro_slot, 0, micro_count - 1)
        fresh = tokens[min(moment, micro_count - 1)]
        source = jnp.where(section_index == 0, fresh, incoming).astype(jnp.float32)
        result, saved = layer_forward(source, weights, rotary, query_places, kv_local)
        if storage is None:
            storage = jax.tree.map(
                lambda element: jnp.zeros((micro_count,) + element.shape, element.dtype), saved
            )
        storage = jax.tree.map(
            lambda buffer, element: put_slot(buffer, element, where_slot, active), storage, saved
        )
        result_low = result.astype(jnp.bfloat16)
        outputs = put_slot(outputs, result_low, where_slot, active)
        if moment < micro_count:
            incoming = from_behind(result_low, "section", 1)
    incoming = jnp.zeros((row_count, model_width), jnp.bfloat16)
    in_grads = jnp.zeros((micro_count, row_count, model_width), jnp.bfloat16)
    running = None
    for moment in range(micro_count + 1):
        micro_slot = moment - 1 + section_index
        active = (micro_slot >= 0) & (micro_slot < micro_count)
        where_slot = jnp.clip(micro_slot, 0, micro_count - 1)
        fresh = out_grad[min(moment, micro_count - 1)]
        upstream = jnp.where(section_index == 1, fresh, incoming).astype(jnp.float32)
        saved = jax.tree.map(
            lambda buffer: lax.dynamic_index_in_dim(buffer, where_slot, 0, keepdims=False), storage
        )
        grad_inputs, pieces = backward_inputs(
            upstream, saved, weights, rotary, query_places, kv_local
        )
        grad_low = grad_inputs.astype(jnp.bfloat16)
        in_grads = put_slot(in_grads, grad_low, where_slot, active)
        if moment < micro_count:
            incoming = from_behind(grad_low, "section", -1)
        terms = weight_terms(saved[2], saved[6], saved[10], saved[13], pieces)
        terms = jax.tree.map(lambda element: jnp.where(active, element, 0.0), terms)
        if running is None:
            running = terms
        else:
            running = jax.tree.map(lambda total, extra: total + extra, running, terms)
    running = (
        lax.psum_scatter(
            running[0].astype(jnp.bfloat16), "wide", scatter_dimension=0, tiled=True
        ).astype(jnp.float32),
        lax.psum_scatter(
            running[1].astype(jnp.bfloat16), "wide", scatter_dimension=0, tiled=True
        ).astype(jnp.float32),
        lax.psum_scatter(
            running[2].astype(jnp.bfloat16), "wide", scatter_dimension=0, tiled=True
        ).astype(jnp.float32),
        lax.psum_scatter(
            running[3].astype(jnp.bfloat16), "wide", scatter_dimension=0, tiled=True
        ).astype(jnp.float32),
        lax.psum_scatter(
            running[4].astype(jnp.bfloat16), "wide", scatter_dimension=1, tiled=True
        ).astype(jnp.float32),
        lax.psum_scatter(
            running[5].astype(jnp.bfloat16), "wide", scatter_dimension=0, tiled=True
        ).astype(jnp.float32),
        lax.psum_scatter(
            running[6].astype(jnp.bfloat16), "wide", scatter_dimension=0, tiled=True
        ).astype(jnp.float32),
        lax.psum_scatter(
            running[7].astype(jnp.bfloat16), "wide", scatter_dimension=0, tiled=True
        ).astype(jnp.float32),
        lax.psum_scatter(
            running[8].astype(jnp.bfloat16), "wide", scatter_dimension=1, tiled=True
        ).astype(jnp.float32),
    )
    gain_first, gain_second = lax.psum((running[0], running[5]), "tp")
    return (
        outputs[None],
        in_grads[None],
        gain_first[None],
        running[1][None],
        running[2][None],
        running[3][None],
        running[4][None],
        gain_second[None],
        running[6][None],
        running[7][None],
        running[8][None],
    )


def solution(mesh):
    return jax.shard_map(
        shards,
        mesh=mesh,
        in_specs=(
            P(None, ("wide", "tp"), None),
            P(None, ("wide", "tp"), None),
            P("section", "wide"),
            P("section", "wide", "tp"),
            P("section", "wide", "tp"),
            P("section", "wide", "tp"),
            P("section", "tp", "wide"),
            P("section", "wide"),
            P("section", "wide", "tp"),
            P("section", "wide", "tp"),
            P("section", "tp", "wide"),
        ),
        out_specs=(
            P("section", None, ("wide", "tp"), None),
            P("section", None, ("wide", "tp"), None),
            P("section", "wide"),
            P("section", "wide", "tp"),
            P("section", "wide", "tp"),
            P("section", "wide", "tp"),
            P("section", "tp", "wide"),
            P("section", "wide"),
            P("section", "wide", "tp"),
            P("section", "wide", "tp"),
            P("section", "tp", "wide"),
        ),
        check_vma=False,
    )
```

profile of v0, /device:TPU:1, one launch (start us, length us, event | category | flops | bytes accessed | tf_op | source)
XLA Modules:
  0.0 4800.2 jit_solution(10385026107356145202)
XLA Ops:
  111.0 39.6 all-gather.38.cloned.1.call-done
  152.8 71.7 %all-gather.68.cloned.1.call-done = bf16[1,2048,1024]{2,1,0:T(8,128)(2,1)} async-done(((bf16[1,256,1024]{2,1,0:T(8,128)(2,1)}), bf16[1,2048,1024]{2,1,0:T(8,128)(2,1)}) %all-gather.68.cloned.1.call-update) | async-done | bytes 4194320 | tf_op jit(solution)/shard_map/all_gather | solution.py:322
  231.4 153.9 %while.84 = (s32[]{:T(128)}, bf16[2,8,512,64]{2,3,1,0:T(8,128)(2,1)S(1)}, f32[2,8,512]{2,1,0:T(8,128)S(1)}, bf16[2,8,512,64]{2,3,1,0:T(8,128)(2,1)}, bf16[2,4096...) while((s32[]{:T(128)}, ...), condition=%wide.region_4.5_spmd.clone, body=%wide.region_1.4_spmd.clone.sunk | while | flops 4498649088 | bytes 211947616 | solution.py:100
  233.3 27.1 fusion.660
  310.4 26.9 fusion.660
  424.0 166.5 %all-gather.72.cloned.1.call-done = bf16[1,2048,2816]{2,1,0:T(8,128)(2,1)} async-done(((bf16[1,256,2816]{2,1,0:T(8,128)(2,1)}), bf16[1,2048,2816]{2,1,0:T(8,128)(2,1)}) %all-gather.72.cloned.1.call-update) | async-done | bytes 11534352 | tf_op jit(solution)/shard_map/all_gather | solution.py:327
  608.9 145.9 %all-gather.74.cloned.1.call-done = bf16[1,2048,2816]{2,1,0:T(8,128)(2,1)} async-done(((bf16[1,256,2816]{2,1,0:T(8,128)(2,1)}), bf16[1,2048,2816]{2,1,0:T(8,128)(2,1)}) %all-gather.74.cloned.1.call-update) | async-done | bytes 11534352 | tf_op jit(solution)/shard_map/all_gather | solution.py:328
  771.8 147.0 %all-gather.76.cloned.1.call-done = bf16[1,2816,2048]{2,1,0:T(8,128)(2,1)} async-done(((bf16[1,2816,256]{2,1,0:T(8,128)(2,1)}), bf16[1,2816,2048]{2,1,0:T(8,128)(2,1)}) %all-gather.76.cloned.1.call-update) | async-done | bytes 11534352 | tf_op jit(solution)/shard_map/all_gather | solution.py:329
  1000.4 31.1 all-gather.46.cloned.1.call-done
  1033.8 39.2 all-gather.44.cloned.1.call-done
  1075.4 152.8 %while.85 = (s32[]{:T(128)}, bf16[2,8,512,64]{2,3,1,0:T(8,128)(2,1)S(1)}, f32[2,8,512]{2,1,0:T(8,128)S(1)}, bf16[2,8,512,64]{2,3,1,0:T(8,128)(2,1)}, bf16[2,4096...) while((s32[]{:T(128)}, ...), condition=%wide.region_12.13_spmd.clone, body=%wide.region_9.12_spmd.clone.sunk | while | flops 4498649088 | bytes 211947616 | solution.py:100
  1077.1 26.9 fusion.664
  1153.3 26.9 fusion.664
  1375.2 31.6 all-gather.52.cloned.1.call-done
  1409.1 39.2 all-gather.54.cloned.1.call-done
  1450.7 153.0 %while.86 = (s32[]{:T(128)}, bf16[2,8,512,64]{2,3,1,0:T(8,128)(2,1)S(1)}, f32[2,8,512]{2,1,0:T(8,128)S(1)}, bf16[2,8,512,64]{2,3,1,0:T(8,128)(2,1)}, bf16[2,4096...) while((s32[]{:T(128)}, ...), condition=%wide.region_20.21_spmd.clone, body=%wide.region_17.20_spmd.clone.sunk | while | flops 4498649088 | bytes 211947616 | solution.py:100
  1452.5 26.9 fusion.668
  1528.8 26.9 fusion.668
  1763.1 476.1 %while.87 = (s32[]{:T(128)}, f32[2,8,512,64]{2,3,1,0:T(8,128)}, bf16[2,4096,64]{1,2,0:T(8,128)(2,1)}, bf16[2,4096,64]{1,2,0:T(8,128)(2,1)S(1)}, bf16[2,8,512,64]...) while((s32[]{:T(128)}, f32[2,8,512,64]{2,3,1,0:T(8,128)}, ...), condition=%wide.region_28.29_spmd.clone, body=%wide.region_26.28_spmd.clone.sunk | while | flops 10974412800 | bytes 749263936 | solution.py:138
  1765.0 26.1 subtract_exponential_fusion.9
  1836.4 82.4 %fusion.683 = bf16[2,4096,64]{1,2,0:T(8,128)(2,1)} fusion(bf16[2,4096,64]{1,2,0:T(8,128)(2,1)} %get-tuple-element.1042, s32[]{:T(128)S(6)} %copy.178, f32[8,512,4096]{2,1,0:T(8,128)} %subtract_exponential_fusion.9, f32[8,512,4096]{2,1,0:T(8,128)} %fusion.681, bf16[2,8,512,64]{2,3,1,0:T(8,128)(2,1)} %get-tuple-element.1055), kind=kOutput, calls=%fused_computation.83.clone.2 | convolution fusion | flops 2231377920 | bytes 270009344 | tf_op jit(solution)/shard_map/while/body/eval_jaxpr/gct,gcd->td/dot_general | solution.py:127
  1918.8 82.2 %fusion.682 = f32[2,8,512,64]{2,3,1,0:T(8,128)} fusion(f32[2,8,512,64]{2,3,1,0:T(8,128)} %get-tuple-element.1041, s32[]{:T(128)S(6)} %copy.178, f32[8,512,4096]{2,1,0:T(8,128)} %subtract_exponential_fusion.9, f32[8,512,4096]{2,1,0:T(8,128)} %fusion.681, bf16[2,4096,64]{1,2,0:T(8,128)(2,1)} %get-tuple-element.1056), kind=kOutput, calls=%fused_computation.87.clone.2 | convolution fusion | flops 2231377920 | bytes 270009344 | tf_op jit(solution)/shard_map/while/body/eval_jaxpr/gct,td->gcd/dot_general | solution.py:124
  2002.7 26.1 subtract_exponential_fusion.9
  2074.1 82.4 %fusion.683 = bf16[2,4096,64]{1,2,0:T(8,128)(2,1)} fusion(bf16[2,4096,64]{1,2,0:T(8,128)(2,1)} %get-tuple-element.1042, s32[]{:T(128)S(6)} %copy.178, f32[8,512,4096]{2,1,0:T(8,128)} %subtract_exponential_fusion.9, f32[8,512,4096]{2,1,0:T(8,128)} %fusion.681, bf16[2,8,512,64]{2,3,1,0:T(8,128)(2,1)} %get-tuple-element.1055), kind=kOutput, calls=%fused_computation.83.clone.2 | convolution fusion | flops 2231377920 | bytes 270009344 | tf_op jit(solution)/shard_map/while/body/eval_jaxpr/gct,gcd->td/dot_general | solution.py:127
  2156.5 82.3 %fusion.682 = f32[2,8,512,64]{2,3,1,0:T(8,128)} fusion(f32[2,8,512,64]{2,3,1,0:T(8,128)} %get-tuple-element.1041, s32[]{:T(128)S(6)} %copy.178, f32[8,512,4096]{2,1,0:T(8,128)} %subtract_exponential_fusion.9, f32[8,512,4096]{2,1,0:T(8,128)} %fusion.681, bf16[2,4096,64]{1,2,0:T(8,128)(2,1)} %get-tuple-element.1056), kind=kOutput, calls=%fused_computation.87.clone.2 | convolution fusion | flops 2231377920 | bytes 270009344 | tf_op jit(solution)/shard_map/while/body/eval_jaxpr/gct,td->gcd/dot_general | solution.py:124
  2246.9 55.6 %reduce-scatter.40.cloned.1.call-done = bf16[512,128]{0,1:T(8,128)(2,1)} async-done(((bf16[4096,128]{0,1:T(8,128)(2,1)}), bf16[512,128]{0,1:T(8,128)(2,1)}) %reduce-scatter.40.cloned.1.call-update) | async-done | bytes 131088 | tf_op jit(solution)/shard_map/reduce_scatter | solution.py:241
  2306.3 62.8 %reduce-scatter.42.cloned.1.call-done = bf16[512,128]{0,1:T(8,128)(2,1)} async-done(((bf16[4096,128]{0,1:T(8,128)(2,1)}), bf16[512,128]{0,1:T(8,128)(2,1)}) %reduce-scatter.42.cloned.1.call-update) | async-done | bytes 131088 | tf_op jit(solution)/shard_map/reduce_scatter | solution.py:244
  2509.2 476.1 %while.88 = (s32[]{:T(128)}, f32[2,8,512,64]{2,3,1,0:T(8,128)}, bf16[2,4096,64]{1,2,0:T(8,128)(2,1)}, bf16[2,4096,64]{1,2,0:T(8,128)(2,1)S(1)}, bf16[2,8,512,64]...) while((s32[]{:T(128)}, f32[2,8,512,64]{2,3,1,0:T(8,128)}, ...), condition=%wide.region_37.38_spmd.clone, body=%wide.region_35.37_spmd.clone.sunk | while | flops 10974412800 | bytes 749263936 | solution.py:138
  2582.5 82.4 %fusion.697 = bf16[2,4096,64]{1,2,0:T(8,128)(2,1)} fusion(bf16[2,4096,64]{1,2,0:T(8,128)(2,1)} %get-tuple-element.1075, s32[]{:T(128)S(6)} %copy.192, f32[8,512,4096]{2,1,0:T(8,128)} %subtract_exponential_fusion.10, f32[8,512,4096]{2,1,0:T(8,128)} %fusion.695, bf16[2,8,512,64]{2,3,1,0:T(8,128)(2,1)} %get-tuple-element.1088), kind=kOutput, calls=%fused_computation.124.clone.1 | convolution fusion | flops 2231377920 | bytes 270009344 | tf_op jit(solution)/shard_map/while/body/eval_jaxpr/gct,gcd->td/dot_general | solution.py:127
  2664.9 82.2 %fusion.696 = f32[2,8,512,64]{2,3,1,0:T(8,128)} fusion(f32[2,8,512,64]{2,3,1,0:T(8,128)} %get-tuple-element.1074, s32[]{:T(128)S(6)} %copy.192, f32[8,512,4096]{2,1,0:T(8,128)} %subtract_exponential_fusion.10, f32[8,512,4096]{2,1,0:T(8,128)} %fusion.695, bf16[2,4096,64]{1,2,0:T(8,128)(2,1)} %get-tuple-element.1089), kind=kOutput, calls=%fused_computation.128.clone.1 | convolution fusion | flops 2231377920 | bytes 270009344 | tf_op jit(solution)/shard_map/while/body/eval_jaxpr/gct,td->gcd/dot_general | solution.py:124
  2748.8 26.1 subtract_exponential_fusion.10
  2820.2 82.4 %fusion.697 = bf16[2,4096,64]{1,2,0:T(8,128)(2,1)} fusion(bf16[2,4096,64]{1,2,0:T(8,128)(2,1)} %get-tuple-element.1075, s32[]{:T(128)S(6)} %copy.192, f32[8,512,4096]{2,1,0:T(8,128)} %subtract_exponential_fusion.10, f32[8,512,4096]{2,1,0:T(8,128)} %fusion.695, bf16[2,8,512,64]{2,3,1,0:T(8,128)(2,1)} %get-tuple-element.1088), kind=kOutput, calls=%fused_computation.124.clone.1 | convolution fusion | flops 2231377920 | bytes 270009344 | tf_op jit(solution)/shard_map/while/body/eval_jaxpr/gct,gcd->td/dot_general | solution.py:127
  2902.6 82.3 %fusion.696 = f32[2,8,512,64]{2,3,1,0:T(8,128)} fusion(f32[2,8,512,64]{2,3,1,0:T(8,128)} %get-tuple-element.1074, s32[]{:T(128)S(6)} %copy.192, f32[8,512,4096]{2,1,0:T(8,128)} %subtract_exponential_fusion.10, f32[8,512,4096]{2,1,0:T(8,128)} %fusion.695, bf16[2,4096,64]{1,2,0:T(8,128)(2,1)} %get-tuple-element.1089), kind=kOutput, calls=%fused_computation.128.clone.1 | convolution fusion | flops 2231377920 | bytes 270009344 | tf_op jit(solution)/shard_map/while/body/eval_jaxpr/gct,td->gcd/dot_general | solution.py:124
  2993.0 55.7 %reduce-scatter.48.cloned.1.call-done = bf16[512,128]{0,1:T(8,128)(2,1)} async-done(((bf16[4096,128]{0,1:T(8,128)(2,1)}), bf16[512,128]{0,1:T(8,128)(2,1)}) %reduce-scatter.48.cloned.1.call-update) | async-done | bytes 131088 | tf_op jit(solution)/shard_map/reduce_scatter | solution.py:241
  3052.5 62.8 %reduce-scatter.50.cloned.1.call-done = bf16[512,128]{0,1:T(8,128)(2,1)} async-done(((bf16[4096,128]{0,1:T(8,128)(2,1)}), bf16[512,128]{0,1:T(8,128)(2,1)}) %reduce-scatter.50.cloned.1.call-update) | async-done | bytes 131088 | tf_op jit(solution)/shard_map/reduce_scatter | solution.py:244
  3254.6 476.2 %while.89 = (s32[]{:T(128)}, f32[2,8,512,64]{2,3,1,0:T(8,128)}, bf16[2,4096,64]{1,2,0:T(8,128)(2,1)}, bf16[2,4096,64]{1,2,0:T(8,128)(2,1)S(1)}, bf16[2,8,512,64]...) while((s32[]{:T(128)}, f32[2,8,512,64]{2,3,1,0:T(8,128)}, ...), condition=%wide.region_46.47_spmd.clone, body=%wide.region_44.46_spmd.clone.sunk | while | flops 10974412800 | bytes 749263936 | solution.py:138
  3256.4 26.1 subtract_exponential_fusion.11
  3327.9 82.4 %fusion.711 = bf16[2,4096,64]{1,2,0:T(8,128)(2,1)} fusion(bf16[2,4096,64]{1,2,0:T(8,128)(2,1)} %get-tuple-element.1108, s32[]{:T(128)S(6)} %copy.205, f32[8,512,4096]{2,1,0:T(8,128)} %subtract_exponential_fusion.11, f32[8,512,4096]{2,1,0:T(8,128)} %fusion.709, bf16[2,8,512,64]{2,3,1,0:T(8,128)(2,1)} %get-tuple-element.1121), kind=kOutput, calls=%fused_computation.165.clone.1 | convolution fusion | flops 2231377920 | bytes 270009344 | tf_op jit(solution)/shard_map/while/body/eval_jaxpr/gct,gcd->td/dot_general | solution.py:127
  3410.3 82.2 %fusion.710 = f32[2,8,512,64]{2,3,1,0:T(8,128)} fusion(f32[2,8,512,64]{2,3,1,0:T(8,128)} %get-tuple-element.1107, s32[]{:T(128)S(6)} %copy.205, f32[8,512,4096]{2,1,0:T(8,128)} %subtract_exponential_fusion.11, f32[8,512,4096]{2,1,0:T(8,128)} %fusion.709, bf16[2,4096,64]{1,2,0:T(8,128)(2,1)} %get-tuple-element.1122), kind=kOutput, calls=%fused_computation.169.clone.1 | convolution fusion | flops 2231377920 | bytes 270009344 | tf_op jit(solution)/shard_map/while/body/eval_jaxpr/gct,td->gcd/dot_general | solution.py:124
  3494.2 26.1 subtract_exponential_fusion.11
  3565.6 82.5 %fusion.711 = bf16[2,4096,64]{1,2,0:T(8,128)(2,1)} fusion(bf16[2,4096,64]{1,2,0:T(8,128)(2,1)} %get-tuple-element.1108, s32[]{:T(128)S(6)} %copy.205, f32[8,512,4096]{2,1,0:T(8,128)} %subtract_exponential_fusion.11, f32[8,512,4096]{2,1,0:T(8,128)} %fusion.709, bf16[2,8,512,64]{2,3,1,0:T(8,128)(2,1)} %get-tuple-element.1121), kind=kOutput, calls=%fused_computation.165.clone.1 | convolution fusion | flops 2231377920 | bytes 270009344 | tf_op jit(solution)/shard_map/while/body/eval_jaxpr/gct,gcd->td/dot_general | solution.py:127
  3648.1 82.2 %fusion.710 = f32[2,8,512,64]{2,3,1,0:T(8,128)} fusion(f32[2,8,512,64]{2,3,1,0:T(8,128)} %get-tuple-element.1107, s32[]{:T(128)S(6)} %copy.205, f32[8,512,4096]{2,1,0:T(8,128)} %subtract_exponential_fusion.11, f32[8,512,4096]{2,1,0:T(8,128)} %fusion.709, bf16[2,4096,64]{1,2,0:T(8,128)(2,1)} %get-tuple-element.1122), kind=kOutput, calls=%fused_computation.169.clone.1 | convolution fusion | flops 2231377920 | bytes 270009344 | tf_op jit(solution)/shard_map/while/body/eval_jaxpr/gct,td->gcd/dot_general | solution.py:124
  3751.6 43.5 reduce-scatter.58.cloned.1.call-done
  3802.3 59.9 %reduce-scatter.56.cloned.1.call-done = bf16[512,128]{0,1:T(8,128)(2,1)} async-done(((bf16[4096,128]{0,1:T(8,128)(2,1)}), bf16[512,128]{0,1:T(8,128)(2,1)}) %reduce-scatter.56.cloned.1.call-update) | async-done | bytes 131088 | tf_op jit(solution)/shard_map/reduce_scatter | solution.py:241
  4113.7 89.7 %reduce-scatter.62.cloned.1.call-done = bf16[256,1024]{1,0:T(8,128)(2,1)} async-done(((bf16[2048,1024]{1,0:T(8,128)(2,1)}), bf16[256,1024]{1,0:T(8,128)(2,1)}) %reduce-scatter.62.cloned.1.call-update) | async-done | bytes 524304 | tf_op jit(solution)/shard_map/reduce_scatter | solution.py:381
  4205.6 193.8 %reduce-scatter.70.cloned.1.call-done = bf16[256,2816]{1,0:T(8,128)(2,1)} async-done(((bf16[2048,2816]{1,0:T(8,128)(2,1)}), bf16[256,2816]{1,0:T(8,128)(2,1)}) %reduce-scatter.70.cloned.1.call-update) | async-done | bytes 1441808 | tf_op jit(solution)/shard_map/reduce_scatter | solution.py:396
  4402.5 192.1 %reduce-scatter.72.cloned.1.call-done = bf16[256,2816]{1,0:T(8,128)(2,1)} async-done(((bf16[2048,2816]{1,0:T(8,128)(2,1)}), bf16[256,2816]{1,0:T(8,128)(2,1)}) %reduce-scatter.72.cloned.1.call-update) | async-done | bytes 1441808 | tf_op jit(solution)/shard_map/reduce_scatter | solution.py:399
  4597.7 192.6 %reduce-scatter.74.cloned.1.call-done = bf16[2816,256]{1,0:T(8,128)(2,1)} async-done(((bf16[2816,2048]{1,0:T(8,128)(2,1)}), bf16[2816,256]{1,0:T(8,128)(2,1)}) %reduce-scatter.74.cloned.1.call-update) | async-done | bytes 1441808 | tf_op jit(solution)/shard_map/reduce_scatter | solution.py:402
  (820 shorter events, 1778.8 us)
Async XLA Ops:
  7.2 49.5 %all-gather.34.cloned.1.call-start = ((), (), s32[]{:S(2)}) async-start(), calls=%async_computation.25 | async-start | bytes 3145728 | tf_op jit(solution)/shard_map/all_gather | solution.py:50
  30.1 78.6 %all-gather.36.cloned.1.call-start = ((), (), s32[]{:S(2)}) async-start(), calls=%async_computation.26 | async-start | bytes 1179648 | tf_op jit(solution)/shard_map/all_gather | solution.py:169
  60.2 90.3 %all-gather.38.cloned.1.call-start = ((), (), s32[]{:S(2)}) async-start(), calls=%async_computation.27 | async-start | bytes 1179648 | tf_op jit(solution)/shard_map/all_gather | solution.py:170
  88.5 136.0 %all-gather.68.cloned.1.call-start = ((), (), s32[]{:S(2)}) async-start(), calls=%async_computation.67 | async-start | bytes 4718592 | tf_op jit(solution)/shard_map/all_gather | solution.py:322
  89.1 296.3 %all-gather.70.cloned.1.call-start = ((), (), s32[]{:S(2)}) async-start(), calls=%async_computation.68 | async-start | bytes 4718592 | tf_op jit(solution)/shard_map/all_gather | solution.py:325
  89.7 317.4 %reduce-scatter.26.cloned.1.call-start = ((), (), s32[]{:S(2)}) async-start(), calls=%async_computation.28 | async-start | bytes 3145728 | tf_op jit(solution)/shard_map/reduce_scatter | solution.py:54
  391.7 32.4 all-gather.40.cloned.1.call-start
  412.1 178.5 %all-gather.72.cloned.1.call-start = ((), (), s32[]{:S(2)}) async-start(), calls=%async_computation.69 | async-start | bytes 12976128 | tf_op jit(solution)/shard_map/all_gather | solution.py:327
  412.8 342.0 %all-gather.74.cloned.1.call-start = ((), (), s32[]{:S(2)}) async-start(), calls=%async_computation.70 | async-start | bytes 12976128 | tf_op jit(solution)/shard_map/all_gather | solution.py:328
  413.5 505.3 %all-gather.76.cloned.1.call-start = ((), (), s32[]{:S(2)}) async-start(), calls=%async_computation.71 | async-start | bytes 12976128 | tf_op jit(solution)/shard_map/all_gather | solution.py:329
  414.1 524.3 %reduce-scatter.28.cloned.1.call-start = ((), (), s32[]{:S(2)}) async-start(), calls=%async_computation.30 | async-start | bytes 3145728 | tf_op jit(solution)/shard_map/reduce_scatter | solution.py:54
  929.7 58.7 %all-gather.42.cloned.1.call-start = ((), (), s32[]{:S(2)}) async-start(), calls=%async_computation.31 | async-start | bytes 3145728 | tf_op jit(solution)/shard_map/all_gather | solution.py:50
  975.0 56.5 %all-gather.46.cloned.1.call-start = ((), (), s32[]{:S(2)}) async-start(), calls=%async_computation.33 | async-start | bytes 1179648 | tf_op jit(solution)/shard_map/all_gather | solution.py:170
  991.5 81.6 %all-gather.44.cloned.1.call-start = ((), (), s32[]{:S(2)}) async-start(), calls=%async_computation.32 | async-start | bytes 1179648 | tf_op jit(solution)/shard_map/all_gather | solution.py:169
  993.3 251.3 %reduce-scatter.30.cloned.1.call-start = ((), (), s32[]{:S(2)}) async-start(), calls=%async_computation.34 | async-start | bytes 3145728 | tf_op jit(solution)/shard_map/reduce_scatter | solution.py:54
  1248.8 61.4 %reduce-scatter.32.cloned.1.call-start = ((), (), s32[]{:S(2)}) async-start(), calls=%async_computation.36 | async-start | bytes 3145728 | tf_op jit(solution)/shard_map/reduce_scatter | solution.py:54
  1299.1 64.2 %all-gather.50.cloned.1.call-start = ((), (), s32[]{:S(2)}) async-start(), calls=%async_computation.37 | async-start | bytes 3145728 | tf_op jit(solution)/shard_map/all_gather | solution.py:50
  1313.9 26.4 collective-permute-start.1
  1349.7 57.2 %all-gather.52.cloned.1.call-start = ((), (), s32[]{:S(2)}) async-start(), calls=%async_computation.38 | async-start | bytes 1179648 | tf_op jit(solution)/shard_map/all_gather | solution.py:169
  1366.7 81.6 %all-gather.54.cloned.1.call-start = ((), (), s32[]{:S(2)}) async-start(), calls=%async_computation.39 | async-start | bytes 1179648 | tf_op jit(solution)/shard_map/all_gather | solution.py:170
  1368.2 251.7 %reduce-scatter.34.cloned.1.call-start = ((), (), s32[]{:S(2)}) async-start(), calls=%async_computation.40 | async-start | bytes 3145728 | tf_op jit(solution)/shard_map/reduce_scatter | solution.py:54
  1610.1 37.4 all-gather.56.cloned.1.call-start
  1624.2 56.1 %all-gather.78.cloned.1.call-start = ((), (), s32[]{:S(2)}) async-start(), calls=%async_computation.72 | async-start | bytes 3145728 | tf_op jit(solution)/shard_map/all_gather | solution.py:60
  1625.3 109.0 %reduce-scatter.38.cloned.1.call-start = ((), (), s32[]{:S(2)}) async-start(), calls=%async_computation.43 | async-start | bytes 3145728 | tf_op jit(solution)/shard_map/reduce_scatter | solution.py:64
  1717.3 37.3 all-gather.58.cloned.1.call-start
  1741.2 561.3 %reduce-scatter.40.cloned.1.call-start = ((), (), s32[]{:S(2)}) async-start(), calls=%async_computation.45 | async-start | bytes 1179648 | tf_op jit(solution)/shard_map/reduce_scatter | solution.py:241
  2239.2 129.8 %reduce-scatter.42.cloned.1.call-start = ((), (), s32[]{:S(2)}) async-start(), calls=%async_computation.46 | async-start | bytes 1179648 | tf_op jit(solution)/shard_map/reduce_scatter | solution.py:244
  2240.2 145.1 %reduce-scatter.44.cloned.1.call-start = ((), (), s32[]{:S(2)}) async-start(), calls=%async_computation.47 | async-start | bytes 3145728 | tf_op jit(solution)/shard_map/reduce_scatter | solution.py:64
  2374.7 59.8 %all-gather.60.cloned.1.call-start = ((), (), s32[]{:S(2)}) async-start(), calls=%async_computation.48 | async-start | bytes 3145728 | tf_op jit(solution)/shard_map/all_gather | solution.py:60
  2422.6 59.4 %reduce-scatter.46.cloned.1.call-start = ((), (), s32[]{:S(2)}) async-start(), calls=%async_computation.49 | async-start | bytes 3145728 | tf_op jit(solution)/shard_map/reduce_scatter | solution.py:64
  2471.1 29.6 all-gather.62.cloned.1.call-start
  2488.8 559.9 %reduce-scatter.48.cloned.1.call-start = ((), (), s32[]{:S(2)}) async-start(), calls=%async_computation.51 | async-start | bytes 1179648 | tf_op jit(solution)/shard_map/reduce_scatter | solution.py:241
  2985.3 130.0 %reduce-scatter.50.cloned.1.call-start = ((), (), s32[]{:S(2)}) async-start(), calls=%async_computation.52 | async-start | bytes 1179648 | tf_op jit(solution)/shard_map/reduce_scatter | solution.py:244
  2986.3 145.3 %reduce-scatter.52.cloned.1.call-start = ((), (), s32[]{:S(2)}) async-start(), calls=%async_computation.53 | async-start | bytes 3145728 | tf_op jit(solution)/shard_map/reduce_scatter | solution.py:64
  3120.9 58.9 %all-gather.64.cloned.1.call-start = ((), (), s32[]{:S(2)}) async-start(), calls=%async_computation.54 | async-start | bytes 3145728 | tf_op jit(solution)/shard_map/all_gather | solution.py:60
  3167.9 59.5 %reduce-scatter.54.cloned.1.call-start = ((), (), s32[]{:S(2)}) async-start(), calls=%async_computation.55 | async-start | bytes 3145728 | tf_op jit(solution)/shard_map/reduce_scatter | solution.py:64
  3216.4 29.6 all-gather.66.cloned.1.call-start
  3234.1 561.0 %reduce-scatter.58.cloned.1.call-start = ((), (), s32[]{:S(2)}) async-start(), calls=%async_computation.58 | async-start | bytes 1179648 | tf_op jit(solution)/shard_map/reduce_scatter | solution.py:244
  3731.7 130.5 %reduce-scatter.56.cloned.1.call-start = ((), (), s32[]{:S(2)}) async-start(), calls=%async_computation.57 | async-start | bytes 1179648 | tf_op jit(solution)/shard_map/reduce_scatter | solution.py:241
  3732.3 309.5 %reduce-scatter.36.cloned.1.call-start = ((), (), s32[]{:S(2)}) async-start(), calls=%async_computation.42 | async-start | bytes 3145728 | tf_op jit(solution)/shard_map/reduce_scatter | solution.py:54
  3743.2 305.4 %reduce-scatter.66.cloned.1.call-start = ((), (), s32[]{:S(2)}) async-start(), calls=%async_computation.62 | async-start | bytes 589824 | tf_op jit(solution)/shard_map/reduce_scatter | solution.py:387
  3798.3 251.8 %reduce-scatter.64.cloned.1.call-start = ((), (), s32[]{:S(2)}) async-start(), calls=%async_computation.61 | async-start | bytes 589824 | tf_op jit(solution)/shard_map/reduce_scatter | solution.py:384
  3866.4 185.2 %reduce-scatter.60.cloned.1.call-start = ((), (), s32[]{:S(2)}) async-start(), calls=%async_computation.59 | async-start | bytes 3145728 | tf_op jit(solution)/shard_map/reduce_scatter | solution.py:64
  3874.5 237.2 %reduce-scatter.68.cloned.1.call-start = ((), (), s32[]{:S(2)}) async-start(), calls=%async_computation.63 | async-start | bytes 4718592 | tf_op jit(solution)/shard_map/reduce_scatter | solution.py:390
  3886.7 316.7 %reduce-scatter.62.cloned.1.call-start = ((), (), s32[]{:S(2)}) async-start(), calls=%async_computation.60 | async-start | bytes 4718592 | tf_op jit(solution)/shard_map/reduce_scatter | solution.py:381
  3906.7 492.6 %reduce-scatter.70.cloned.1.call-start = ((), (), s32[]{:S(2)}) async-start(), calls=%async_computation.64 | async-start | bytes 12976128 | tf_op jit(solution)/shard_map/reduce_scatter | solution.py:396
  3950.9 643.7 %reduce-scatter.72.cloned.1.call-start = ((), (), s32[]{:S(2)}) async-start(), calls=%async_computation.65 | async-start | bytes 12976128 | tf_op jit(solution)/shard_map/reduce_scatter | solution.py:399
  3992.5 797.8 %reduce-scatter.74.cloned.1.call-start = ((), (), s32[]{:S(2)}) async-start(), calls=%async_computation.66 | async-start | bytes 12976128 | tf_op jit(solution)/shard_map/reduce_scatter | solution.py:402
  (198 other events, 4929.2 us)
Sparse Core Ops, SparseCore 0:
  30.2 11.9 all-gather.33
  60.3 48.3 all-gather.35
  111.4 39.0 all-gather.37
  152.5 71.9 all-gather.67
  226.4 74.0 all-gather.69
  391.8 9.4 reduce-scatter.25
  412.2 11.8 all-gather.39
  426.5 164.0 all-gather.71
  593.0 161.8 all-gather.73
  756.9 161.9 all-gather.75
  929.8 8.6 reduce-scatter.27
  975.1 13.1 all-gather.41
  991.6 39.9 all-gather.45
  1034.1 38.8 all-gather.43
  1234.8 9.7 reduce-scatter.29
  1248.9 11.7 all-gather.47
  1299.3 10.9 reduce-scatter.31
  1349.8 13.4 all-gather.49
  1366.9 39.9 all-gather.51
  1409.4 38.8 all-gather.53
  1610.2 9.7 reduce-scatter.33
  1624.3 11.7 all-gather.55
  1638.3 11.7 all-gather.77
  1717.4 10.7 reduce-scatter.37
  1741.3 11.7 all-gather.57
  2239.3 63.1 reduce-scatter.39
  2306.1 62.8 reduce-scatter.41
  2374.8 10.5 reduce-scatter.43
  2422.7 11.7 all-gather.59
  2471.2 10.7 reduce-scatter.45
  2488.9 11.7 all-gather.61
  2985.4 63.2 reduce-scatter.47
  3052.3 62.9 reduce-scatter.49
  3121.0 10.5 reduce-scatter.51
  3168.0 11.7 all-gather.63
  3216.6 10.7 reduce-scatter.53
  3234.2 11.7 all-gather.65
  3731.8 63.2 reduce-scatter.57
  3799.3 62.8 reduce-scatter.55
  3864.4 10.5 reduce-scatter.35
  3878.7 60.8 reduce-scatter.65
  3943.5 60.8 reduce-scatter.63
  4007.2 10.8 reduce-scatter.59
  4021.7 89.8 reduce-scatter.67
  4115.6 87.8 reduce-scatter.61
  4206.9 192.3 reduce-scatter.69
  4402.8 191.7 reduce-scatter.71
  4598.0 192.1 reduce-scatter.73
where the time goes:
time: 4810 us; the launch traced here: 4800 us
  matrix products  2210 us (46%)
  waiting for transfers between devices  2030 us (42%)
  other arithmetic  308 us (6%)
  blocking collectives  111 us (2%)
  local copies, waits for them, and re-layouts  103 us (2%)
    dot_general x6, matrix products, per_group(): jnp.einsum('gct,gcd->td', grad_scores, query_group, preferred_element_typ...  494 us
    dot_general x6, matrix products, per_group(): jnp.einsum('gct,td->gcd', grad_scores, key_group, preferred_element_type=...  493 us
    dot_general x12, matrix products, per_group(): jnp.einsum('gcd,td->gct', query_group, key_group, preferred_element_type=...  318 us
    reduce_scatter x1, waiting for transfers between devices, shards(): lax.psum_scatter(running[6].astype(jnp.bfloat16), 'wide', scatter_dimensi...  194 us
    reduce_scatter x1, waiting for transfers between devices, shards(): lax.psum_scatter(running[8].astype(jnp.bfloat16), 'wide', scatter_dimensi...  193 us
    reduce_scatter x1, waiting for transfers between devices, shards(): lax.psum_scatter(running[7].astype(jnp.bfloat16), 'wide', scatter_dimensi...  192 us
    reduce_scatter x3, waiting for transfers between devices, backward_inputs(): lax.psum_scatter(grad_key_part.astype(jnp.bfloat16), 'wide', scatter_dime...  171 us
    reduce_scatter x3, waiting for transfers between devices, backward_inputs(): lax.psum_scatter(grad_value_part.astype(jnp.bfloat16), 'wide', scatter_di...  169 us
  transfers between devices with their start and end apart: 52, of which 41 were waited for; matrix products, arithmetic and copies ran while one was open for 11% of the time, Pallas kernels for 0%

commit v1 on v0

v1 whole, which is shorter than its diff:
```python
import functools
import math

import jax
import jax.numpy as jnp
from jax import lax
from jax.experimental import pallas as pl
from jax.experimental.pallas import tpu as pltpu
from jax.sharding import PartitionSpec as P

HD = 64
PAIR = 2 * HD
EPSILON = 1e-05
GAIN_ROWS = 16
VMEM = 48 * 2**20
BF = jnp.bfloat16
F32 = jnp.float32
ANY = pl.BlockSpec(memory_space=pl.ANY)


def partner(x, axis, bit):
    peers = lax.axis_size(axis)
    return lax.ppermute(x, axis, [(i, i ^ bit) for i in range(peers)])


def after(value, *events):
    return lax.optimization_barrier((value,) + events)[0]


def product(left, right):
    return jnp.dot(left, right, preferred_element_type=F32)


def cross(left, right):
    return lax.dot_general(left, right, (((0,), (0,)), ((), ())), preferred_element_type=F32)


def against(left, right):
    return lax.dot_general(left, right, (((1,), (1,)), ((), ())), preferred_element_type=F32)


def call(body, ins, outs, scratch, flops, exps=0, **more):
    moved = sum(x.size * x.dtype.itemsize for x in list(ins) + list(outs))
    return pl.pallas_call(
        body,
        out_shape=outs,
        scratch_shapes=scratch,
        compiler_params=pltpu.CompilerParams(vmem_limit_bytes=VMEM),
        cost_estimate=pl.CostEstimate(
            flops=int(flops), bytes_accessed=int(moved), transcendentals=int(exps)
        ),
        **more,
    )(*ins)


def shaped(*dims, kind=BF):
    return jax.ShapeDtypeStruct(dims, kind)


def lines():
    count = lax.axis_size("wide")
    return [list(range(y, count, 2)) for y in range(2)]


def side():
    return lax.axis_index("wide") % 2


def gather_line(shard):
    return lax.all_gather(shard, "wide", axis=0, tiled=True, axis_index_groups=lines())


def reduce_line(near):
    return lax.psum_scatter(
        near, "wide", scatter_dimension=0, tiled=True, axis_index_groups=lines()
    )


def gather_blocks(shard):
    count = lax.axis_size("wide")
    far = [shard if k == 0 else partner(shard, "wide", k) for k in range(0, count, 2)]
    blocks = []
    for block in far:
        blocks += [block, partner(block, "wide", 1)]
    return blocks


def reduce_blocks(send, keep):
    near = keep.astype(F32) + partner(send, "wide", 1).astype(F32)
    total = near[0]
    for j in range(1, keep.shape[0]):
        total = total + partner(near[j].astype(BF), "wide", 2 * j).astype(F32)
    return total


def mirror(x):
    count = lax.axis_size("wide")
    pairs = []
    for w in range(count):
        pairs.append((2 * w, 2 * w))
        pairs.append((2 * w + 1, 2 * (count - 1 - w) + 1))
    return lax.ppermute(x, ("wide", "tp"), pairs)


def spread(values):
    other = partner(values, "section", 1)
    return [values, other, partner(values, "tp", 1), partner(other, "tp", 1)]


def fold(own, send):
    rows = own.shape[0] // 2
    got = partner(send, "tp", 1)
    away = (own[rows:].astype(F32) + got[rows:].astype(F32)).astype(BF)
    mine = own[:rows].astype(F32) + got[:rows].astype(F32)
    return mine + partner(away, "section", 1).astype(F32)


def load_attn(ref, dest, sem, depth, start):
    copies = []
    for k in range(dest.shape[0] // depth):
        copies.append(
            pltpu.make_async_copy(
                ref.at[pl.ds(k * (depth + GAIN_ROWS), depth), pl.ds(start, dest.shape[1])],
                dest.at[pl.ds(k * depth, depth)],
                sem.at[k],
            )
        )
        copies[-1].start()
    return copies


def load_sides(refs, dest, sem, depth, first=0):
    copies = []
    y = side()
    for s, ref in enumerate(refs):
        for j in range(dest.shape[0] // (2 * depth)):
            place = pl.multiple_of((2 * j + (y + s) % 2) * depth, depth)
            copies.append(
                pltpu.make_async_copy(
                    ref.at[pl.ds(j * depth, depth)],
                    dest.at[pl.ds(place, depth)],
                    sem.at[first + 2 * j + s],
                )
            )
            copies[-1].start()
    return copies


def qkv_kernel(depth, *refs):
    pieces, attn, tables = refs[:4], refs[4], refs[5:9]
    q_ref, kv_ref, w, sem = refs[9:]
    width = w.shape[1]
    for copy in load_attn(attn, w, sem, depth, 0):
        copy.wait()
    cos, sin, cos_kv, sin_kv = tables
    for p, piece in enumerate(pieces):
        linear = product(piece[...], w[...])
        micro, rows = q_ref.shape[1], q_ref.shape[2]
        first = lax.broadcasted_iota(jnp.int32, (rows, PAIR), 1) % HD < HD // 2
        span = slice(p * rows, (p + 1) * rows)
        for m in range(micro):
            for start in range(0, width, PAIR):
                part = linear[m * rows : (m + 1) * rows, start : start + PAIR]
                turned = jnp.where(
                    first, pltpu.roll(part, PAIR - HD // 2, 1), pltpu.roll(part, HD // 2, 1)
                )
                if start + PAIR < width:
                    out = part * cos[span] + turned * sin[span]
                    q_ref[p, m, :, start : start + PAIR] = out.astype(BF)
                else:
                    out = part * cos_kv[span] + turned * sin_kv[span]
                    kv_ref[p, m] = out.astype(BF)


def qkv_project(pieces, attn, tables, micro, depth, width):
    total, d = pieces[0].shape
    rows = total // micro
    vmem = pl.BlockSpec(memory_space=pltpu.VMEM)
    return call(
        functools.partial(qkv_kernel, depth),
        [*pieces, attn, *tables],
        [shaped(4, micro, rows, width - PAIR), shaped(4, micro, rows, PAIR)],
        [pltpu.VMEM((d, width), BF), pltpu.SemaphoreType.DMA((d // depth,))],
        8 * total * d * width,
        in_specs=[vmem] * 4 + [ANY] + [vmem] * 4,
        out_specs=[vmem] * 2,
    )


def gate_up_kernel(depth, *refs):
    pieces, gates, ups = refs[:4], refs[4:6], refs[6:8]
    outs = refs[8:11]
    x, w_gate, w_up, buffer, x_sem, w_sem, out_sem = refs[11:]
    copies = load_sides(gates, w_gate, w_sem, depth)
    copies += load_sides(ups, w_up, w_sem, depth, w_gate.shape[0] // depth)
    inputs = []
    for p, piece in enumerate(pieces):
        inputs.append(pltpu.make_async_copy(piece, x.at[p], x_sem.at[p]))
        inputs[-1].start()
    for copy in copies:
        copy.wait()
    rows = x.shape[1]
    results = []
    for p in range(4):
        inputs[p].wait()
        gate = product(x[p], w_gate[...])
        up = product(x[p], w_up[...])
        if p >= 2:
            for copy in results[p - 2]:
                copy.wait()
        slot = p % 2
        buffer[slot, 0] = gate.astype(BF)
        buffer[slot, 1] = up.astype(BF)
        buffer[slot, 2] = (gate * jax.nn.sigmoid(gate) * up).astype(BF)
        results.append(
            [
                pltpu.make_async_copy(
                    buffer.at[slot, i], outs[i].at[pl.ds(p * rows, rows)], out_sem.at[p, i]
                )
                for i in range(3)
            ]
        )
        for copy in results[p]:
            copy.start()
    for p in (2, 3):
        for copy in results[p]:
            copy.wait()


def gate_up(pieces, gates, ups, depth):
    rows, d = pieces[0].shape
    hidden = gates[0].shape[1]
    return call(
        functools.partial(gate_up_kernel, depth),
        [*pieces, *gates, *ups],
        [shaped(4 * rows, hidden)] * 3,
        [
            pltpu.VMEM((4, rows, d), BF),
            pltpu.VMEM((d, hidden), BF),
            pltpu.VMEM((d, hidden), BF),
            pltpu.VMEM((2, 3, rows, hidden), BF),
            pltpu.SemaphoreType.DMA((4,)),
            pltpu.SemaphoreType.DMA((2 * d // depth,)),
            pltpu.SemaphoreType.DMA((4, 3)),
        ],
        16 * rows * d * hidden,
        4 * rows * hidden,
        in_specs=[ANY] * 8,
        out_specs=[ANY] * 3,
    )


def hidden_back_kernel(depth, *refs):
    pieces, downs = refs[:4], refs[4:6]
    gate_ref, up_ref = refs[6:8]
    outs = refs[8:10]
    x, w, kept, buffer, x_sem, w_sem, kept_sem, out_sem = refs[10:]
    copies = load_sides(downs, w, w_sem, depth)
    rows = x.shape[1]
    inputs = []
    for p, piece in enumerate(pieces):
        span = pl.ds(p * rows, rows)
        inputs.append(
            [
                pltpu.make_async_copy(piece, x.at[p], x_sem.at[p]),
                pltpu.make_async_copy(gate_ref.at[span], kept.at[p, 0], kept_sem.at[p, 0]),
                pltpu.make_async_copy(up_ref.at[span], kept.at[p, 1], kept_sem.at[p, 1]),
            ]
        )
        for copy in inputs[-1]:
            copy.start()
    for copy in copies:
        copy.wait()
    results = []
    for p in range(4):
        for copy in inputs[p]:
            copy.wait()
        grad = product(x[p], w[...])
        gate = kept[p, 0].astype(F32)
        up = kept[p, 1].astype(F32)
        sigma = jax.nn.sigmoid(gate)
        if p >= 2:
            for copy in results[p - 2]:
                copy.wait()
        slot = p % 2
        buffer[slot, 0] = (grad * up * sigma * (1.0 + gate * (1.0 - sigma))).astype(BF)
        buffer[slot, 1] = (grad * gate * sigma).astype(BF)
        results.append(
            [
                pltpu.make_async_copy(
                    buffer.at[slot, i], outs[i].at[pl.ds(p * rows, rows)], out_sem.at[p, i]
                )
                for i in range(2)
            ]
        )
        for copy in results[p]:
            copy.start()
    for p in (2, 3):
        for copy in results[p]:
            copy.wait()


def hidden_back(pieces, downs, gate, up, depth):
    rows, d = pieces[0].shape
    hidden = downs[0].shape[1]
    return call(
        functools.partial(hidden_back_kernel, depth),
        [*pieces, *downs, gate, up],
        [shaped(4 * rows, hidden)] * 2,
        [
            pltpu.VMEM((4, rows, d), BF),
            pltpu.VMEM((d, hidden), BF),
            pltpu.VMEM((4, 2, rows, hidden), BF),
            pltpu.VMEM((2, 2, rows, hidden), BF),
            pltpu.SemaphoreType.DMA((4,)),
            pltpu.SemaphoreType.DMA((d // depth,)),
            pltpu.SemaphoreType.DMA((4, 2)),
            pltpu.SemaphoreType.DMA((4, 2)),
        ],
        8 * rows * d * hidden,
        4 * rows * hidden,
        in_specs=[ANY] * 8,
        out_specs=[ANY] * 2,
    )


def out_back_kernel(depth, offset, *refs):
    pieces, attn = refs[:4], refs[4]
    out_ref, w, sem = refs[5:]
    for copy in load_attn(attn, w, sem, depth, offset):
        copy.wait()
    rows = pieces[0].shape[0]
    for p, piece in enumerate(pieces):
        out_ref[p * rows : (p + 1) * rows] = product(piece[...], w[...]).astype(BF)


def out_back(pieces, attn, depth, offset, width):
    rows, d = pieces[0].shape
    vmem = pl.BlockSpec(memory_space=pltpu.VMEM)
    return call(
        functools.partial(out_back_kernel, depth, offset),
        [*pieces, attn],
        [shaped(4 * rows, width)],
        [pltpu.VMEM((d, width), BF), pltpu.SemaphoreType.DMA((d // depth,))],
        8 * rows * d * width,
        in_specs=[vmem] * 4 + [ANY],
        out_specs=[vmem],
    )[0]


def contract_kernel(depth, starts, *refs):
    sides = len(starts)
    lefts, refs = refs[:sides], refs[sides:]
    sources = []
    for start in starts:
        size = 2 if start is None else 1
        sources.append(refs[:size])
        refs = refs[size:]
    own_ref, send_ref = refs[:2]
    weights, sem = refs[2:-1], refs[-1]
    step = pl.program_id(0)
    half = pl.num_programs(0) // 2

    @pl.when(step == 0)
    def _():
        copies = []
        for s, start in enumerate(starts):
            if start is None:
                copies += load_sides(sources[s], weights[s], sem.at[s], depth)
            else:
                copies += load_attn(sources[s][0], weights[s], sem.at[s], depth, start)
        for copy in copies:
            copy.wait()

    total = against(lefts[0][...], weights[0][...])
    for s in range(1, sides):
        total = total + against(lefts[s][...], weights[s][...])
    total = total.astype(BF)

    @pl.when(step < half)
    def _():
        send_ref[...] = total

    @pl.when(step >= half)
    def _():
        own_ref[...] = total


def contract(lefts, sources, starts, depth, width):
    sides = len(lefts)
    total = lefts[0].shape[0]
    tile = total // 4
    flat = [ref for group in sources for ref in group]
    return call(
        functools.partial(contract_kernel, depth, starts),
        [*lefts, *flat],
        [shaped(total // 2, width)] * 2,
        [pltpu.VMEM((width, left.shape[1]), BF) for left in lefts]
        + [pltpu.SemaphoreType.DMA((sides, width // depth))],
        sum(2 * total * left.shape[1] * width for left in lefts),
        grid=(4,),
        in_specs=[
            pl.BlockSpec((tile, left.shape[1]), lambda i: ((i + 2) % 4, 0)) for left in lefts
        ]
        + [ANY] * len(flat),
        out_specs=[
            pl.BlockSpec((tile, width), lambda i: (jnp.maximum(i - 2, 0), 0)),
            pl.BlockSpec((tile, width), lambda i: (jnp.minimum(i, 1), 0)),
        ],
    )


def weight_kernel(x0, x1, x2, x3, right_ref, send_ref, keep_ref):
    left = jnp.concatenate([x0[...], x1[...], x2[...], x3[...]], axis=0)
    grad = cross(left, right_ref[...]).astype(BF)
    depth = keep_ref.shape[1]
    for y, (first, second) in enumerate(((keep_ref, send_ref), (send_ref, keep_ref))):

        @pl.when(side() == y)
        def _():
            first[0] = grad[:depth]
            second[0] = grad[depth:]


def weight_grad(pieces, right, n):
    rows, d = pieces[0].shape
    width = right.shape[1]
    depth = d // n
    out = pl.BlockSpec((1, depth, width), lambda j: (j, 0, 0))
    return call(
        weight_kernel,
        [*pieces, right],
        [shaped(n // 2, depth, width)] * 2,
        [],
        8 * rows * d * width,
        grid=(n // 2,),
        in_specs=[pl.BlockSpec((rows, 2 * depth), lambda j: (0, j))] * 4
        + [pl.BlockSpec((4 * rows, width), lambda j: (0, 0))],
        out_specs=[out, out],
    )


def attn_weight_kernel(*refs):
    xs, gs = refs[:4], refs[4:8]
    dq_ref, dkv_ref, att_ref, gain_ref, send_ref, keep_ref = refs[8:]
    depth = keep_ref.shape[1] - GAIN_ROWS
    left = jnp.concatenate([x[...] for x in xs], axis=0)
    grad = jnp.concatenate([g[...] for g in gs], axis=0)
    start = 0
    for source, right in ((left, dq_ref), (left, dkv_ref), (grad, att_ref)):
        term = cross(source, right[...]).astype(BF)
        span = slice(start, start + right.shape[1])
        start += right.shape[1]
        for y, (first, second) in enumerate(((keep_ref, send_ref), (send_ref, keep_ref))):

            @pl.when(side() == y)
            def _():
                first[0, :depth, span] = term[:depth]
                second[0, :depth, span] = term[depth:]

    for y, (first, second) in enumerate(((keep_ref, send_ref), (send_ref, keep_ref))):

        @pl.when(side() == y)
        def _():
            first[0, depth:] = gain_ref[0, 0]
            second[0, depth:] = gain_ref[0, 1]


def attn_weight_grad(xs, gs, dq, dkv, attended, gains, n):
    rows, d = xs[0].shape
    depth = d // n
    width = dq.shape[1] + dkv.shape[1] + attended.shape[1]
    out = pl.BlockSpec((1, depth + GAIN_ROWS, width), lambda j: (j, 0, 0))
    whole = lambda x: pl.BlockSpec(x.shape, lambda j: (0, 0))
    return call(
        attn_weight_kernel,
        [*xs, *gs, dq, dkv, attended, gains],
        [shaped(n // 2, depth + GAIN_ROWS, width)] * 2,
        [],
        8 * rows * d * width,
        grid=(n // 2,),
        in_specs=[pl.BlockSpec((rows, 2 * depth), lambda j: (0, j))] * 8
        + [
            whole(dq),
            whole(dkv),
            whole(attended),
            pl.BlockSpec((1, 2, GAIN_ROWS, width), lambda j: (j, 0, 0, 0)),
        ],
        out_specs=[out, out],
    )


def stack_heads(x):
    return jnp.concatenate([x[:, h : h + HD] for h in range(0, x.shape[1], HD)], axis=0)


def turn_heads(x):
    pairs = [x[:, g : g + PAIR].T for g in range(0, x.shape[1], PAIR)]
    return jnp.concatenate([part for pair in pairs for part in (pair[:HD], pair[HD:])], axis=1)


def back_heads(x, rows, g):
    even = x[:, 2 * g * rows : (2 * g + 1) * rows]
    odd = x[:, (2 * g + 1) * rows : (2 * g + 2) * rows]
    return jnp.concatenate([even, odd], axis=0).T


def attend_kernel(
    block, loc_ref, pos_ref, q_ref, kv_ref, o_ref, lse_ref, k_ref, vt_ref, m_ref, acc_ref
):
    piece = pl.program_id(1)
    rows = q_ref.shape[2]
    count = kv_ref.shape[0]
    per_block = block // rows

    @pl.when(piece == 0)
    def _():
        def one(i, _):
            kv = kv_ref[loc_ref[i], 0]
            k_ref[i] = kv[:, :HD]
            ones = jnp.ones((GAIN_ROWS, rows), BF)
            vt_ref[i] = jnp.concatenate([kv.T[HD:], ones], axis=0)
            return 0

        lax.fori_loop(0, count, one, 0)

    pos = pos_ref[piece]
    queries = turn_heads(q_ref[0, 0] * BF(1.0 / math.sqrt(HD)))
    m_ref[...] = jnp.full(m_ref.shape, -1e30, F32)
    acc_ref[...] = jnp.zeros(acc_ref.shape, F32)

    def step(j, masked):
        first = j * per_block
        keys = jnp.concatenate([k_ref[first + i] for i in range(per_block)], axis=0)
        values = jnp.concatenate([vt_ref[first + i] for i in range(per_block)], axis=1)
        scores = product(keys, queries)
        if masked:
            row = lax.broadcasted_iota(jnp.int32, scores.shape, 0)
            column = lax.broadcasted_iota(jnp.int32, scores.shape, 1) % rows
            scores = jnp.where(row + j * block <= column + pos, scores, -1e30)
        before = m_ref[...]
        now = jnp.maximum(before, jnp.max(scores, axis=0, keepdims=True))
        terms = jnp.exp(scores - now)
        shrink = jnp.exp(before - now)
        acc_ref[...] = acc_ref[...] * shrink + product(values, terms.astype(BF))
        m_ref[...] = now

    full = pos // block

    def loop(j, _):
        step(j, False)
        return 0

    lax.fori_loop(0, full, loop, 0)
    step(full, True)
    total = acc_ref[HD : HD + 1]
    out = acc_ref[:HD] / total
    lse_ref[0, 0] = m_ref[...] + jnp.log(total)
    for g in range(q_ref.shape[3] // PAIR):
        o_ref[0, 0, :, g * PAIR : (g + 1) * PAIR] = back_heads(out, rows, g).astype(BF)


def attend(q, kv, loc, pos):
    pieces, micro, rows, width = q.shape
    count = kv.shape[0]
    stacked = rows * width // HD
    block = min(512, rows * count)
    scores = micro * pieces * stacked * rows * count // 2
    heads = pl.BlockSpec((1, 1, rows, width), lambda m, p, *_: (p, m, 0, 0))
    return call(
        functools.partial(attend_kernel, block),
        [loc, pos, q, kv],
        [shaped(*q.shape), shaped(pieces, micro, 1, stacked, kind=F32)],
        (),
        scores * 2750,
        scores,
        grid_spec=pltpu.PrefetchScalarGridSpec(
            num_scalar_prefetch=2,
            grid=(micro, pieces),
            in_specs=[
                heads,
                pl.BlockSpec((count, 1, rows, PAIR), lambda m, p, *_: (0, m, 0, 0)),
            ],
            out_specs=[
                heads,
                pl.BlockSpec((1, 1, 1, stacked), lambda m, p, *_: (p, m, 0, 0)),
            ],
            scratch_shapes=[
                pltpu.VMEM((count, rows, HD), BF),
                pltpu.VMEM((count, HD + GAIN_ROWS, rows), BF),
                pltpu.VMEM((1, stacked), F32),
                pltpu.VMEM((HD + GAIN_ROWS, stacked), F32),
            ],
        ),
    )


def attend_back_kernel(
    block,
    loc_ref,
    pos_ref,
    q_ref,
    do_ref,
    o_ref,
    lse_ref,
    kv_ref,
    cos_ref,
    sin_ref,
    dq_ref,
    send_ref,
    keep_ref,
    k_ref,
    v_ref,
    kt_ref,
    dq_acc,
    dk_acc,
    dv_acc,
):
    piece = pl.program_id(1)
    rows = q_ref.shape[2]
    count = kv_ref.shape[0]
    per_block = block // rows
    scale = 1.0 / math.sqrt(HD)

    @pl.when(piece == 0)
    def _():
        def one(i, _):
            kv = kv_ref[loc_ref[i], 0]
            k_ref[i] = kv[:, :HD]
            v_ref[i] = kv[:, HD:]
            kt_ref[i] = kv.T[:HD]
            dk_acc[i] = jnp.zeros(dk_acc.shape[1:], F32)
            dv_acc[i] = jnp.zeros(dv_acc.shape[1:], F32)
            return 0

        lax.fori_loop(0, count, one, 0)

    pos = pos_ref[piece]
    q = q_ref[0, 0] * BF(scale)
    do = do_ref[0, 0]
    queries, queries_t = stack_heads(q), turn_heads(q)
    grads, grads_t = stack_heads(do), turn_heads(do)
    dots = turn_heads(do.astype(F32) * o_ref[0, 0].astype(F32))
    delta = jnp.sum(dots, axis=0, keepdims=True)
    logs = lse_ref[0, 0]
    dq_acc[...] = jnp.zeros(dq_acc.shape, F32)

    def step(j, masked):
        first = j * per_block
        keys = jnp.concatenate([k_ref[first + i] for i in range(per_block)], axis=0)
        values = jnp.concatenate([v_ref[first + i] for i in range(per_block)], axis=0)
        keys_t = jnp.concatenate([kt_ref[first + i] for i in range(per_block)], axis=1)
        scores = product(keys, queries_t)
        probs = jnp.exp(scores - logs)
        if masked:
            row = lax.broadcasted_iota(jnp.int32, scores.shape, 0)
            column = lax.broadcasted_iota(jnp.int32, scores.shape, 1) % rows
            probs = jnp.where(row + j * block <= column + pos, probs, 0.0)
        grad_probs = product(values, grads_t)
        grad_low = (probs * (grad_probs - delta)).astype(BF)
        dv = product(probs.astype(BF), grads)
        dk = product(grad_low, queries)
        dq_acc[...] += product(keys_t, grad_low)
        for i in range(per_block):
            dk_acc[first + i] += dk[i * rows : (i + 1) * rows]
            dv_acc[first + i] += dv[i * rows : (i + 1) * rows]

    full = pos // block

    def loop(j, _):
        step(j, False)
        return 0

    lax.fori_loop(0, full, loop, 0)
    step(full, True)

    first = lax.broadcasted_iota(jnp.int32, (rows, PAIR), 1) % HD < HD // 2
    for g in range(q_ref.shape[3] // PAIR):
        part = back_heads(dq_acc[...], rows, g) * scale
        turned = jnp.where(
            first, pltpu.roll(part, PAIR - HD // 2, 1), pltpu.roll(part, HD // 2, 1)
        )
        out = part * cos_ref[...] - turned * sin_ref[...]
        dq_ref[0, 0, :, g * PAIR : (g + 1) * PAIR] = out.astype(BF)

    @pl.when(piece == pl.num_programs(1) - 1)
    def _():
        pieces = pl.num_programs(1)

        def one(i, _):
            grad = jnp.concatenate([dk_acc[i], dv_acc[i]], axis=1).astype(BF)
            place = loc_ref[i]
            owner = place // pieces
            slot = owner // 2 * pieces + place % pieces

            @pl.when(owner % 2 == 0)
            def _():
                keep_ref[slot, 0] = grad

            @pl.when(owner % 2 == 1)
            def _():
                send_ref[slot, 0] = grad

            return 0

        lax.fori_loop(0, count, one, 0)


def attend_back(q, grad, attended, lse, kv, cos, sin, loc, pos):
    pieces, micro, rows, width = q.shape
    count = kv.shape[0]
    stacked = rows * width // HD
    block = min(512, rows * count)
    scores = micro * pieces * stacked * rows * count // 2
    heads = pl.BlockSpec((1, 1, rows, width), lambda m, p, *_: (p, m, 0, 0))
    whole = pl.BlockSpec((count, 1, rows, PAIR), lambda m, p, *_: (0, m, 0, 0))
    half = pl.BlockSpec((count // 2, 1, rows, PAIR), lambda m, p, *_: (0, m, 0, 0))
    table = pl.BlockSpec((rows, PAIR), lambda m, p, *_: (p, 0))
    return call(
        functools.partial(attend_back_kernel, block),
        [loc, pos, q, grad, attended, lse, kv, cos, sin],
        [shaped(*q.shape)] + [shaped(count // 2, micro, rows, PAIR)] * 2,
        (),
        scores * 4600,
        scores,
        grid_spec=pltpu.PrefetchScalarGridSpec(
            num_scalar_prefetch=2,
            grid=(micro, pieces),
            in_specs=[
                heads,
                heads,
                heads,
                pl.BlockSpec((1, 1, 1, stacked), lambda m, p, *_: (p, m, 0, 0)),
                whole,
                table,
                table,
            ],
            out_specs=[heads, half, half],
            scratch_shapes=[
                pltpu.VMEM((count, rows, HD), BF),
                pltpu.VMEM((count, rows, HD), BF),
                pltpu.VMEM((count, HD, rows), BF),
                pltpu.VMEM((HD, stacked), F32),
                pltpu.VMEM((count, rows, HD), F32),
                pltpu.VMEM((count, rows, HD), F32),
            ],
        ),
    )


def rope_tables(positions):
    inverse = 1.0 / 10000.0 ** (jnp.arange(0, HD, 2).astype(F32) / HD)
    angle = positions.astype(F32)[:, None] * inverse[None, :]
    cos, sin = jnp.cos(angle), jnp.sin(angle)
    cos_head = jnp.concatenate([cos, cos], axis=1)
    sin_head = jnp.concatenate([-sin, sin], axis=1)
    ones, zeros = jnp.ones_like(cos_head), jnp.zeros_like(sin_head)
    return (
        jnp.concatenate([cos_head, cos_head], axis=1),
        jnp.concatenate([sin_head, sin_head], axis=1),
        jnp.concatenate([cos_head, ones], axis=1),
        jnp.concatenate([sin_head, zeros], axis=1),
    )


def normalize(values, gain):
    scale = lax.rsqrt(jnp.mean(values * values, axis=-1, keepdims=True) + EPSILON)
    return scale, (values * scale * gain).astype(BF)


def normalize_back(values, scale, gain, grad):
    norm = values * scale
    scaled = grad * gain
    inner = scale * (scaled - norm * jnp.mean(scaled * norm, axis=-1, keepdims=True))
    return inner, jnp.sum(grad * norm, axis=0)


class Sizes:
    def __init__(self, tokens, w_query):
        self.micro, self.held, self.width = tokens.shape
        self.rows = self.held // 2
        self.count = lax.axis_size("wide")
        self.depth = self.width // self.count
        self.heads = w_query.shape[2] // 2
        self.qkv = self.heads + PAIR


def shards(
    tokens, out_grad, attn_gain, w_query, w_key, w_value, w_out, ffn_gain, w_gate, w_up, w_down
):
    s = Sizes(tokens, w_query)
    section = lax.axis_index("section")
    wide = lax.axis_index("wide")
    core = lax.axis_index("tp")
    count, rows = s.count, s.rows
    home = section == 0

    pos = jnp.stack(
        [
            jnp.where((core ^ (p // 2)) == 0, 2 * wide, 2 * count - 1 - 2 * wide) * s.held
            + (section ^ (p % 2)) * rows
            for p in range(4)
        ]
    ).astype(jnp.int32)
    order = jnp.arange(4 * count)
    half_block = order // 2
    odd = half_block % 2
    owner = jnp.where(odd == 0, half_block, 2 * count - 1 - half_block) // 2
    loc = ((owner ^ wide) * 4 + (odd ^ core) * 2 + ((order % 2) ^ section)).astype(jnp.int32)
    positions = (pos[:, None] + jnp.arange(rows)[None, :]).reshape(-1)
    tables = rope_tables(positions)
    place = (tables, loc, pos)

    def halves(array, axis):
        size = array.shape[axis] // 2
        own = lax.dynamic_slice_in_dim(array, section * size, size, axis)
        away = lax.dynamic_slice_in_dim(array, (1 - section) * size, size, axis)
        return own, away

    def pack_attn(parts):
        query, key, value, out = parts
        main = jnp.concatenate([query, key, value, out.T], axis=1)
        gains = jnp.concatenate([attn_gain, ffn_gain], axis=0)
        gains = jnp.pad(gains, ((0, GAIN_ROWS - 2), (0, main.shape[1] - gains.shape[1])))
        return jnp.concatenate([main, gains], axis=0)

    def both_layers(own, away):
        other = partner(away, "section", 1)
        return jnp.where(home, own, other), jnp.where(home, other, own)

    def take(values):
        part = lax.dynamic_slice_in_dim(values, section * rows, rows, 1)
        return mirror(part).reshape(-1, s.width)

    attn = [halves(w_query[0], 1), halves(w_key[0], 1), halves(w_value[0], 1), halves(w_out[0], 0)]
    gate_h, up_h, down_h = halves(w_gate[0], 1), halves(w_up[0], 1), halves(w_down[0], 0)
    attn_l = both_layers(*[pack_attn([part[i] for part in attn]) for i in range(2)])
    gate_l = both_layers(*gate_h)
    up_l = both_layers(*up_h)
    down_l = both_layers(*[half.T for half in down_h])

    u = take(tokens).astype(F32)
    layers, kept, outs = [], [], []
    for layer in range(2):
        attn = lax.all_gather(
            after(attn_l[layer], *layers[0][2]) if layer else attn_l[layer],
            "wide",
            axis=0,
            tiled=True,
        )
        by_block = attn.reshape(count, s.depth + GAIN_ROWS, -1)
        gains = by_block[:, s.depth : s.depth + 2, : s.depth]
        gains = gains.transpose(1, 0, 2).reshape(2, s.width).astype(F32)
        first_scale, low = normalize(u, gains[0])
        normed = spread(low)
        line_gate = gather_line(after(gate_l[layer], attn))
        q, kv_own = qkv_project(normed, attn, tables, s.micro, s.depth, s.qkv)
        kv = jnp.concatenate(gather_blocks(kv_own), axis=0)
        line_up = gather_line(after(up_l[layer], kv))
        gate_w = (line_gate, partner(after(line_gate, kv), "wide", 1))
        attended, lse = attend(q, kv, loc, pos)
        flat = attended.reshape(-1, s.heads)
        own, send = contract([flat], [(attn,)], (s.qkv,), s.depth, s.width)
        line_down = gather_line(after(down_l[layer], line_up))
        up_w = (line_up, partner(after(line_up, gate_w[1], own), "wide", 1))
        middle = u + fold(own, send)
        second_scale, low = normalize(middle, gains[1])
        normed_ffn = spread(low)
        gate, up, hidden = gate_up(normed_ffn, gate_w, up_w, s.depth)
        down_w = (line_down, partner(after(line_down, up_w[1]), "wide", 1))
        own, send = contract([hidden], [down_w], (None,), s.depth, s.width)
        result = middle + fold(own, send)
        layers.append((gains, attn, gate_w, up_w, down_w))
        kept.append(
            (u, first_scale, normed, q, kv, attended, lse, middle, second_scale, normed_ffn)
            + (gate, up, hidden)
        )
        outs.append(result.astype(BF))
        u = outs[layer].astype(F32)

    def reduce(send, keep, *events):
        got = partner(after(send, *events), "wide", 1)
        near = (keep.astype(F32) + got.astype(F32)).astype(BF)
        return reduce_line(near.reshape(-1, near.shape[-1])).astype(F32)

    upstream = take(out_grad).astype(F32)
    grads, terms = [None, None], [None, None]
    for layer in (1, 0):
        gains, attn, gate_w, up_w, down_w = layers[layer]
        u, first_scale, normed, q, kv, attended, lse, middle, second_scale, normed_ffn = kept[
            layer
        ][:10]
        gate, up, hidden = kept[layer][10:]
        grad2 = spread(upstream.astype(BF))
        grad_gate, grad_up = hidden_back(grad2, down_w, gate, up, s.depth)
        own, send = contract(
            [grad_gate, grad_up], [gate_w, up_w], (None, None), s.depth, s.width
        )
        d_down = reduce(*weight_grad(grad2, hidden, count))
        inner, second_gain = normalize_back(middle, second_scale, gains[1], fold(own, send))
        grad_middle = upstream + inner
        grad1 = spread(grad_middle.astype(BF))
        d_gate = reduce(*weight_grad(normed_ffn, grad_gate, count))
        grad_attended = out_back(grad1, attn, s.depth, s.qkv, s.heads).reshape(q.shape)
        dq, send, keep = attend_back(
            q, grad_attended, attended, lse, kv, tables[0], tables[1], loc, pos
        )
        halved = lambda x: x.reshape(count // 2, 4, s.micro, rows, PAIR)
        dkv = reduce_blocks(halved(send), halved(keep))
        d_up = reduce(*weight_grad(normed_ffn, grad_up, count), dkv)
        half = HD // 2
        turned = jnp.concatenate(
            [dkv[..., half:HD], dkv[..., :half], jnp.zeros_like(dkv[..., HD:])], axis=-1
        )
        by_piece = lambda table: table.reshape(4, 1, rows, PAIR)
        dkv = (dkv * by_piece(tables[2]) - turned * by_piece(tables[3])).astype(BF)
        dq, dkv = dq.reshape(-1, s.heads), dkv.reshape(-1, PAIR)
        own, send = contract([dq, dkv], [(attn,), (attn,)], (0, s.heads), s.depth, s.width)
        inner, first_gain = normalize_back(u, first_scale, gains[0], fold(own, send))
        grads[layer] = (grad_middle + inner).astype(BF)
        gain_rows = jnp.stack([first_gain, second_gain]).astype(BF)
        gain_rows = gain_rows.reshape(2, count // 2, 2, s.depth).transpose(1, 2, 0, 3)
        gain_rows = jnp.pad(
            gain_rows,
            ((0, 0), (0, 0), (0, GAIN_ROWS - 2), (0, s.qkv + s.heads - s.depth)),
        )
        d_attn = reduce(
            *attn_weight_grad(
                normed, grad1, dq, dkv, attended.reshape(-1, s.heads), gain_rows, count
            )
        )
        terms[layer] = (d_attn, d_gate, d_up, d_down)
        upstream = grads[layer].astype(F32)

    def give(first, second):
        first, second = [x.reshape(s.micro, rows, s.width) for x in (first, second)]
        own = jnp.where(home, first, second)
        other = partner(jnp.where(home, second, first), "section", 1)
        both = jnp.concatenate(
            [jnp.where(home, own, other), jnp.where(home, other, own)], axis=1
        )
        return mirror(both)

    section_out = give(*outs)
    input_grads = give(*grads)

    def settle(index):
        first, second = terms[0][index], terms[1][index]
        own = jnp.where(home, first, second)
        other = partner(jnp.where(home, second, first).astype(BF), "section", 1).astype(F32)
        return jnp.where(home, own, other), jnp.where(home, other, own)

    depth, heads = s.depth, s.heads
    low, high = settle(0)
    cut = lambda start, size: jnp.concatenate(
        [low[:depth, start : start + size], high[:depth, start : start + size]], axis=1
    )
    d_query = cut(0, heads)
    d_key = cut(heads, HD)
    d_value = cut(heads + HD, HD)
    d_out = jnp.concatenate([low[:depth, s.qkv :].T, high[:depth, s.qkv :].T], axis=0)
    gains = (low + high)[depth : depth + 2, :depth]
    gains = gains + partner(gains, "tp", 1)
    d_gate = jnp.concatenate(settle(1), axis=1)
    d_up = jnp.concatenate(settle(2), axis=1)
    d_down = jnp.concatenate([half.T for half in settle(3)], axis=0)
    return (
        section_out[None],
        input_grads[None],
        gains[0:1],
        d_query[None],
        d_key[None],
        d_value[None],
        d_out[None],
        gains[1:2],
        d_gate[None],
        d_up[None],
        d_down[None],
    )


def solution(mesh):
    return jax.shard_map(
        shards,
        mesh=mesh,
        in_specs=(
            P(None, ("wide", "tp"), None),
            P(None, ("wide", "tp"), None),
            P("section", "wide"),
            P("section", "wide", "tp"),
            P("section", "wide", "tp"),
            P("section", "wide", "tp"),
            P("section", "tp", "wide"),
            P("section", "wide"),
            P("section", "wide", "tp"),
            P("section", "wide", "tp"),
            P("section", "tp", "wide"),
        ),
        out_specs=(
            P("section", None, ("wide", "tp"), None),
            P("section", None, ("wide", "tp"), None),
            P("section", "wide"),
            P("section", "wide", "tp"),
            P("section", "wide", "tp"),
            P("section", "wide", "tp"),
            P("section", "tp", "wide"),
            P("section", "wide"),
            P("section", "wide", "tp"),
            P("section", "wide", "tp"),
            P("section", "tp", "wide"),
        ),
        check_vma=False,
    )
```

time: 4810 us -> 1880 us (0.39)
  matrix products: 2210 us -> 0 us
  waiting for transfers between devices: 2030 us -> 1010 us
  Pallas kernels: 0 us -> 507 us
  other arithmetic: 308 us -> 111 us
  starting transfers between devices: 14 us -> 156 us
  blocking collectives: 111 us -> 0 us
    dot_general x105 -> x0, matrix products: 2210 us -> none  [the longest x6 494 us: per_group(): jnp.einsum('gct,gcd->td', grad_scores, query_group, preferred_element_typ...]
    reduce_scatter x25 -> x8, waiting for transfers between devices: 1120 us -> 36 us  [reduce_line(): lax.psum_scatter(near, 'wide', scatter_dimension=0, tiled=True, axis_inde...]
    ppermute x4 -> x91, waiting for transfers between devices: 90.2 us -> 862 us  [the longest x87 826 us: partner(): return lax.ppermute(x, axis, [(i, i ^ bit) for i in range(peers)])]
    all_gather x23 -> x8, waiting for transfers between devices: 822 us -> 115 us  [the longest x2 60.7 us: shards(): lax.all_gather(after(attn_l[layer], *layers[0][2]) if layer else attn_l[l...]
    pallas_call x0 -> x28, Pallas kernels: none -> 507 us  [call(): pl.pallas_call(body, out_shape=outs, scratch_shapes=scratch, compiler_par...]
    ppermute x4 -> x91, starting transfers between devices: 10.7 us -> 155 us  [the longest x87 137 us: partner(): return lax.ppermute(x, axis, [(i, i ^ bit) for i in range(peers)])]
    reduce_sum x18 -> x8, other arithmetic: 158 us -> 15.9 us  [the longest x4 8 us: normalize(): jnp.mean(values * values, axis=-1, keepdims=True) + EPSILON]
    all_gather x4 -> x0, blocking collectives: 85 us -> none  [the longest x1 26.1 us: shards(): lax.all_gather(w_value[0], 'wide', axis=0, tiled=True)]
  transfers between devices with their start and end apart: 52 -> 107, of which waited for: 41 -> 59; matrix products, arithmetic and copies ran while one was open for 11% -> 6% of each run, Pallas kernels for 0% -> 21%
where the time goes in v1:
time: 1880 us; the launch traced here: 1860 us
  waiting for transfers between devices  1010 us (54%)
  Pallas kernels  507 us (27%)
  starting transfers between devices  156 us (8%)
  other arithmetic  111 us (6%)
  local copies, waits for them, and re-layouts  56.4 us (3%)
    ppermute x87, waiting for transfers between devices, partner(): return lax.ppermute(x, axis, [(i, i ^ bit) for i in range(peers)])  826 us
    pallas_call x28, Pallas kernels, call(): pl.pallas_call(body, out_shape=outs, scratch_shapes=scratch, compiler_par...  507 us
    ppermute x87, starting transfers between devices, partner(): return lax.ppermute(x, axis, [(i, i ^ bit) for i in range(peers)])  137 us
    all_gather x2, waiting for transfers between devices, shards(): lax.all_gather(after(attn_l[layer], *layers[0][2]) if layer else attn_l[l...  60.7 us
    all_gather x6, waiting for transfers between devices, gather_line(): lax.all_gather(shard, 'wide', axis=0, tiled=True, axis_index_groups=lines())  54.6 us
  transfers between devices with their start and end apart: 107, of which 59 were waited for; matrix products, arithmetic and copies ran while one was open for 6% of the time, Pallas kernels for 21%

profile of v1, /device:TPU:1, one launch (start us, length us, event | category | flops | bytes accessed | tf_op | source)
XLA Modules:
  0.0 1860.0 jit_solution(5983272688544647930)
XLA Ops:
  16.5 13.0 collective-permute-done.1
  53.2 16.4 collective-permute-done
  70.0 60.7 %all-gather.9.cloned.1.call-done.refs_4_.refs_1_.refs_2_.refs_3_ = bf16[2176,1152]{1,0:T(8,128)(2,1)} async-done(((bf16[272,1152]{1,0:T(8,128)(2,1)}), bf16[2176,1152]{1,0:T(8,128)(2,1)}) %all-gather.9.cloned.1.call-update) | async-done | bytes 5013520 | tf_op jit(solution)/shard_map/all_gather | solution.py:845
  135.6 20.0 %collective-permute-done.2.refs_1_ = bf16[256,2048]{1,0:T(8,128)(2,1)S(1)} collective-permute-done((bf16[256,2048]{1,0:T(8,128)(2,1)S(1)}, bf16[256,2048]{1,0:T(8,128)(2,1)S(1)}, u32[]{:S(2)}, u32[]{:S(2)}) %collective-permute-start.2) | collective-permute-done | bytes 1048608 | tf_op jit(solution)/shard_map/ppermute | solution.py:23
  182.4 14.0 collective-permute-done.6
  219.6 15.4 collective-permute-done.21
  238.5 41.3 %all-gather.13.cloned.1.call-done.refs_6_.refs_4_ = bf16[1024,1408]{1,0:T(8,128)(2,1)} async-done(((bf16[256,1408]{1,0:T(8,128)(2,1)}), bf16[1024,1408]{1,0:T(8,128)(2,1)}) %all-gather.13.cloned.1.call-update) | async-done | bytes 2883600 | tf_op jit(solution)/shard_map/all_gather | solution.py:70
  282.0 41.9 %shard_map.195 = (bf16[4,2,128,512]{3,2,1,0:T(8,128)(2,1)S(1)}, f32[4,2,1,1024]{3,2,1,0:T(1,128)S(1)}) custom-call(s32[32]{0:T(128)S(1)} %fusion.51.loc_ref, s32[4]{0:T(128)S(1)} %pad_add_fusion.pos_ref, bf16[4,2,128,512]{3,2,1,0:T(8,128)(2,1)S(1)} %copy-done.42, bf16[32,2,128,128]{3,2,1,0:T(8,128)(2,1)S(1)} %copy-done.38), custom_call_target="tpu_custom_call" | custom-call | flops 46137344000 | bytes 4227216 | tf_op jit(solution)/shard_map/pallas_call | solution.py:44
  339.3 23.2 %collective-permute-done.13 = bf16[256,2048]{1,0:T(8,128)(2,1)} collective-permute-done((bf16[256,2048]{1,0:T(8,128)(2,1)S(1)}, bf16[256,2048]{1,0:T(8,128)(2,1)}, u32[]{:S(2)}, u32[]{:S(2)}) %collective-permute-start.13) | collective-permute-done | bytes 1048608 | tf_op jit(solution)/shard_map/ppermute | solution.py:23
  367.9 53.2 %collective-permute-done.20.refs_7_.refs_5_ = bf16[1024,1408]{1,0:T(8,128)(2,1)} collective-permute-done((bf16[1024,1408]{1,0:T(8,128)(2,1)}, bf16[1024,1408]{1,0:T(8,128)(2,1)}, u32[]{:S(2)}, u32[]{:S(2)}) %collective-permute-start.20) | collective-permute-done | bytes 2883616 | tf_op jit(solution)/shard_map/ppermute | solution.py:23
  429.2 20.8 %shard_map.197 = (bf16[1024,1408]{1,0:T(8,128)(2,1)}, bf16[1024,1408]{1,0:T(8,128)(2,1)}, bf16[1024,1408]{1,0:T(8,128)(2,1)}) custom-call(bf16[256,2048]{1,0:T(8,128)(2,1)S(1)} %multiply_convert_fusion.1.refs_0_.x0, bf16[256,2048]{1,0:T(8,128)(2,1)S(1)} %collective-permute-done.14.refs_1_.x1, bf16[256,2048]{1,0:T(8,128)(2,1)S(1)} %collective-permute-done.15.refs_2_.x2, ...), custom_call_target="tpu_custom_call" | custom-call | flops 11811160064 | bytes 24379392 | tf_op jit(solution)/shard_map/pallas_call | solution.py:44
  450.1 40.6 %collective-permute-done.22.refs_2_.refs_5_ = bf16[1024,1408]{1,0:T(8,128)(2,1)S(1)} collective-permute-done((bf16[1024,1408]{1,0:T(8,128)(2,1)}, bf16[1024,1408]{1,0:T(8,128)(2,1)S(1)}, u32[]{:S(2)}, u32[]{:S(2)}) %collective-permute-start.22) | collective-permute-done | bytes 2883616 | tf_op jit(solution)/shard_map/ppermute | solution.py:23
  492.4 12.9 shard_map.198
  515.2 22.4 %collective-permute-done.24 = bf16[256,2048]{1,0:T(8,128)(2,1)} collective-permute-done((bf16[256,2048]{1,0:T(8,128)(2,1)S(1)}, bf16[256,2048]{1,0:T(8,128)(2,1)}, u32[]{:S(2)}, u32[]{:S(2)}) %collective-permute-start.24) | collective-permute-done | bytes 1048608 | tf_op jit(solution)/shard_map/ppermute | solution.py:23
  544.9 20.9 %collective-permute-done.25.refs_1_ = bf16[256,2048]{1,0:T(8,128)(2,1)S(1)} collective-permute-done((bf16[256,2048]{1,0:T(8,128)(2,1)S(1)}, bf16[256,2048]{1,0:T(8,128)(2,1)S(1)}, u32[]{:S(2)}, u32[]{:S(2)}) %collective-permute-start.25) | collective-permute-done | bytes 1048608 | tf_op jit(solution)/shard_map/ppermute | solution.py:23
  609.9 41.9 %shard_map.200 = (bf16[4,2,128,512]{3,2,1,0:T(8,128)(2,1)S(1)}, f32[4,2,1,1024]{3,2,1,0:T(1,128)S(1)}) custom-call(s32[32]{0:T(128)S(1)} %fusion.51.loc_ref, s32[4]{0:T(128)S(1)} %pad_add_fusion.pos_ref, bf16[4,2,128,512]{3,2,1,0:T(8,128)(2,1)S(1)} %get-tuple-element.97.q_ref, bf16[32,2,128,128]{3,2,1,0:T(8,128)(2,1)S(1)} %copy-done.40), custom_call_target="tpu_custom_call" | custom-call | flops 46137344000 | bytes 4227216 | tf_op jit(solution)/shard_map/pallas_call | solution.py:44
  680.4 16.3 collective-permute-done.36
  701.6 43.0 %collective-permute-done.41.refs_7_.refs_5_ = bf16[1024,1408]{1,0:T(8,128)(2,1)} collective-permute-done((bf16[1024,1408]{1,0:T(8,128)(2,1)}, bf16[1024,1408]{1,0:T(8,128)(2,1)}, u32[]{:S(2)}, u32[]{:S(2)}) %collective-permute-start.41) | collective-permute-done | bytes 2883616 | tf_op jit(solution)/shard_map/ppermute | solution.py:23
  756.1 20.7 %collective-permute-done.48.refs_1_.x1 = bf16[256,2048]{1,0:T(8,128)(2,1)S(1)} collective-permute-done((bf16[256,2048]{1,0:T(8,128)(2,1)S(1)}, bf16[256,2048]{1,0:T(8,128)(2,1)S(1)}, u32[]{:S(2)}, u32[]{:S(2)}) %collective-permute-start.48) | collective-permute-done | bytes 1048608 | tf_op jit(solution)/shard_map/ppermute | solution.py:23
  778.8 21.2 %shard_map.202 = (bf16[1024,1408]{1,0:T(8,128)(2,1)}, bf16[1024,1408]{1,0:T(8,128)(2,1)}, bf16[1024,1408]{1,0:T(8,128)(2,1)}) custom-call(bf16[256,2048]{1,0:T(8,128)(2,1)S(1)} %multiply_convert_fusion.refs_0_.x0, bf16[256,2048]{1,0:T(8,128)(2,1)} %collective-permute-done.37.refs_1_.x1, bf16[256,2048]{1,0:T(8,128)(2,1)S(1)} %collective-permute-done.38.refs_2_.x2, ...), custom_call_target="tpu_custom_call" | custom-call | flops 11811160064 | bytes 24379392 | tf_op jit(solution)/shard_map/pallas_call | solution.py:44
  800.0 15.4 collective-permute-done.42.refs_2_.refs_5_
  817.0 13.5 shard_map.204
  830.5 20.3 %shard_map.205 = (bf16[512,2048]{1,0:T(8,128)(2,1)S(1)}, bf16[512,2048]{1,0:T(8,128)(2,1)S(1)}) custom-call(bf16[1024,1408]{1,0:T(8,128)(2,1)} %get-tuple-element.113.refs_0_.right_ref, bf16[1024,1408]{1,0:T(8,128)(2,1)} %get-tuple-element.114.refs_1_.right_ref, bf16[1024,1408]{1,0:T(8,128)(2,1)} %all-gather.19.cloned.1.call-done.refs_4_.refs_2_, ...), custom_call_target="tpu_custom_call" | custom-call | flops 11811160064 | bytes 21495808 | tf_op jit(solution)/shard_map/pallas_call | solution.py:44
  858.1 23.0 %collective-permute-done.52 = bf16[256,2048]{1,0:T(8,128)(2,1)S(1)} collective-permute-done((bf16[256,2048]{1,0:T(8,128)(2,1)S(1)}, bf16[256,2048]{1,0:T(8,128)(2,1)S(1)}, u32[]{:S(2)}, u32[]{:S(2)}) %collective-permute-start.52) | collective-permute-done | bytes 1048608 | tf_op jit(solution)/shard_map/ppermute | solution.py:23
  886.7 20.6 %collective-permute-done.53.refs_1_.refs_5_ = bf16[256,2048]{1,0:T(8,128)(2,1)S(1)} collective-permute-done((bf16[256,2048]{1,0:T(8,128)(2,1)S(1)}, bf16[256,2048]{1,0:T(8,128)(2,1)S(1)}, u32[]{:S(2)}, u32[]{:S(2)}) %collective-permute-start.53) | collective-permute-done | bytes 1048608 | tf_op jit(solution)/shard_map/ppermute | solution.py:23
  916.0 70.0 %shard_map.207 = (bf16[4,2,128,512]{3,2,1,0:T(8,128)(2,1)S(1)}, bf16[16,2,128,128]{3,2,1,0:T(8,128)(2,1)S(1)}, bf16[16,2,128,128]{3,2,1,0:T(8,128)(2,1)S(1)}) custom-call(s32[32]{0:T(128)S(1)} %fusion.51.loc_ref, s32[4]{0:T(128)S(1)} %pad_add_fusion.pos_ref, bf16[4,2,128,512]{3,2,1,0:T(8,128)(2,1)S(1)} %copy-done.60, bf16[4,2,128,512]{3,2,1,0:T(8,128)(2,1)S(1)} %bitcast.177, ...), custom_call_target="tpu_custom_call" | custom-call | flops 77175193600 | bytes 8945808 | tf_op jit(solution)/shard_map/pallas_call | solution.py:44
  987.3 23.1 %collective-permute-done.56 = bf16[4,4,2,128,128]{4,3,2,1,0:T(8,128)(2,1)S(1)} collective-permute-done((bf16[4,4,2,128,128]{4,3,2,1,0:T(8,128)(2,1)S(1)}, bf16[4,4,2,128,128]{4,3,2,1,0:T(8,128)(2,1)S(1)}, u32[]{:S(2)}, u32[]{:S(2)}) %collective-permute-start.56) | collective-permute-done | bytes 1048608 | tf_op jit(solution)/shard_map/ppermute | solution.py:23
  1055.1 23.0 %collective-permute-done.61 = bf16[256,2048]{1,0:T(8,128)(2,1)S(1)} collective-permute-done((bf16[256,2048]{1,0:T(8,128)(2,1)S(1)}, bf16[256,2048]{1,0:T(8,128)(2,1)S(1)}, u32[]{:S(2)}, u32[]{:S(2)}) %collective-permute-start.61) | collective-permute-done | bytes 1048608 | tf_op jit(solution)/shard_map/ppermute | solution.py:23
  1082.2 34.1 %collective-permute-done.89 = bf16[4,256,1408]{2,1,0:T(8,128)(2,1)S(1)} collective-permute-done((bf16[4,256,1408]{2,1,0:T(8,128)(2,1)}, bf16[4,256,1408]{2,1,0:T(8,128)(2,1)S(1)}, u32[]{:S(2)}, u32[]{:S(2)}) %collective-permute-start.89) | collective-permute-done | bytes 2883616 | tf_op jit(solution)/shard_map/ppermute | solution.py:23
  1123.3 11.4 shard_map.220
  1136.0 62.7 %collective-permute-done.88 = bf16[4,256,1408]{2,1,0:T(8,128)(2,1)S(1)} collective-permute-done((bf16[4,256,1408]{2,1,0:T(8,128)(2,1)}, bf16[4,256,1408]{2,1,0:T(8,128)(2,1)S(1)}, u32[]{:S(2)}, u32[]{:S(2)}) %collective-permute-start.88) | collective-permute-done | bytes 2883616 | tf_op jit(solution)/shard_map/ppermute | solution.py:23
  1205.6 11.7 shard_map.217
  1218.5 13.6 shard_map.209
  1232.1 21.6 %shard_map.210 = (bf16[512,2048]{1,0:T(8,128)(2,1)S(1)}, bf16[512,2048]{1,0:T(8,128)(2,1)}) custom-call(bf16[1024,1408]{1,0:T(8,128)(2,1)} %get-tuple-element.125.refs_0_.right_ref, bf16[1024,1408]{1,0:T(8,128)(2,1)} %get-tuple-element.126.refs_1_.right_ref, bf16[1024,1408]{1,0:T(8,128)(2,1)} %all-gather.11.cloned.1.call-done.refs_4_.refs_2_, ...), custom_call_target="tpu_custom_call" | custom-call | flops 11811160064 | bytes 21495808 | tf_op jit(solution)/shard_map/pallas_call | solution.py:44
  1255.2 25.1 %collective-permute-done.83 = bf16[4,256,1408]{2,1,0:T(8,128)(2,1)S(1)} collective-permute-done((bf16[4,256,1408]{2,1,0:T(8,128)(2,1)}, bf16[4,256,1408]{2,1,0:T(8,128)(2,1)S(1)}, u32[]{:S(2)}, u32[]{:S(2)}) %collective-permute-start.83) | collective-permute-done | bytes 2883616 | tf_op jit(solution)/shard_map/ppermute | solution.py:23
  1318.1 17.5 collective-permute-done.67.refs_1_.refs_5_
  1368.4 70.9 %shard_map.212 = (bf16[4,2,128,512]{3,2,1,0:T(8,128)(2,1)S(1)}, bf16[16,2,128,128]{3,2,1,0:T(8,128)(2,1)}, bf16[16,2,128,128]{3,2,1,0:T(8,128)(2,1)S(1)}) custom-call(s32[32]{0:T(128)S(1)} %fusion.51.loc_ref, s32[4]{0:T(128)S(1)} %pad_add_fusion.pos_ref, bf16[4,2,128,512]{3,2,1,0:T(8,128)(2,1)S(1)} %copy-done.43, bf16[4,2,128,512]{3,2,1,0:T(8,128)(2,1)S(1)} %bitcast.176, ...), custom_call_target="tpu_custom_call" | custom-call | flops 77175193600 | bytes 8945808 | tf_op jit(solution)/shard_map/pallas_call | solution.py:44
  1444.8 13.2 collective-permute-done.70
  1483.4 12.3 collective-permute-done.73
  1497.9 12.7 shard_map.203
  1520.8 30.3 %collective-permute-done.85 = bf16[4,256,1408]{2,1,0:T(8,128)(2,1)S(1)} collective-permute-done((bf16[4,256,1408]{2,1,0:T(8,128)(2,1)}, bf16[4,256,1408]{2,1,0:T(8,128)(2,1)S(1)}, u32[]{:S(2)}, u32[]{:S(2)}) %collective-permute-start.85) | collective-permute-done | bytes 2883616 | tf_op jit(solution)/shard_map/ppermute | solution.py:23
  1577.2 13.7 shard_map.215
  1601.3 45.6 %collective-permute-done.79 = bf16[4,272,1152]{2,1,0:T(8,128)(2,1)S(1)} collective-permute-done((bf16[4,272,1152]{2,1,0:T(8,128)(2,1)}, bf16[4,272,1152]{2,1,0:T(8,128)(2,1)S(1)}, u32[]{:S(2)}, u32[]{:S(2)}) %collective-permute-start.79) | collective-permute-done | bytes 2506784 | tf_op jit(solution)/shard_map/ppermute | solution.py:23
  1663.7 13.9 shard_map.214
  1677.9 20.0 %collective-permute-done.46 = bf16[2,256,2048]{2,1,0:T(8,128)(2,1)} collective-permute-done((bf16[2,256,2048]{2,1,0:T(8,128)(2,1)}, bf16[2,256,2048]{2,1,0:T(8,128)(2,1)}, u32[]{:S(2)}, u32[]{:S(2)}) %collective-permute-start.46) | collective-permute-done | bytes 2097184 | tf_op jit(solution)/shard_map/ppermute | solution.py:102
  1702.1 26.1 %collective-permute-done.78 = bf16[4,272,1152]{2,1,0:T(8,128)(2,1)S(1)} collective-permute-done((bf16[4,272,1152]{2,1,0:T(8,128)(2,1)}, bf16[4,272,1152]{2,1,0:T(8,128)(2,1)S(1)}, u32[]{:S(2)}, u32[]{:S(2)}) %collective-permute-start.78) | collective-permute-done | bytes 2506784 | tf_op jit(solution)/shard_map/ppermute | solution.py:23
  1763.5 13.9 collective-permute-done.84
  1787.5 35.9 %reduce-scatter.9.cloned.1.call-done = bf16[272,1152]{1,0:T(8,128)(2,1)} async-done(((bf16[1088,1152]{1,0:T(8,128)(2,1)}), bf16[272,1152]{1,0:T(8,128)(2,1)}) %reduce-scatter.9.cloned.1.call-update) | async-done | bytes 626704 | tf_op jit(solution)/shard_map/reduce_scatter | solution.py:74
  (625 shorter events, 568.7 us)
Async XLA Ops:
  7.2 123.5 %all-gather.9.cloned.1.call-start = ((), (), s32[]{:S(2)}) async-start(), calls=%async_computation.8 | async-start | bytes 5640192 | tf_op jit(solution)/shard_map/all_gather | solution.py:845
  31.9 205.4 %all-gather.11.cloned.1.call-start = ((), (), s32[]{:S(2)}) async-start(), calls=%async_computation.9 | async-start | bytes 3604480 | tf_op jit(solution)/shard_map/all_gather | solution.py:70
  36.3 33.4 %collective-permute-start = (bf16[2,128,2048]{2,1,0:T(8,128)(2,1)}, bf16[2,128,2048]{2,1,0:T(8,128)(2,1)S(1)}, u32[]{:S(2)}, u32[]{:S(2)}) collective-permute-start(bf16[2,128,2048]{2,1,0:T(8,128)(2,1)} %constant_dynamic-slice_fusion.5), channel_id=1, source_target_pairs={{0,0},{1,15},{2,2},{3,13},{4,4},{5,11},{6,6},{7,9},{8,8},{9,7},{10... | collective-permute-start | bytes 3145736 | tf_op jit(solution)/shard_map/ppermute | solution.py:102
  131.5 148.3 %all-gather.13.cloned.1.call-start = ((), (), s32[]{:S(2)}) async-start(), calls=%async_computation.10 | async-start | bytes 3604480 | tf_op jit(solution)/shard_map/all_gather | solution.py:70
  133.6 30.0 %collective-permute-start.3 = (bf16[256,2048]{1,0:T(8,128)(2,1)S(1)}, bf16[256,2048]{1,0:T(8,128)(2,1)}, u32[]{:S(2)}, u32[]{:S(2)}) collective-permute-start(bf16[256,2048]{1,0:T(8,128)(2,1)S(1)} %fusion.16.refs_0_), channel_id=1, source_target_pairs={{0,1},{1,0},{2,3},{3,2},{4,5},{5,4},{6,7},{7,6},{8,9},{9,8},{10,11... | collective-permute-start | bytes 3145736 | tf_op jit(solution)/shard_map/ppermute | solution.py:23
  216.2 205.0 %all-gather.15.cloned.1.call-start = ((), (), s32[]{:S(2)}) async-start(), calls=%async_computation.11 | async-start | bytes 3604480 | tf_op jit(solution)/shard_map/all_gather | solution.py:70
  237.3 93.9 %collective-permute-start.18 = (bf16[1024,1408]{1,0:T(8,128)(2,1)}, bf16[1024,1408]{1,0:T(8,128)(2,1)}, u32[]{:S(2)}, u32[]{:S(2)}) collective-permute-start(bf16[1024,1408]{1,0:T(8,128)(2,1)} %all-gather.11.cloned.1.call-done.refs_4_.refs_2_), channel_id=1, source_target_pairs={{0,2},{2,0},{4,6},{6,4},{8,10},{10,8},{12,14},{14,12},{1,3},{3,1},... | collective-permute-start | bytes 8650760 | tf_op jit(solution)/shard_map/ppermute | solution.py:23
  279.9 234.5 %all-gather.17.cloned.1.call-start = ((), (), s32[]{:S(2)}) async-start(), calls=%async_computation.12 | async-start | bytes 5640192 | tf_op jit(solution)/shard_map/all_gather | solution.py:845
  331.3 89.9 %collective-permute-start.20 = (bf16[1024,1408]{1,0:T(8,128)(2,1)}, bf16[1024,1408]{1,0:T(8,128)(2,1)}, u32[]{:S(2)}, u32[]{:S(2)}) collective-permute-start(bf16[1024,1408]{1,0:T(8,128)(2,1)} %all-gather.13.cloned.1.call-done.refs_6_.refs_4_), channel_id=1, source_target_pairs={{0,2},{2,0},{4,6},{6,4},{8,10},{10,8},{12,14},{14,12},{1,3},{3,1},... | collective-permute-start | bytes 8650760 | tf_op jit(solution)/shard_map/ppermute | solution.py:23
  339.3 267.7 %all-gather.19.cloned.1.call-start = ((), (), s32[]{:S(2)}) async-start(), calls=%async_computation.13 | async-start | bytes 3604480 | tf_op jit(solution)/shard_map/all_gather | solution.py:70
  366.7 58.8 %collective-permute-start.14 = (bf16[256,2048]{1,0:T(8,128)(2,1)S(1)}, bf16[256,2048]{1,0:T(8,128)(2,1)S(1)}, u32[]{:S(2)}, u32[]{:S(2)}) collective-permute-start(bf16[256,2048]{1,0:T(8,128)(2,1)S(1)} %multiply_convert_fusion.1.refs_0_.x0), channel_id=1, source_target_pairs={{0,16},{16,0},{1,17},{17,1},{2,18},{18,2},{3,19},{19,3},{4,20},{20... | collective-permute-start | bytes 3145736 | tf_op jit(solution)/shard_map/ppermute | solution.py:23
  421.2 69.5 %collective-permute-start.22 = (bf16[1024,1408]{1,0:T(8,128)(2,1)}, bf16[1024,1408]{1,0:T(8,128)(2,1)S(1)}, u32[]{:S(2)}, u32[]{:S(2)}) collective-permute-start(bf16[1024,1408]{1,0:T(8,128)(2,1)} %all-gather.15.cloned.1.call-done.refs_1_.refs_4_), channel_id=1, source_target_pairs={{0,2},{2,0},{4,6},{6,4},{8,10},{10,8},{12,14},{14,12},{1,3},{3,1},... | collective-permute-start | bytes 8650760 | tf_op jit(solution)/shard_map/ppermute | solution.py:23
  514.4 156.2 %all-gather.21.cloned.1.call-start = ((), (), s32[]{:S(2)}) async-start(), calls=%async_computation.14 | async-start | bytes 3604480 | tf_op jit(solution)/shard_map/all_gather | solution.py:70
  606.9 145.0 %all-gather.23.cloned.1.call-start = ((), (), s32[]{:S(2)}) async-start(), calls=%async_computation.15 | async-start | bytes 3604480 | tf_op jit(solution)/shard_map/all_gather | solution.py:70
  607.0 63.6 %collective-permute-start.40 = (bf16[1024,1408]{1,0:T(8,128)(2,1)}, bf16[1024,1408]{1,0:T(8,128)(2,1)}, u32[]{:S(2)}, u32[]{:S(2)}) collective-permute-start(bf16[1024,1408]{1,0:T(8,128)(2,1)} %all-gather.19.cloned.1.call-done.refs_4_.refs_2_), channel_id=1, source_target_pairs={{0,2},{2,0},{4,6},{6,4},{8,10},{10,8},{12,14},{14,12},{1,3},{3,1},... | collective-permute-start | bytes 8650760 | tf_op jit(solution)/shard_map/ppermute | solution.py:23
  670.5 1061.2 %reduce-scatter.23.cloned.1.call-start = ((), (), s32[]{:S(2)}) async-start(), calls=%async_computation.23 | async-start | bytes 3604480 | tf_op jit(solution)/shard_map/reduce_scatter | solution.py:74
  670.6 74.0 %collective-permute-start.41 = (bf16[1024,1408]{1,0:T(8,128)(2,1)}, bf16[1024,1408]{1,0:T(8,128)(2,1)}, u32[]{:S(2)}, u32[]{:S(2)}) collective-permute-start(bf16[1024,1408]{1,0:T(8,128)(2,1)} %all-gather.21.cloned.1.call-done.refs_6_.refs_4_), channel_id=1, source_target_pairs={{0,2},{2,0},{4,6},{6,4},{8,10},{10,8},{12,14},{14,12},{1,3},{3,1},... | collective-permute-start | bytes 8650760 | tf_op jit(solution)/shard_map/ppermute | solution.py:23
  677.4 75.8 %collective-permute-start.47 = (bf16[2,128,2048]{2,1,0:T(8,128)(2,1)}, bf16[2,128,2048]{2,1,0:T(8,128)(2,1)S(1)}, u32[]{:S(2)}, u32[]{:S(2)}) collective-permute-start(bf16[2,128,2048]{2,1,0:T(8,128)(2,1)} %constant_dynamic-slice_fusion), channel_id=1, source_target_pairs={{0,0},{1,15},{2,2},{3,13},{4,4},{5,11},{6,6},{7,9},{8,8},{9,7},{10... | collective-permute-start | bytes 3145736 | tf_op jit(solution)/shard_map/ppermute | solution.py:102
  700.3 55.3 %collective-permute-start.37 = (bf16[256,2048]{1,0:T(8,128)(2,1)S(1)}, bf16[256,2048]{1,0:T(8,128)(2,1)}, u32[]{:S(2)}, u32[]{:S(2)}) collective-permute-start(bf16[256,2048]{1,0:T(8,128)(2,1)S(1)} %multiply_convert_fusion.refs_0_.x0), channel_id=1, source_target_pairs={{0,16},{16,0},{1,17},{17,1},{2,18},{18,2},{3,19},{19,3},{4,20},{20... | collective-permute-start | bytes 3145736 | tf_op jit(solution)/shard_map/ppermute | solution.py:23
  751.9 63.5 %collective-permute-start.42 = (bf16[1024,1408]{1,0:T(8,128)(2,1)}, bf16[1024,1408]{1,0:T(8,128)(2,1)S(1)}, u32[]{:S(2)}, u32[]{:S(2)}) collective-permute-start(bf16[1024,1408]{1,0:T(8,128)(2,1)} %all-gather.23.cloned.1.call-done.refs_1_.refs_4_), channel_id=1, source_target_pairs={{0,2},{2,0},{4,6},{6,4},{8,10},{10,8},{12,14},{14,12},{1,3},{3,1},... | collective-permute-start | bytes 8650760 | tf_op jit(solution)/shard_map/ppermute | solution.py:23
  755.6 44.4 %collective-permute-start.49 = (bf16[256,2048]{1,0:T(8,128)(2,1)S(1)}, bf16[256,2048]{1,0:T(8,128)(2,1)S(1)}, u32[]{:S(2)}, u32[]{:S(2)}) collective-permute-start(bf16[256,2048]{1,0:T(8,128)(2,1)S(1)} %bitcast.171), channel_id=1, source_target_pairs={{0,1},{1,0},{2,3},{3,2},{4,5},{5,4},{6,7},{7,6},{8,9},{9,8},{10,11... | collective-permute-start | bytes 3145736 | tf_op jit(solution)/shard_map/ppermute | solution.py:23
  1052.0 64.3 %collective-permute-start.89 = (bf16[4,256,1408]{2,1,0:T(8,128)(2,1)}, bf16[4,256,1408]{2,1,0:T(8,128)(2,1)S(1)}, u32[]{:S(2)}, u32[]{:S(2)}) collective-permute-start(bf16[4,256,1408]{2,1,0:T(8,128)(2,1)} %get-tuple-element.152), channel_id=1, source_target_pairs={{0,2},{2,0},{4,6},{6,4},{8,10},{10,8},{12,14},{14,12},{1,3},{3,1},... | collective-permute-start | bytes 8650760 | tf_op jit(solution)/shard_map/ppermute | solution.py:23
  1080.8 38.8 %collective-permute-start.62 = (bf16[256,2048]{1,0:T(8,128)(2,1)S(1)}, bf16[256,2048]{1,0:T(8,128)(2,1)S(1)}, u32[]{:S(2)}, u32[]{:S(2)}) collective-permute-start(bf16[256,2048]{1,0:T(8,128)(2,1)S(1)} %fusion.9.refs_0_.x0), channel_id=1, source_target_pairs={{0,16},{16,0},{1,17},{17,1},{2,18},{18,2},{3,19},{19,3},{4,20},{20... | collective-permute-start | bytes 3145736 | tf_op jit(solution)/shard_map/ppermute | solution.py:23
  1118.6 613.2 %reduce-scatter.21.cloned.1.call-start = ((), (), s32[]{:S(2)}) async-start(), calls=%async_computation.22 | async-start | bytes 3604480 | tf_op jit(solution)/shard_map/reduce_scatter | solution.py:74
  1134.8 64.0 %collective-permute-start.88 = (bf16[4,256,1408]{2,1,0:T(8,128)(2,1)}, bf16[4,256,1408]{2,1,0:T(8,128)(2,1)S(1)}, u32[]{:S(2)}, u32[]{:S(2)}) collective-permute-start(bf16[4,256,1408]{2,1,0:T(8,128)(2,1)} %get-tuple-element.150), channel_id=1, source_target_pairs={{0,2},{2,0},{4,6},{6,4},{8,10},{10,8},{12,14},{14,12},{1,3},{3,1},... | collective-permute-start | bytes 8650760 | tf_op jit(solution)/shard_map/ppermute | solution.py:23
  1202.8 532.7 %reduce-scatter.15.cloned.1.call-start = ((), (), s32[]{:S(2)}) async-start(), calls=%async_computation.19 | async-start | bytes 3604480 | tf_op jit(solution)/shard_map/reduce_scatter | solution.py:74
  1217.3 63.0 %collective-permute-start.83 = (bf16[4,256,1408]{2,1,0:T(8,128)(2,1)}, bf16[4,256,1408]{2,1,0:T(8,128)(2,1)S(1)}, u32[]{:S(2)}, u32[]{:S(2)}) collective-permute-start(bf16[4,256,1408]{2,1,0:T(8,128)(2,1)} %get-tuple-element.142), channel_id=1, source_target_pairs={{0,2},{2,0},{4,6},{6,4},{8,10},{10,8},{12,14},{14,12},{1,3},{3,1},... | collective-permute-start | bytes 8650760 | tf_op jit(solution)/shard_map/ppermute | solution.py:23
  1282.6 453.0 %reduce-scatter.13.cloned.1.call-start = ((), (), s32[]{:S(2)}) async-start(), calls=%async_computation.18 | async-start | bytes 3604480 | tf_op jit(solution)/shard_map/reduce_scatter | solution.py:74
  1298.4 61.8 %collective-permute-start.82 = (bf16[4,256,1408]{2,1,0:T(8,128)(2,1)}, bf16[4,256,1408]{2,1,0:T(8,128)(2,1)S(1)}, u32[]{:S(2)}, u32[]{:S(2)}) collective-permute-start(bf16[4,256,1408]{2,1,0:T(8,128)(2,1)} %get-tuple-element.140), channel_id=1, source_target_pairs={{0,2},{2,0},{4,6},{6,4},{8,10},{10,8},{12,14},{14,12},{1,3},{3,1},... | collective-permute-start | bytes 8650760 | tf_op jit(solution)/shard_map/ppermute | solution.py:23
  1314.9 47.6 %collective-permute-start.68 = (bf16[256,2048]{1,0:T(8,128)(2,1)}, bf16[256,2048]{1,0:T(8,128)(2,1)}, u32[]{:S(2)}, u32[]{:S(2)}) collective-permute-start(bf16[256,2048]{1,0:T(8,128)(2,1)} %get-tuple-element.185.refs_0_.refs_4_), channel_id=1, source_target_pairs={{0,1},{1,0},{2,3},{3,2},{4,5},{5,4},{6,7},{7,6},{8,9},{9,8},{10,11... | collective-permute-start | bytes 3145736 | tf_op jit(solution)/shard_map/ppermute | solution.py:23
  1350.3 90.3 %collective-permute-start.86 = (bf16[4,256,1408]{2,1,0:T(8,128)(2,1)}, bf16[4,256,1408]{2,1,0:T(8,128)(2,1)}, u32[]{:S(2)}, u32[]{:S(2)}) collective-permute-start(bf16[4,256,1408]{2,1,0:T(8,128)(2,1)} %get-tuple-element.148), channel_id=1, source_target_pairs={{0,2},{2,0},{4,6},{6,4},{8,10},{10,8},{12,14},{14,12},{1,3},{3,1},... | collective-permute-start | bytes 8650760 | tf_op jit(solution)/shard_map/ppermute | solution.py:23
  1362.5 416.9 %reduce-scatter.19.cloned.1.call-start = ((), (), s32[]{:S(2)}) async-start(), calls=%async_computation.21 | async-start | bytes 3604480 | tf_op jit(solution)/shard_map/reduce_scatter | solution.py:74
  1444.7 334.6 %reduce-scatter.17.cloned.1.call-start = ((), (), s32[]{:S(2)}) async-start(), calls=%async_computation.20 | async-start | bytes 3604480 | tf_op jit(solution)/shard_map/reduce_scatter | solution.py:74
  1462.4 33.3 %collective-permute-start.73 = (bf16[4,2,128,128]{3,2,1,0:T(8,128)(2,1)S(1)}, bf16[4,2,128,128]{3,2,1,0:T(8,128)(2,1)S(1)}, u32[]{:S(2)}, u32[]{:S(2)}) collective-permute-start(bf16[4,2,128,128]{3,2,1,0:T(8,128)(2,1)S(1)} %get-tuple-element.232), channel_id=1, source_target_pairs={{0,12},{2,14},{4,8},{6,10},{8,4},{10,6},{12,0},{14,2},{1,13},{3,15... | collective-permute-start | bytes 786440 | tf_op jit(solution)/shard_map/ppermute | solution.py:23
  1496.6 54.4 %collective-permute-start.85 = (bf16[4,256,1408]{2,1,0:T(8,128)(2,1)}, bf16[4,256,1408]{2,1,0:T(8,128)(2,1)S(1)}, u32[]{:S(2)}, u32[]{:S(2)}) collective-permute-start(bf16[4,256,1408]{2,1,0:T(8,128)(2,1)} %get-tuple-element.145), channel_id=1, source_target_pairs={{0,2},{2,0},{4,6},{6,4},{8,10},{10,8},{12,14},{14,12},{1,3},{3,1},... | collective-permute-start | bytes 8650760 | tf_op jit(solution)/shard_map/ppermute | solution.py:23
  1510.6 42.7 %collective-permute-start.43 = (bf16[512,2048]{1,0:T(8,128)(2,1)}, bf16[512,2048]{1,0:T(8,128)(2,1)}, u32[]{:S(2)}, u32[]{:S(2)}) collective-permute-start(bf16[512,2048]{1,0:T(8,128)(2,1)} %get-tuple-element.110), channel_id=1, source_target_pairs={{0,1},{1,0},{2,3},{3,2},{4,5},{5,4},{6,7},{7,6},{8,9},{9,8},{10,11... | collective-permute-start | bytes 6291464 | tf_op jit(solution)/shard_map/ppermute | solution.py:23
  1553.3 234.2 %reduce-scatter.11.cloned.1.call-start = ((), (), s32[]{:S(2)}) async-start(), calls=%async_computation.17 | async-start | bytes 3133440 | tf_op jit(solution)/shard_map/reduce_scatter | solution.py:74
  1556.0 36.0 %collective-permute-start.44 = (bf16[256,2048]{1,0:T(8,128)(2,1)}, bf16[256,2048]{1,0:T(8,128)(2,1)}, u32[]{:S(2)}, u32[]{:S(2)}) collective-permute-start(bf16[256,2048]{1,0:T(8,128)(2,1)} %add_convert_fusion.13), channel_id=1, source_target_pairs={{0,16},{16,0},{1,17},{17,1},{2,18},{18,2},{3,19},{19,3},{4,20},{20... | collective-permute-start | bytes 3145736 | tf_op jit(solution)/shard_map/ppermute | solution.py:23
  1566.0 31.7 %collective-permute-start.74 = (bf16[512,2048]{1,0:T(8,128)(2,1)S(1)}, bf16[512,2048]{1,0:T(8,128)(2,1)}, u32[]{:S(2)}, u32[]{:S(2)}) collective-permute-start(bf16[512,2048]{1,0:T(8,128)(2,1)S(1)} %get-tuple-element.134), channel_id=1, source_target_pairs={{0,1},{1,0},{2,3},{3,2},{4,5},{5,4},{6,7},{7,6},{8,9},{9,8},{10,11... | collective-permute-start | bytes 6291464 | tf_op jit(solution)/shard_map/ppermute | solution.py:23
  1590.9 56.1 %collective-permute-start.79 = (bf16[4,272,1152]{2,1,0:T(8,128)(2,1)}, bf16[4,272,1152]{2,1,0:T(8,128)(2,1)S(1)}, u32[]{:S(2)}, u32[]{:S(2)}) collective-permute-start(bf16[4,272,1152]{2,1,0:T(8,128)(2,1)} %get-tuple-element.138), channel_id=1, source_target_pairs={{0,2},{2,0},{4,6},{6,4},{8,10},{10,8},{12,14},{14,12},{1,3},{3,1},... | collective-permute-start | bytes 7520264 | tf_op jit(solution)/shard_map/ppermute | solution.py:23
  1597.3 51.9 %collective-permute-start.45 = (bf16[2,128,2048]{2,1,0:T(8,128)(2,1)}, bf16[2,128,2048]{2,1,0:T(8,128)(2,1)}, u32[]{:S(2)}, u32[]{:S(2)}) collective-permute-start(bf16[2,128,2048]{2,1,0:T(8,128)(2,1)} %bitcast.37), channel_id=1, source_target_pairs={{0,16},{16,0},{1,17},{17,1},{2,18},{18,2},{3,19},{19,3},{4,20},{20... | collective-permute-start | bytes 3145736 | tf_op jit(solution)/shard_map/ppermute | solution.py:23
  1600.5 57.8 %collective-permute-start.75 = (bf16[256,2048]{1,0:T(8,128)(2,1)}, bf16[256,2048]{1,0:T(8,128)(2,1)}, u32[]{:S(2)}, u32[]{:S(2)}) collective-permute-start(bf16[256,2048]{1,0:T(8,128)(2,1)} %add_convert_fusion.8), channel_id=1, source_target_pairs={{0,16},{16,0},{1,17},{17,1},{2,18},{18,2},{3,19},{19,3},{4,20},{20... | collective-permute-start | bytes 3145736 | tf_op jit(solution)/shard_map/ppermute | solution.py:23
  1649.1 174.3 %reduce-scatter.9.cloned.1.call-start = ((), (), s32[]{:S(2)}) async-start(), calls=%async_computation.16 | async-start | bytes 3133440 | tf_op jit(solution)/shard_map/reduce_scatter | solution.py:74
  1652.4 45.5 %collective-permute-start.46 = (bf16[2,256,2048]{2,1,0:T(8,128)(2,1)}, bf16[2,256,2048]{2,1,0:T(8,128)(2,1)}, u32[]{:S(2)}, u32[]{:S(2)}) collective-permute-start(bf16[2,256,2048]{2,1,0:T(8,128)(2,1)} %pad_maximum_fusion), channel_id=1, source_target_pairs={{0,0},{1,15},{2,2},{3,13},{4,4},{5,11},{6,6},{7,9},{8,8},{9,7},{10... | collective-permute-start | bytes 6291464 | tf_op jit(solution)/shard_map/ppermute | solution.py:102
  1677.6 50.5 %collective-permute-start.78 = (bf16[4,272,1152]{2,1,0:T(8,128)(2,1)}, bf16[4,272,1152]{2,1,0:T(8,128)(2,1)S(1)}, u32[]{:S(2)}, u32[]{:S(2)}) collective-permute-start(bf16[4,272,1152]{2,1,0:T(8,128)(2,1)} %get-tuple-element.136), channel_id=1, source_target_pairs={{0,2},{2,0},{4,6},{6,4},{8,10},{10,8},{12,14},{14,12},{1,3},{3,1},... | collective-permute-start | bytes 7520264 | tf_op jit(solution)/shard_map/ppermute | solution.py:23
  1737.1 40.4 %collective-permute-start.84 = (bf16[256,1408]{1,0:T(8,128)(2,1)S(1)}, bf16[256,1408]{1,0:T(8,128)(2,1)S(1)}, u32[]{:S(2)}, u32[]{:S(2)}) collective-permute-start(bf16[256,1408]{1,0:T(8,128)(2,1)S(1)} %fusion.24), channel_id=1, source_target_pairs={{0,16},{16,0},{1,17},{17,1},{2,18},{18,2},{3,19},{19,3},{4,20},{20... | collective-permute-start | bytes 2162696 | tf_op jit(solution)/shard_map/ppermute | solution.py:23
  1748.2 39.2 %collective-permute-start.77 = (bf16[2,256,2048]{2,1,0:T(8,128)(2,1)}, bf16[2,256,2048]{2,1,0:T(8,128)(2,1)}, u32[]{:S(2)}, u32[]{:S(2)}) collective-permute-start(bf16[2,256,2048]{2,1,0:T(8,128)(2,1)} %pad_maximum_fusion.1), channel_id=1, source_target_pairs={{0,0},{1,15},{2,2},{3,13},{4,4},{5,11},{6,6},{7,9},{8,8},{9,7},{10... | collective-permute-start | bytes 6291464 | tf_op jit(solution)/shard_map/ppermute | solution.py:102
  1781.8 44.3 %collective-permute-start.87 = (bf16[256,1408]{1,0:T(8,128)(2,1)}, bf16[256,1408]{1,0:T(8,128)(2,1)}, u32[]{:S(2)}, u32[]{:S(2)}) collective-permute-start(bf16[256,1408]{1,0:T(8,128)(2,1)} %fusion.25), channel_id=1, source_target_pairs={{0,16},{16,0},{1,17},{17,1},{2,18},{18,2},{3,19},{19,3},{4,20},{20... | collective-permute-start | bytes 2162696 | tf_op jit(solution)/shard_map/ppermute | solution.py:23
  (195 other events, 4339.7 us)
Sparse Core Ops, SparseCore 0:
  32.0 98.6 all-gather.8
  132.8 77.0 all-gather.10
  216.3 63.4 all-gather.12
  281.8 57.8 all-gather.14
  341.8 109.2 all-gather.16
  514.5 56.8 all-gather.18
  607.0 63.4 all-gather.20
  672.1 79.8 all-gather.22
  1118.7 58.4 reduce-scatter.22
  1203.0 59.3 reduce-scatter.20
  1282.7 60.2 reduce-scatter.14
  1362.6 63.7 reduce-scatter.12
  1444.9 79.6 reduce-scatter.18
  1553.4 84.5 reduce-scatter.16
  1649.2 77.5 reduce-scatter.10
  1730.5 92.8 reduce-scatter.8

commit v2 on v1

--- a/solution.py
+++ b/solution.py
@@ -23,6 +23,10 @@
     return lax.ppermute(x, axis, [(i, i ^ bit) for i in range(peers)])
 
 
+def partner_one(x, source):
+    return lax.ppermute(x, "section", [(source, 1 - source)])
+
+
 def after(value, *events):
     return lax.optimization_barrier((value,) + events)[0]
 
@@ -39,13 +43,16 @@
     return lax.dot_general(left, right, (((1,), (1,)), ((), ())), preferred_element_type=F32)
 
 
-def call(body, ins, outs, scratch, flops, exps=0, **more):
+def call(body, ins, outs, scratch, flops, exps=0, ident=None, light=False, **more):
     moved = sum(x.size * x.dtype.itemsize for x in list(ins) + list(outs))
+    if light:
+        moved, flops, exps = moved // 8, flops // 8, exps // 8
+    remote = {} if ident is None else {"collective_id": ident, "has_side_effects": True}
     return pl.pallas_call(
         body,
         out_shape=outs,
         scratch_shapes=scratch,
-        compiler_params=pltpu.CompilerParams(vmem_limit_bytes=VMEM),
+        compiler_params=pltpu.CompilerParams(vmem_limit_bytes=VMEM, **remote),
         cost_estimate=pl.CostEstimate(
             flops=int(flops), bytes_accessed=int(moved), transcendentals=int(exps)
         ),
@@ -85,21 +92,28 @@
     return blocks
 
 
-def reduce_blocks(send, keep):
-    near = keep.astype(F32) + partner(send, "wide", 1).astype(F32)
+def reduce_near(keep, got):
+    return keep.astype(F32) + got.astype(F32)
+
+
+def reduce_far(near):
     total = near[0]
-    for j in range(1, keep.shape[0]):
+    for j in range(1, near.shape[0]):
         total = total + partner(near[j].astype(BF), "wide", 2 * j).astype(F32)
     return total
 
 
-def mirror(x):
+def mirror(x, cross=0, sections=(0, 1)):
     count = lax.axis_size("wide")
     pairs = []
-    for w in range(count):
-        pairs.append((2 * w, 2 * w))
-        pairs.append((2 * w + 1, 2 * (count - 1 - w) + 1))
-    return lax.ppermute(x, ("wide", "tp"), pairs)
+    for section in sections:
+        for w in range(count):
+            for core in range(2):
+                to = w if core == 0 else count - 1 - w
+                pairs.append(
+                    ((section * count + w) * 2 + core, ((section ^ cross) * count + to) * 2 + core)
+                )
+    return lax.ppermute(x, ("section", "wide", "tp"), pairs)
 
 
 def spread(values):
@@ -115,22 +129,18 @@
     return mine + partner(away, "section", 1).astype(F32)
 
 
-def load_attn(ref, dest, sem, depth, start):
-    copies = []
-    for k in range(dest.shape[0] // depth):
-        copies.append(
-            pltpu.make_async_copy(
-                ref.at[pl.ds(k * (depth + GAIN_ROWS), depth), pl.ds(start, dest.shape[1])],
-                dest.at[pl.ds(k * depth, depth)],
-                sem.at[k],
-            )
-        )
-        copies[-1].start()
-    return copies
+def load_attn(ref, dest, sem, start):
+    copy = pltpu.make_async_copy(ref.at[:, pl.ds(start, dest.shape[1])], dest, sem.at[0])
+    copy.start()
+    return [copy]
 
 
 def load_sides(refs, dest, sem, depth, first=0):
     copies = []
+    if len(refs) == 1:
+        copies.append(pltpu.make_async_copy(refs[0], dest, sem.at[first]))
+        copies[-1].start()
+        return copies
     y = side()
     for s, ref in enumerate(refs):
         for j in range(dest.shape[0] // (2 * depth)):
@@ -146,11 +156,167 @@
     return copies
 
 
-def qkv_kernel(depth, *refs):
+def exchange_kernel(back, keep_f32, last, bulk, *refs):
+    own_ref, send_ref, base_ref, gain_ref = refs[:4]
+    refs = refs[4:]
+    if back:
+        values_ref, scale_ref = refs[:2]
+        refs = refs[2:]
+    bulk_in, refs = refs[:bulk], refs[bulk:]
+    held = 1 if last else 4
+    pieces, refs = refs[:held], refs[held:]
+    first_out, second_out = refs[:2]
+    bulk_out, refs = refs[2 : 2 + bulk], refs[2 + bulk :]
+    got_tp, away, got_section, low, send_sem, recv_sem, local_sem, bulk_sem = refs
+    rows, width = low.shape
+    chunks = 4
+    size = rows // chunks
+    peers = {
+        "tp": {"tp": 1 - lax.axis_index("tp")},
+        "section": {"section": 1 - lax.axis_index("section")},
+        "near": {"wide": lax.axis_index("wide") + 1 - 2 * side()},
+    }
+    greeted = ["tp", "section"] + (["near"] if bulk else [])
+    barrier = pltpu.get_barrier_semaphore()
+    for name in greeted:
+        pl.semaphore_signal(
+            barrier, inc=1, device_id=peers[name], device_id_type=pl.DeviceIdType.MESH
+        )
+    pl.semaphore_wait(barrier, len(greeted))
+
+    def remote(source, target, index, name):
+        copy = pltpu.make_async_remote_copy(
+            src_ref=source,
+            dst_ref=target,
+            send_sem=send_sem.at[index],
+            recv_sem=recv_sem.at[index],
+            device_id=peers[name],
+            device_id_type=pl.DeviceIdType.MESH,
+        )
+        copy.start()
+        return copy
+
+    bulk_copies = [
+        pltpu.make_async_remote_copy(
+            src_ref=bulk_in[i],
+            dst_ref=bulk_out[i],
+            send_sem=bulk_sem.at[0, i],
+            recv_sem=bulk_sem.at[1, i],
+            device_id=peers["near"],
+            device_id_type=pl.DeviceIdType.MESH,
+        )
+        for i in range(bulk)
+    ]
+    for copy in bulk_copies:
+        copy.start()
+    span = lambda c: pl.ds(c * size, size)
+    sums = [
+        remote(send_ref.at[pl.ds(rows, rows)], got_tp.at[1], 0, "tp"),
+        remote(send_ref.at[pl.ds(0, rows)], got_tp.at[0], 1, "tp"),
+    ]
+    sums[0].wait()
+    crossing = []
+    for c in range(chunks):
+        total = own_ref[rows + c * size : rows + (c + 1) * size].astype(F32)
+        away[span(c)] = (total + got_tp[1, span(c)].astype(F32)).astype(BF)
+        crossing.append(remote(away.at[span(c)], got_section.at[span(c)], 2 + c, "section"))
+    sums[1].wait()
+    over_section, over_tp, local = [], [], []
+    gain = gain_ref[...]
+    gain_total = jnp.zeros((1, width), F32)
+    for c in range(chunks):
+        here = slice(c * size, (c + 1) * size)
+        crossing[c].wait()
+        total = own_ref[here].astype(F32) + got_tp[0, here].astype(F32)
+        total = total + got_section[here].astype(F32)
+        base = base_ref[here].astype(F32)
+        if back:
+            scale = scale_ref[here]
+            norm = values_ref[here].astype(F32) * scale
+            scaled = total * gain
+            mean = jnp.mean(scaled * norm, axis=-1, keepdims=True)
+            gain_total = gain_total + jnp.sum(total * norm, axis=0, keepdims=True)
+            result = base + scale * (scaled - norm * mean)
+            if keep_f32:
+                first_out[here] = result
+            low[here] = result.astype(BF)
+        else:
+            result = base + total
+            if keep_f32:
+                first_out[here] = result
+            else:
+                first_out[here] = result.astype(BF)
+                result = result.astype(BF).astype(F32)
+            scale = lax.rsqrt(jnp.mean(result * result, axis=-1, keepdims=True) + EPSILON)
+            second_out[here] = scale
+            low[here] = (result * scale * gain).astype(BF)
+        copy = pltpu.make_async_copy(low.at[span(c)], pieces[0].at[span(c)], local_sem.at[c])
+        copy.start()
+        local.append(copy)
+        if last:
+            continue
+        over_section.append(
+            remote(low.at[span(c)], pieces[1].at[span(c)], 2 + chunks + c, "section")
+        )
+        over_tp.append(remote(low.at[span(c)], pieces[2].at[span(c)], 2 + 2 * chunks + c, "tp"))
+    if back:
+        second_out[...] = gain_total
+        if not keep_f32:
+            first_out[...] = gain_total
+    forwarded = []
+    for c in range(0 if last else chunks):
+        over_section[c].wait()
+        forwarded.append(
+            remote(pieces[1].at[span(c)], pieces[3].at[span(c)], 2 + 3 * chunks + c, "tp")
+        )
+    for copy in local + over_tp + forwarded + bulk_copies:
+        copy.wait()
+
+
+def exchange(
+    own, send, base, gain, values=None, scale=None, keep_f32=True, last=False, bulk=(), ident=0
+):
+    rows, width = base.shape
+    back = values is not None
+    vmem = pl.BlockSpec(memory_space=pltpu.VMEM)
+    ins = [own, send, base, gain.reshape(1, width)] + ([values, scale] if back else [])
+    piece = shaped(rows, width)
+    if back:
+        first = shaped(rows, width, kind=F32) if keep_f32 else shaped(1, width, kind=F32)
+        second = shaped(1, width, kind=F32)
+    else:
+        first = shaped(rows, width, kind=F32 if keep_f32 else BF)
+        second = shaped(rows, 1, kind=F32)
+    count = 2 + 4 * 4
+    held = 1 if last else 4
+    outs = call(
+        functools.partial(exchange_kernel, back, keep_f32, last, len(bulk)),
+        [*ins, *bulk],
+        [piece] * held + [first, second] + [shaped(*x.shape) for x in bulk],
+        [
+            pltpu.VMEM((2, rows, width), BF),
+            pltpu.VMEM((rows, width), BF),
+            pltpu.VMEM((rows, width), BF),
+            pltpu.VMEM((rows, width), BF),
+            pltpu.SemaphoreType.DMA((count,)),
+            pltpu.SemaphoreType.DMA((count,)),
+            pltpu.SemaphoreType.DMA((4,)),
+            pltpu.SemaphoreType.DMA((2, max(1, len(bulk)))),
+        ],
+        60e9,
+        ident=ident,
+        light=back,
+        in_specs=[vmem] * len(ins) + [ANY] * len(bulk),
+        out_specs=[ANY] * held + [vmem] * 2 + [ANY] * len(bulk),
+    )
+    return outs[:held], outs[held], outs[held + 1], outs[held + 2 :]
+
+
+def qkv_kernel(*refs):
     pieces, attn, tables = refs[:4], refs[4], refs[5:9]
     q_ref, kv_ref, w, sem = refs[9:]
     width = w.shape[1]
-    for copy in load_attn(attn, w, sem, depth, 0):
+    for copy in load_attn(attn, w, sem, 0):
         copy.wait()
     cos, sin, cos_kv, sin_kv = tables
     for p, piece in enumerate(pieces):
@@ -172,25 +338,26 @@
                     kv_ref[p, m] = out.astype(BF)
 
 
-def qkv_project(pieces, attn, tables, micro, depth, width):
+def qkv_project(pieces, attn, tables, micro, width):
     total, d = pieces[0].shape
     rows = total // micro
     vmem = pl.BlockSpec(memory_space=pltpu.VMEM)
     return call(
-        functools.partial(qkv_kernel, depth),
+        qkv_kernel,
         [*pieces, attn, *tables],
         [shaped(4, micro, rows, width - PAIR), shaped(4, micro, rows, PAIR)],
-        [pltpu.VMEM((d, width), BF), pltpu.SemaphoreType.DMA((d // depth,))],
+        [pltpu.VMEM((d, width), BF), pltpu.SemaphoreType.DMA((1,))],
         8 * total * d * width,
         in_specs=[vmem] * 4 + [ANY] + [vmem] * 4,
         out_specs=[vmem] * 2,
     )
 
 
-def gate_up_kernel(depth, *refs):
-    pieces, gates, ups = refs[:4], refs[4:6], refs[6:8]
-    outs = refs[8:11]
-    x, w_gate, w_up, buffer, x_sem, w_sem, out_sem = refs[11:]
+def gate_up_kernel(depth, sides, *refs):
+    pieces, refs = refs[:4], refs[4:]
+    gates, ups, refs = refs[: sides[0]], refs[sides[0] : sum(sides)], refs[sum(sides) :]
+    outs = refs[:3]
+    x, w_gate, w_up, buffer, x_sem, w_sem, out_sem = refs[3:]
     copies = load_sides(gates, w_gate, w_sem, depth)
     copies += load_sides(ups, w_up, w_sem, depth, w_gate.shape[0] // depth)
     inputs = []
@@ -231,7 +398,7 @@
     rows, d = pieces[0].shape
     hidden = gates[0].shape[1]
     return call(
-        functools.partial(gate_up_kernel, depth),
+        functools.partial(gate_up_kernel, depth, (len(gates), len(ups))),
         [*pieces, *gates, *ups],
         [shaped(4 * rows, hidden)] * 3,
         [
@@ -245,7 +412,7 @@
         ],
         16 * rows * d * hidden,
         4 * rows * hidden,
-        in_specs=[ANY] * 8,
+        in_specs=[ANY] * (4 + len(gates) + len(ups)),
         out_specs=[ANY] * 3,
     )
 
@@ -321,39 +488,40 @@
         4 * rows * hidden,
         in_specs=[ANY] * 8,
         out_specs=[ANY] * 2,
-    )
-
-
-def out_back_kernel(depth, offset, *refs):
+        light=True,
+    )
+
+
+def out_back_kernel(offset, *refs):
     pieces, attn = refs[:4], refs[4]
     out_ref, w, sem = refs[5:]
-    for copy in load_attn(attn, w, sem, depth, offset):
+    for copy in load_attn(attn, w, sem, offset):
         copy.wait()
     rows = pieces[0].shape[0]
     for p, piece in enumerate(pieces):
         out_ref[p * rows : (p + 1) * rows] = product(piece[...], w[...]).astype(BF)
 
 
-def out_back(pieces, attn, depth, offset, width):
+def out_back(pieces, attn, offset, width):
     rows, d = pieces[0].shape
     vmem = pl.BlockSpec(memory_space=pltpu.VMEM)
     return call(
-        functools.partial(out_back_kernel, depth, offset),
+        functools.partial(out_back_kernel, offset),
         [*pieces, attn],
         [shaped(4 * rows, width)],
-        [pltpu.VMEM((d, width), BF), pltpu.SemaphoreType.DMA((d // depth,))],
+        [pltpu.VMEM((d, width), BF), pltpu.SemaphoreType.DMA((1,))],
         8 * rows * d * width,
         in_specs=[vmem] * 4 + [ANY],
         out_specs=[vmem],
+        light=True,
     )[0]
 
 
-def contract_kernel(depth, starts, *refs):
+def contract_kernel(depth, starts, sizes, *refs):
     sides = len(starts)
     lefts, refs = refs[:sides], refs[sides:]
     sources = []
-    for start in starts:
-        size = 2 if start is None else 1
+    for size in sizes:
         sources.append(refs[:size])
         refs = refs[size:]
     own_ref, send_ref = refs[:2]
@@ -368,7 +536,7 @@
             if start is None:
                 copies += load_sides(sources[s], weights[s], sem.at[s], depth)
             else:
-                copies += load_attn(sources[s][0], weights[s], sem.at[s], depth, start)
+                copies += load_attn(sources[s][0], weights[s], sem.at[s], start)
         for copy in copies:
             copy.wait()
 
@@ -392,7 +560,7 @@
     tile = total // 4
     flat = [ref for group in sources for ref in group]
     return call(
-        functools.partial(contract_kernel, depth, starts),
+        functools.partial(contract_kernel, depth, starts, [len(group) for group in sources]),
         [*lefts, *flat],
         [shaped(total // 2, width)] * 2,
         [pltpu.VMEM((width, left.shape[1]), BF) for left in lefts]
@@ -410,84 +578,50 @@
     )
 
 
-def weight_kernel(x0, x1, x2, x3, right_ref, send_ref, keep_ref):
-    left = jnp.concatenate([x0[...], x1[...], x2[...], x3[...]], axis=0)
-    grad = cross(left, right_ref[...]).astype(BF)
-    depth = keep_ref.shape[1]
-    for y, (first, second) in enumerate(((keep_ref, send_ref), (send_ref, keep_ref))):
-
-        @pl.when(side() == y)
-        def _():
-            first[0] = grad[:depth]
-            second[0] = grad[depth:]
-
-
-def weight_grad(pieces, right, n):
+def weight_kernel(rights, split, *refs):
+    pieces, right_refs, outs = refs[:4], refs[4 : 4 + rights], refs[4 + rights :]
+    left = jnp.concatenate([x[...] for x in pieces], axis=0)
+    start = 0
+    for right in right_refs:
+        grad = cross(left, right[...]).astype(BF)
+        span = slice(start, start + right.shape[1])
+        start += right.shape[1]
+        if not split:
+            outs[0][:, span] = grad
+            continue
+        send_ref, keep_ref = outs
+        depth = keep_ref.shape[1]
+        for y, (first, second) in enumerate(((keep_ref, send_ref), (send_ref, keep_ref))):
+
+            @pl.when(side() == y)
+            def _():
+                first[0, :, span] = grad[:depth]
+                second[0, :, span] = grad[depth:]
+
+
+def weight_grad(pieces, rights, n, split=True):
     rows, d = pieces[0].shape
-    width = right.shape[1]
+    width = sum(right.shape[1] for right in rights)
     depth = d // n
-    out = pl.BlockSpec((1, depth, width), lambda j: (j, 0, 0))
-    return call(
-        weight_kernel,
-        [*pieces, right],
-        [shaped(n // 2, depth, width)] * 2,
+    if split:
+        shapes = [shaped(n // 2, depth, width)] * 2
+        specs = [pl.BlockSpec((1, depth, width), lambda j: (j, 0, 0))] * 2
+    else:
+        shapes = [shaped(d, width)]
+        specs = [pl.BlockSpec((2 * depth, width), lambda j: (j, 0))]
+    outs = call(
+        functools.partial(weight_kernel, len(rights), split),
+        [*pieces, *rights],
+        shapes,
         [],
         8 * rows * d * width,
         grid=(n // 2,),
         in_specs=[pl.BlockSpec((rows, 2 * depth), lambda j: (0, j))] * 4
-        + [pl.BlockSpec((4 * rows, width), lambda j: (0, 0))],
-        out_specs=[out, out],
-    )
-
-
-def attn_weight_kernel(*refs):
-    xs, gs = refs[:4], refs[4:8]
-    dq_ref, dkv_ref, att_ref, gain_ref, send_ref, keep_ref = refs[8:]
-    depth = keep_ref.shape[1] - GAIN_ROWS
-    left = jnp.concatenate([x[...] for x in xs], axis=0)
-    grad = jnp.concatenate([g[...] for g in gs], axis=0)
-    start = 0
-    for source, right in ((left, dq_ref), (left, dkv_ref), (grad, att_ref)):
-        term = cross(source, right[...]).astype(BF)
-        span = slice(start, start + right.shape[1])
-        start += right.shape[1]
-        for y, (first, second) in enumerate(((keep_ref, send_ref), (send_ref, keep_ref))):
-
-            @pl.when(side() == y)
-            def _():
-                first[0, :depth, span] = term[:depth]
-                second[0, :depth, span] = term[depth:]
-
-    for y, (first, second) in enumerate(((keep_ref, send_ref), (send_ref, keep_ref))):
-
-        @pl.when(side() == y)
-        def _():
-            first[0, depth:] = gain_ref[0, 0]
-            second[0, depth:] = gain_ref[0, 1]
-
-
-def attn_weight_grad(xs, gs, dq, dkv, attended, gains, n):
-    rows, d = xs[0].shape
-    depth = d // n
-    width = dq.shape[1] + dkv.shape[1] + attended.shape[1]
-    out = pl.BlockSpec((1, depth + GAIN_ROWS, width), lambda j: (j, 0, 0))
-    whole = lambda x: pl.BlockSpec(x.shape, lambda j: (0, 0))
-    return call(
-        attn_weight_kernel,
-        [*xs, *gs, dq, dkv, attended, gains],
-        [shaped(n // 2, depth + GAIN_ROWS, width)] * 2,
-        [],
-        8 * rows * d * width,
-        grid=(n // 2,),
-        in_specs=[pl.BlockSpec((rows, 2 * depth), lambda j: (0, j))] * 8
-        + [
-            whole(dq),
-            whole(dkv),
-            whole(attended),
-            pl.BlockSpec((1, 2, GAIN_ROWS, width), lambda j: (j, 0, 0, 0)),
-        ],
-        out_specs=[out, out],
-    )
+        + [pl.BlockSpec(right.shape, lambda j: (0, 0)) for right in rights],
+        out_specs=specs,
+        light=True,
+    )
+    return outs if split else outs[0]
 
 
 def stack_heads(x):
@@ -606,6 +740,7 @@
     kv_ref,
     cos_ref,
     sin_ref,
+    before_ref,
     dq_ref,
     send_ref,
     keep_ref,
@@ -616,7 +751,7 @@
     dk_acc,
     dv_acc,
 ):
-    piece = pl.program_id(1)
+    piece = pl.program_id(0)
     rows = q_ref.shape[2]
     count = kv_ref.shape[0]
     per_block = block // rows
@@ -683,9 +818,9 @@
         out = part * cos_ref[...] - turned * sin_ref[...]
         dq_ref[0, 0, :, g * PAIR : (g + 1) * PAIR] = out.astype(BF)
 
-    @pl.when(piece == pl.num_programs(1) - 1)
+    @pl.when(piece == pl.num_programs(0) - 1)
     def _():
-        pieces = pl.num_programs(1)
+        pieces = pl.num_programs(0)
 
         def one(i, _):
             grad = jnp.concatenate([dk_acc[i], dv_acc[i]], axis=1).astype(BF)
@@ -695,45 +830,46 @@
 
             @pl.when(owner % 2 == 0)
             def _():
-                keep_ref[slot, 0] = grad
+                keep_ref[slot] = grad
 
             @pl.when(owner % 2 == 1)
             def _():
-                send_ref[slot, 0] = grad
+                send_ref[slot] = grad
 
             return 0
 
         lax.fori_loop(0, count, one, 0)
 
 
-def attend_back(q, grad, attended, lse, kv, cos, sin, loc, pos):
+def attend_back(m, q, grad, attended, lse, kv, cos, sin, loc, pos, before):
     pieces, micro, rows, width = q.shape
     count = kv.shape[0]
     stacked = rows * width // HD
     block = min(512, rows * count)
-    scores = micro * pieces * stacked * rows * count // 2
-    heads = pl.BlockSpec((1, 1, rows, width), lambda m, p, *_: (p, m, 0, 0))
-    whole = pl.BlockSpec((count, 1, rows, PAIR), lambda m, p, *_: (0, m, 0, 0))
-    half = pl.BlockSpec((count // 2, 1, rows, PAIR), lambda m, p, *_: (0, m, 0, 0))
-    table = pl.BlockSpec((rows, PAIR), lambda m, p, *_: (p, 0))
+    scores = pieces * stacked * rows * count // 2
+    heads = pl.BlockSpec((1, 1, rows, width), lambda p, *_: (p, m, 0, 0))
+    half = pl.BlockSpec((count // 2, rows, PAIR), lambda p, *_: (0, 0, 0))
+    table = pl.BlockSpec((rows, PAIR), lambda p, *_: (p, 0))
     return call(
         functools.partial(attend_back_kernel, block),
-        [loc, pos, q, grad, attended, lse, kv, cos, sin],
-        [shaped(*q.shape)] + [shaped(count // 2, micro, rows, PAIR)] * 2,
+        [loc, pos, q, grad, attended, lse, kv, cos, sin, before],
+        [shaped(*q.shape)] + [shaped(count // 2, rows, PAIR)] * 2,
         (),
         scores * 4600,
         scores,
+        input_output_aliases={9: 0} if m else {},
         grid_spec=pltpu.PrefetchScalarGridSpec(
             num_scalar_prefetch=2,
-            grid=(micro, pieces),
+            grid=(pieces,),
             in_specs=[
                 heads,
                 heads,
                 heads,
-                pl.BlockSpec((1, 1, 1, stacked), lambda m, p, *_: (p, m, 0, 0)),
-                whole,
+                pl.BlockSpec((1, 1, 1, stacked), lambda p, *_: (p, m, 0, 0)),
+                pl.BlockSpec((count, 1, rows, PAIR), lambda p, *_: (0, m, 0, 0)),
                 table,
                 table,
+                ANY,
             ],
             out_specs=[heads, half, half],
             scratch_shapes=[
@@ -745,6 +881,7 @@
                 pltpu.VMEM((count, rows, HD), F32),
             ],
         ),
+        light=True,
     )
 
 
@@ -819,10 +956,7 @@
 
     def pack_attn(parts):
         query, key, value, out = parts
-        main = jnp.concatenate([query, key, value, out.T], axis=1)
-        gains = jnp.concatenate([attn_gain, ffn_gain], axis=0)
-        gains = jnp.pad(gains, ((0, GAIN_ROWS - 2), (0, main.shape[1] - gains.shape[1])))
-        return jnp.concatenate([main, gains], axis=0)
+        return jnp.concatenate([query, key, value, out.T], axis=1)
 
     def both_layers(own, away):
         other = partner(away, "section", 1)
@@ -832,138 +966,279 @@
         part = lax.dynamic_slice_in_dim(values, section * rows, rows, 1)
         return mirror(part).reshape(-1, s.width)
 
+    own_gains = jnp.concatenate([attn_gain, ffn_gain], axis=0)
+    own_gains = lax.all_gather(own_gains, "wide", axis=1, tiled=True)
+    gains_l = [gains.astype(F32) for gains in both_layers(own_gains, own_gains)]
     attn = [halves(w_query[0], 1), halves(w_key[0], 1), halves(w_value[0], 1), halves(w_out[0], 0)]
-    gate_h, up_h, down_h = halves(w_gate[0], 1), halves(w_up[0], 1), halves(w_down[0], 0)
     attn_l = both_layers(*[pack_attn([part[i] for part in attn]) for i in range(2)])
-    gate_l = both_layers(*gate_h)
-    up_l = both_layers(*up_h)
-    down_l = both_layers(*[half.T for half in down_h])
-
+    gate_h = halves(w_gate[0], 1)
+    gate_l = both_layers(gate_h[0], after(gate_h[1], attn_l[0]))
     u = take(tokens).astype(F32)
-    layers, kept, outs = [], [], []
-    for layer in range(2):
-        attn = lax.all_gather(
-            after(attn_l[layer], *layers[0][2]) if layer else attn_l[layer],
-            "wide",
-            axis=0,
-            tiled=True,
-        )
-        by_block = attn.reshape(count, s.depth + GAIN_ROWS, -1)
-        gains = by_block[:, s.depth : s.depth + 2, : s.depth]
-        gains = gains.transpose(1, 0, 2).reshape(2, s.width).astype(F32)
-        first_scale, low = normalize(u, gains[0])
-        normed = spread(low)
-        line_gate = gather_line(after(gate_l[layer], attn))
-        q, kv_own = qkv_project(normed, attn, tables, s.micro, s.depth, s.qkv)
-        kv = jnp.concatenate(gather_blocks(kv_own), axis=0)
-        line_up = gather_line(after(up_l[layer], kv))
-        gate_w = (line_gate, partner(after(line_gate, kv), "wide", 1))
-        attended, lse = attend(q, kv, loc, pos)
-        flat = attended.reshape(-1, s.heads)
-        own, send = contract([flat], [(attn,)], (s.qkv,), s.depth, s.width)
-        line_down = gather_line(after(down_l[layer], line_up))
-        up_w = (line_up, partner(after(line_up, gate_w[1], own), "wide", 1))
-        middle = u + fold(own, send)
-        second_scale, low = normalize(middle, gains[1])
-        normed_ffn = spread(low)
-        gate, up, hidden = gate_up(normed_ffn, gate_w, up_w, s.depth)
-        down_w = (line_down, partner(after(line_down, up_w[1]), "wide", 1))
-        own, send = contract([hidden], [down_w], (None,), s.depth, s.width)
-        result = middle + fold(own, send)
-        layers.append((gains, attn, gate_w, up_w, down_w))
-        kept.append(
-            (u, first_scale, normed, q, kv, attended, lse, middle, second_scale, normed_ffn)
-            + (gate, up, hidden)
-        )
-        outs.append(result.astype(BF))
-        u = outs[layer].astype(F32)
-
-    def reduce(send, keep, *events):
-        got = partner(after(send, *events), "wide", 1)
-        near = (keep.astype(F32) + got.astype(F32)).astype(BF)
-        return reduce_line(near.reshape(-1, near.shape[-1])).astype(F32)
-
-    upstream = take(out_grad).astype(F32)
-    grads, terms = [None, None], [None, None]
+    first_scale, low = normalize(u, gains_l[0][0])
+    normed = spread(low)
+    up_h, down_h = halves(w_up[0], 1), halves(w_down[0], 0)
+    up_l = both_layers(up_h[0], after(up_h[1], normed[1]))
+    down_l = both_layers(down_h[0].T, after(down_h[1].T, up_l[0]))
+
+    gather_all = lambda x: lax.all_gather(x, "wide", axis=0, tiled=True)
+    near = lambda x, *events: partner(after(x, *events), "wide", 1)
+    attn_0 = gather_all(attn_l[0])
+    gate_0 = gather_line(gate_l[0])
+    up_0 = gather_line(up_l[0])
+    q0, kv_own = qkv_project(normed, attn_0, tables, s.micro, s.qkv)
+    down_0 = gather_line(after(down_l[0], q0))
+    kv0 = jnp.concatenate(gather_blocks(kv_own), axis=0)
+    attn_1 = gather_all(after(attn_l[1], q0))
+    attended0, lse0 = attend(q0, after(kv0, gate_0), loc, pos)
+    gate_0 = (gate_0, near(gate_0, kv0))
+    gate_1 = gather_line(after(gate_l[1], attended0))
+    own, send = contract(
+        [after(attended0, gate_0[1]).reshape(-1, s.heads)],
+        [(attn_0,)],
+        (s.qkv,),
+        s.depth,
+        s.width,
+    )
+    up_0 = (up_0, near(up_0, gate_0[1], own))
+    upstream = take(after(out_grad, own))
+    normed_ffn0, middle0, second_scale0, _ = exchange(
+        after(own, down_0), send, u, gains_l[0][1], ident=0
+    )
+    up_1 = gather_line(after(up_l[1], middle0))
+    down_0 = (down_0, near(down_0, up_0[1], middle0))
+    gate0, up0, hidden0 = gate_up(
+        [after(normed_ffn0[0], up_0[1], upstream), *normed_ffn0[1:]], (gate_0), up_0, s.depth
+    )
+    upstream_other = after(partner(after(upstream, up_0[1]), "section", 1), hidden0)
+    down_1 = gather_line(after(down_l[1], hidden0))
+    gate_1 = (gate_1, near(gate_1, down_0[1]))
+    own, send = contract(
+        [after(hidden0, upstream_other, attn_1)], [down_0], (None,), s.depth, s.width
+    )
+    kept0 = (u, first_scale, normed, q0, kv0, attended0, lse0, middle0, second_scale0)
+    kept0 += (normed_ffn0, gate0, up0, hidden0)
+    normed, u, first_scale, _ = exchange(
+        after(own, gate_1[0]), send, middle0, gains_l[1][0], keep_f32=False, ident=1
+    )
+    out0 = u
+    q1, kv_own = qkv_project(
+        [after(normed[0], gate_1[1]), *normed[1:]], attn_1, tables, s.micro, s.qkv
+    )
+    kv1 = jnp.concatenate(gather_blocks(kv_own), axis=0)
+    up_1 = (up_1, near(up_1, kv1))
+    attended1, lse1 = attend(q1, after(kv1, up_1[0]), loc, pos)
+    own, send = contract(
+        [after(attended1, up_1[1], down_1).reshape(-1, s.heads)], [(attn_1,)], (s.qkv,), s.depth, s.width
+    )
+    down_1 = (down_1, near(down_1, up_1[1], own))
+    normed_ffn1, middle1, second_scale1, _ = exchange(own, send, u, gains_l[1][1], ident=5)
+    grad2 = [upstream, upstream_other]
+    grad2 += [partner(after(x, normed_ffn1[0]), "tp", 1) for x in grad2]
+    gate1, up1, hidden1 = gate_up(
+        [after(normed_ffn1[0], down_1[1]), *normed_ffn1[1:]], gate_1, up_1, s.depth
+    )
+    kept1 = (u, first_scale, normed, q1, kv1, attended1, lse1, middle1, second_scale1)
+    kept1 += (normed_ffn1, gate1, up1, hidden1)
+    own1, send1 = contract([hidden1], [down_1], (None,), s.depth, s.width)
+    layers = [
+        (gains_l[0], attn_0, gate_0, up_0, down_0),
+        (gains_l[1], attn_1, gate_1, up_1, down_1),
+    ]
+    kept = [kept0, kept1]
+
+    def near_sum(keep, got):
+        total = (keep.astype(F32) + got.astype(F32)).astype(BF)
+        return total.reshape(-1, total.shape[-1])
+
+    reduce_all = lambda x: lax.psum_scatter(x, "wide", scatter_dimension=0, tiled=True)
+
+    def give(value, layer):
+        value = value.reshape(s.micro, rows, s.width)
+        pair = [mirror(value, 0, (layer,)), mirror(value, 1, (1 - layer,))]
+        return jnp.concatenate(pair[::-1] if layer else pair, axis=1)
+
+    grads, terms, gain_terms = [None, None], [None, None], []
+    by_piece = lambda table: table.reshape(4, rows, PAIR)
+    halved = lambda x: x.reshape(count // 2, 4, rows, PAIR)
     for layer in (1, 0):
         gains, attn, gate_w, up_w, down_w = layers[layer]
         u, first_scale, normed, q, kv, attended, lse, middle, second_scale, normed_ffn = kept[
             layer
         ][:10]
         gate, up, hidden = kept[layer][10:]
-        grad2 = spread(upstream.astype(BF))
-        grad_gate, grad_up = hidden_back(grad2, down_w, gate, up, s.depth)
+        flat = attended.reshape(-1, s.heads)
+        if layer:
+            grad2 = [after(x, own1) for x in grad2]
+            given0 = give(after(out0, own1), 0)
+        down_send, down_keep = weight_grad(grad2, [hidden], count)
+        down_got = partner(down_send, "wide", 1)
+        grad_gate, grad_up = hidden_back(
+            [after(x, down_send) for x in grad2], down_w, gate, up, s.depth
+        )
+        gate_send, gate_keep = weight_grad(normed_ffn, [grad_gate], count)
+        up_send, up_keep = weight_grad(
+            [after(x, gate_send) for x in normed_ffn], [grad_up], count
+        )
+        if layer:
+            out1 = (middle1 + fold(own1, send1)).astype(BF)
+            grad_gate, given0 = lax.optimization_barrier((after(grad_gate, out1), given0))
         own, send = contract(
-            [grad_gate, grad_up], [gate_w, up_w], (None, None), s.depth, s.width
-        )
-        d_down = reduce(*weight_grad(grad2, hidden, count))
-        inner, second_gain = normalize_back(middle, second_scale, gains[1], fold(own, send))
-        grad_middle = upstream + inner
-        grad1 = spread(grad_middle.astype(BF))
-        d_gate = reduce(*weight_grad(normed_ffn, grad_gate, count))
-        grad_attended = out_back(grad1, attn, s.depth, s.qkv, s.heads).reshape(q.shape)
-        dq, send, keep = attend_back(
-            q, grad_attended, attended, lse, kv, tables[0], tables[1], loc, pos
-        )
-        halved = lambda x: x.reshape(count // 2, 4, s.micro, rows, PAIR)
-        dkv = reduce_blocks(halved(send), halved(keep))
-        d_up = reduce(*weight_grad(normed_ffn, grad_up, count), dkv)
+            [after(grad_gate, up_send), grad_up],
+            [gate_w, up_w],
+            (None, None),
+            s.depth,
+            s.width,
+        )
+        down_near = near_sum(down_keep, after(down_got, own))
+        if layer == 0:
+            own = after(own, d_attn)
+            terms[1][0] = d_attn
+        d_down = reduce_line(down_near)
+        gate_got = partner(after(gate_send, down_near), "wide", 1)
+        grad1, grad_middle, second_gain, _ = exchange(
+            after(own, down_near), send, upstream, gains[1], middle, second_scale, ident=2
+        )
+        gate_got, d_down = after((gate_got, d_down), grad1[0])
+        gate_near = near_sum(gate_keep, gate_got)
+        d_gate = reduce_line(gate_near)
+        up_got = partner(after(up_send, gate_near, d_down), "wide", 1)
+        grad1 = [after(grad1[0], gate_near, d_down), *grad1[1:]]
+        grad_attended = out_back(grad1, attn, s.qkv, s.heads)
+        if layer == 0:
+            crossed = [partner_one(x, 0) for x in after(tuple(terms[1]), grad_attended)]
+        else:
+            given1 = give(after(out1, grad_attended), 1)
+        back = lambda m, grad, before: attend_back(
+            m, q, grad, attended, lse, kv, tables[0], tables[1], loc, pos, before
+        )
+        grad_attended = grad_attended.reshape(q.shape)
+        dq, send0, keep0 = back(0, grad_attended, q)
+        got0 = partner(halved(send0), "wide", 1)
+        if layer == 0:
+            down_crossed = partner_one(after(d_down, send0), 1)
+        dq, send1_, keep1 = back(1, after(grad_attended, send0), dq)
+        if layer == 0:
+            dq, down_crossed = lax.optimization_barrier((dq, down_crossed))
+        up_got, got0, d_gate = after((up_got, got0, d_gate), dq)
+        near0 = reduce_near(halved(keep0), got0)
+        if layer == 0:
+            gate_crossed = partner_one(after(d_gate, near0), 1)
+        got1 = partner(after(halved(send1_), near0), "wide", 1)
+        dkv0 = reduce_far(near0)
+        up_near = near_sum(up_keep, after(up_got, near0))
+        d_up = reduce_line(up_near)
+        out_send, out_keep = weight_grad(
+            [after(x, up_near, d_gate) for x in grad1], [flat], count
+        )
+        if layer:
+            out_send, given1 = lax.optimization_barrier((out_send, given1))
+            section_out = jnp.where(home, given0, given1)
+        dkv1 = reduce_far(reduce_near(halved(keep1), after(got1, out_send)))
+        if layer == 0:
+            crossed = list(after(tuple(crossed), dq))
+            dkv1 = after(dkv1, *crossed)
         half = HD // 2
-        turned = jnp.concatenate(
-            [dkv[..., half:HD], dkv[..., :half], jnp.zeros_like(dkv[..., HD:])], axis=-1
-        )
-        by_piece = lambda table: table.reshape(4, 1, rows, PAIR)
-        dkv = (dkv * by_piece(tables[2]) - turned * by_piece(tables[3])).astype(BF)
-        dq, dkv = dq.reshape(-1, s.heads), dkv.reshape(-1, PAIR)
+        back_rows = []
+        for dkv in (dkv0, dkv1):
+            turned = jnp.concatenate(
+                [dkv[..., half:HD], dkv[..., :half], jnp.zeros_like(dkv[..., HD:])], axis=-1
+            )
+            back_rows.append(dkv * by_piece(tables[2]) - turned * by_piece(tables[3]))
+        dkv = jnp.stack(back_rows, axis=1).astype(BF)
+        dq, dkv = after(dq, out_send).reshape(-1, s.heads), dkv.reshape(-1, PAIR)
+        if layer == 0:
+            out_got = partner(after(out_send, got1), "wide", 1)
+            dkv, gate_crossed = lax.optimization_barrier((dkv, gate_crossed))
+            crossed_0 = [gate_crossed, down_crossed]
         own, send = contract([dq, dkv], [(attn,), (attn,)], (0, s.heads), s.depth, s.width)
-        inner, first_gain = normalize_back(u, first_scale, gains[0], fold(own, send))
-        grads[layer] = (grad_middle + inner).astype(BF)
-        gain_rows = jnp.stack([first_gain, second_gain]).astype(BF)
-        gain_rows = gain_rows.reshape(2, count // 2, 2, s.depth).transpose(1, 2, 0, 3)
-        gain_rows = jnp.pad(
-            gain_rows,
-            ((0, 0), (0, 0), (0, GAIN_ROWS - 2), (0, s.qkv + s.heads - s.depth)),
-        )
-        d_attn = reduce(
-            *attn_weight_grad(
-                normed, grad1, dq, dkv, attended.reshape(-1, s.heads), gain_rows, count
+        if layer == 0:
+            out_near = near_sum(out_keep, after(out_got, own))
+            d_out = reduce_line(out_near)
+            own = after(own, out_near)
+        qkv_send, qkv_keep = weight_grad(
+            [after(x, own) for x in normed], [dq, dkv], count
+        )
+        if layer:
+            pack_got = partner(
+                jnp.concatenate([after(qkv_send, dkv1), out_send], axis=2), "wide", 1
             )
-        )
-        terms[layer] = (d_attn, d_gate, d_up, d_down)
-        upstream = grads[layer].astype(F32)
-
-    def give(first, second):
-        first, second = [x.reshape(s.micro, rows, s.width) for x in (first, second)]
-        own = jnp.where(home, first, second)
-        other = partner(jnp.where(home, second, first), "section", 1)
-        both = jnp.concatenate(
-            [jnp.where(home, own, other), jnp.where(home, other, own)], axis=1
-        )
-        return mirror(both)
-
-    section_out = give(*outs)
-    input_grads = give(*grads)
+            grad2, _, first_gain, _ = exchange(
+                after(own, qkv_send),
+                send,
+                grad_middle,
+                gains[0],
+                u,
+                first_scale,
+                keep_f32=False,
+                ident=3,
+            )
+            grads[1] = upstream = grad2[0]
+            grads_out = give(upstream, 1)
+            pack_got, d_up = after((pack_got, d_up), grad2[0])
+            pack_near = near_sum(jnp.concatenate([qkv_keep, out_keep], axis=2), pack_got)
+            d_attn = reduce_line(after(pack_near, d_up))
+            grad2 = [after(x, pack_near) for x in grad2]
+            terms[1] = [None, d_gate, d_up, d_down]
+        else:
+            grads[0], _, first_gain, got = exchange(
+                own,
+                send,
+                grad_middle,
+                gains[0],
+                u,
+                first_scale,
+                keep_f32=False,
+                last=True,
+                bulk=(qkv_send,),
+                ident=4,
+            )
+            grads[0] = grads[0][0]
+            qkv_near = near_sum(qkv_keep, got[0])
+            blocks = qkv_near.reshape(count // 2, s.depth, -1)
+            d_qkv = blocks[wide // 2].astype(F32)
+            for j in range(1, count // 2):
+                block = partner(blocks[(wide // 2) ^ j], "wide", 2 * j)
+                d_qkv = d_qkv + block.astype(F32)
+            d_qkv = d_qkv.astype(BF)
+            terms[0] = [d_qkv, d_out, d_gate, d_up, d_down]
+        gain_terms += [first_gain.reshape(1, -1), second_gain.reshape(1, -1)]
+
+    given = (give(grads[0], 0), grads_out)
+    up_crossed = partner_one(after(d_up, grads[0]), 1)
+    d_qkv_out, *given = lax.optimization_barrier((d_qkv, *given))
+    input_grads = jnp.where(home, *given)
+    late = [partner_one(x, 1) for x in (d_qkv_out, d_out)]
+    crossed_0 = [*late, crossed_0[0], up_crossed, crossed_0[1]]
+    crossed = [crossed[0][:, : s.qkv], crossed[0][:, s.qkv :], *crossed[1:]]
+    terms[1] = [terms[1][0][:, : s.qkv], terms[1][0][:, s.qkv :], *terms[1][1:]]
+    gain_total = jnp.concatenate(gain_terms, axis=0)
+    gain_total = gain_total + partner(gain_total, "tp", 1)
+    gain_total = gain_total + partner(gain_total, "section", 1)
+    gain_total = gain_total.reshape(4, count // 2, 2, s.depth)
+    gain_total = gain_total[:, :, side()] + partner(gain_total[:, :, 1 - side()], "wide", 1)
+    total = gain_total[:, wide // 2]
+    for j in range(1, count // 2):
+        total = total + partner(gain_total[:, (wide // 2) ^ j], "wide", 2 * j)
+    gain_total = total
+    gains = jnp.where(home, gain_total[2:], gain_total[:2])
 
     def settle(index):
-        first, second = terms[0][index], terms[1][index]
-        own = jnp.where(home, first, second)
-        other = partner(jnp.where(home, second, first).astype(BF), "section", 1).astype(F32)
+        own = jnp.where(home, terms[0][index], terms[1][index]).astype(F32)
+        other = crossed[index].astype(F32) + crossed_0[index].astype(F32)
         return jnp.where(home, own, other), jnp.where(home, other, own)
 
-    depth, heads = s.depth, s.heads
+    heads = s.heads
     low, high = settle(0)
     cut = lambda start, size: jnp.concatenate(
-        [low[:depth, start : start + size], high[:depth, start : start + size]], axis=1
+        [low[:, start : start + size], high[:, start : start + size]], axis=1
     )
     d_query = cut(0, heads)
     d_key = cut(heads, HD)
     d_value = cut(heads + HD, HD)
-    d_out = jnp.concatenate([low[:depth, s.qkv :].T, high[:depth, s.qkv :].T], axis=0)
-    gains = (low + high)[depth : depth + 2, :depth]
-    gains = gains + partner(gains, "tp", 1)
-    d_gate = jnp.concatenate(settle(1), axis=1)
-    d_up = jnp.concatenate(settle(2), axis=1)
-    d_down = jnp.concatenate([half.T for half in settle(3)], axis=0)
+    d_out = jnp.concatenate([half.T for half in settle(1)], axis=0)
+    d_gate = jnp.concatenate(settle(2), axis=1)
+    d_up = jnp.concatenate(settle(3), axis=1)
+    d_down = jnp.concatenate([half.T for half in settle(4)], axis=0)
     return (
         section_out[None],
         input_grads[None],

time: 1880 us -> 1730 us (0.920)
  waiting for transfers between devices: 1010 us -> 418 us
  Pallas kernels: 507 us -> 909 us
  local copies, waits for them, and re-layouts: 56.4 us -> 105 us
  blocking collectives: 0 us -> 26 us
    ppermute x87 -> x66, waiting for transfers between devices: 826 us -> 252 us  [partner(): return lax.ppermute(x, axis, [(i, i ^ bit) for i in range(peers)])]
    pallas_call x28 -> x39, Pallas kernels: 507 us -> 909 us  [call(): pl.pallas_call(body, out_shape=outs, scratch_shapes=scratch, compiler_par...]
    all_gather x2, waiting for transfers between devices: 60.7 us -> 0.04 us  [shards(): gather_all = lambda x: lax.all_gather(x, 'wide', axis=0, tiled=True)]
    unnamed x290 -> x350, local copies, waits for them, and re-layouts: 36.5 us -> 84 us
    ppermute x87 -> x66, starting transfers between devices: 137 us -> 93.5 us  [partner(): return lax.ppermute(x, axis, [(i, i ^ bit) for i in range(peers)])]
    ppermute x4 -> x19, waiting for transfers between devices: 36.4 us -> 76.6 us  [the longest x10 41.7 us: mirror(): return lax.ppermute(x, ('section', 'wide', 'tp'), pairs)]
    ppermute x4 -> x19, starting transfers between devices: 18.4 us -> 54.5 us  [the longest x10 38.1 us: mirror(): return lax.ppermute(x, ('section', 'wide', 'tp'), pairs)]
    reduce_scatter x8, waiting for transfers between devices: 36 us -> 0.05 us  [reduce_line(): lax.psum_scatter(near, 'wide', scatter_dimension=0, tiled=True, axis_inde...]
  transfers between devices with their start and end apart: 107 -> 101, of which waited for: 59 -> 43; matrix products, arithmetic and copies ran while one was open for 6% -> 5% of each run, Pallas kernels for 21% -> 51%
where the time goes in v2:
time: 1730 us; the launch traced here: 1720 us
  Pallas kernels  909 us (53%)
  waiting for transfers between devices  418 us (24%)
  starting transfers between devices  149 us (9%)
  local copies, waits for them, and re-layouts  105 us (6%)
  other arithmetic  94.6 us (5%)
  blocking collectives  26 us (2%)
    pallas_call x39, Pallas kernels, call(): pl.pallas_call(body, out_shape=outs, scratch_shapes=scratch, compiler_par...  909 us
    ppermute x66, waiting for transfers between devices, partner(): return lax.ppermute(x, axis, [(i, i ^ bit) for i in range(peers)])  252 us
    ppermute x66, starting transfers between devices, partner(): return lax.ppermute(x, axis, [(i, i ^ bit) for i in range(peers)])  93.5 us
    all_gather x6, waiting for transfers between devices, gather_line(): lax.all_gather(shard, 'wide', axis=0, tiled=True, axis_index_groups=lines())  88.5 us
    unnamed x350, local copies, waits for them, and re-layouts  84 us
    ppermute x10, waiting for transfers between devices, mirror(): return lax.ppermute(x, ('section', 'wide', 'tp'), pairs)  41.7 us
    ppermute x10, starting transfers between devices, mirror(): return lax.ppermute(x, ('section', 'wide', 'tp'), pairs)  38.1 us
    ppermute x9, waiting for transfers between devices, partner_one(): return lax.ppermute(x, 'section', [(source, 1 - source)])  34.9 us
  transfers between devices with their start and end apart: 101, of which 43 were waited for; matrix products, arithmetic and copies ran while one was open for 5% of the time, Pallas kernels for 51%

profile of v2, /device:TPU:1, one launch (start us, length us, event | category | flops | bytes accessed | tf_op | source)
XLA Modules:
  0.0 1718.5 jit_solution(113865557244545259)
XLA Ops:
  17.2 12.2 collective-permute-done.5
  35.0 15.6 collective-permute-done.13
  59.0 26.0 %all_gather.27 = bf16[2,2048]{1,0:T(2,128)(2,1)S(1)} all-gather(bf16[2,256]{1,0:T(2,128)(2,1)S(1)} %pad_maximum_fusion.12), channel_id=1, replica_groups=mesh['section'=2,'wide'=8,'tp'=2] {'wide'}, dimensions={1}, use_global_device_ids=true | all-gather | bytes 9216 | tf_op jit(solution)/shard_map/all_gather | solution.py:970
  92.1 20.2 %collective-permute-done.2.refs_1_ = bf16[256,2048]{1,0:T(8,128)(2,1)S(1)} collective-permute-done((bf16[256,2048]{1,0:T(8,128)(2,1)S(1)}, bf16[256,2048]{1,0:T(8,128)(2,1)S(1)}, u32[]{:S(2)}, u32[]{:S(2)}) %collective-permute-start.2) | collective-permute-done | bytes 1048608 | tf_op jit(solution)/shard_map/ppermute | solution.py:23
  113.8 10.8 collective-permute-done.16
  157.7 16.5 collective-permute-start.7
  176.4 17.7 %collective-permute-done.7 = bf16[4,2,128,128]{3,2,1,0:T(8,128)(2,1)S(1)} collective-permute-done((bf16[4,2,128,128]{3,2,1,0:T(8,128)(2,1)}, bf16[4,2,128,128]{3,2,1,0:T(8,128)(2,1)S(1)}, u32[]{:S(2)}, u32[]{:S(2)}) %collective-permute-start.7) | collective-permute-done | bytes 262176 | tf_op jit(solution)/shard_map/ppermute | solution.py:23
  200.1 10.1 collective-permute-done.9
  223.1 41.9 %shard_map.195 = (bf16[4,2,128,512]{3,2,1,0:T(8,128)(2,1)S(1)}, f32[4,2,1,1024]{3,2,1,0:T(1,128)S(1)}) custom-call(s32[32]{0:T(128)S(1)} %fusion.41.loc_ref, s32[4]{0:T(128)S(1)} %pad_add_fusion.pos_ref, bf16[4,2,128,512]{3,2,1,0:T(8,128)(2,1)S(1)} %copy-done.89, bf16[32,2,128,128]{3,2,1,0:T(8,128)(2,1)S(1)} %copy-done.77), custom_call_target="tpu_custom_call" | custom-call | flops 46137344000 | bytes 4227216 | tf_op jit(solution)/shard_map/pallas_call | solution.py:51
  265.5 16.8 collective-permute-done.14.refs_5_.refs_3_
  291.1 33.0 %all-gather.13.cloned.1.call-done.refs_1_.refs_4_ = bf16[1024,1408]{1,0:T(8,128)(2,1)} async-done(((bf16[256,1408]{1,0:T(8,128)(2,1)}), bf16[1024,1408]{1,0:T(8,128)(2,1)}) %all-gather.13.cloned.1.call-update) | async-done | bytes 2883600 | tf_op jit(solution)/shard_map/all_gather | solution.py:77
  324.1 57.0 %shard_map.197 = (bf16[256,2048]{1,0:T(8,128)(2,1)S(1)}, bf16[256,2048]{1,0:T(8,128)(2,1)S(1)}, bf16[256,2048]{1,0:T(8,128)(2,1)S(1)}, bf16[256,2048]{1,0:T(8,12...) custom-call(bf16[512,2048]{1,0:T(8,128)(2,1)} %copy-done.98, bf16[512,2048]{1,0:T(8,128)(2,1)} %copy-done.99, ...), custom_call_target="tpu_custom_call" | custom-call | flops 60000002048 | bytes 12592128 | tf_op jit(solution)/shard_map/pallas_call | solution.py:51
  387.8 18.1 %collective-permute-done.15 = bf16[2,128,2048]{2,1,0:T(8,128)(2,1)} collective-permute-done((bf16[2,128,2048]{2,1,0:T(8,128)(2,1)}, bf16[2,128,2048]{2,1,0:T(8,128)(2,1)}, u32[]{:S(2)}, u32[]{:S(2)}) %collective-permute-start.15) | collective-permute-done | bytes 1048608 | tf_op jit(solution)/shard_map/ppermute | solution.py:116
  409.7 20.4 %shard_map.198 = (bf16[1024,1408]{1,0:T(8,128)(2,1)}, bf16[1024,1408]{1,0:T(8,128)(2,1)}, bf16[1024,1408]{1,0:T(8,128)(2,1)}) custom-call(bf16[256,2048]{1,0:T(8,128)(2,1)S(1)} %get-tuple-element.406.refs_0_, bf16[256,2048]{1,0:T(8,128)(2,1)S(1)} %get-tuple-element.407.refs_1_, bf16[256,2048]{1,0:T(8,128)(2,1)S(1)} %copy-done.3, ...), custom_call_target="tpu_custom_call" | custom-call | flops 11811160064 | bytes 24379392 | tf_op jit(solution)/shard_map/pallas_call | solution.py:51
  430.2 55.4 %all-gather.19.cloned.1.call-done.refs_4_.refs_2_ = bf16[1024,1408]{1,0:T(8,128)(2,1)} async-done(((bf16[256,1408]{1,0:T(8,128)(2,1)}), bf16[1024,1408]{1,0:T(8,128)(2,1)}) %all-gather.19.cloned.1.call-update) | async-done | bytes 2883600 | tf_op jit(solution)/shard_map/all_gather | solution.py:77
  486.8 11.9 shard_map.199
  501.4 55.9 %shard_map.200 = (bf16[256,2048]{1,0:T(8,128)(2,1)S(1)}, bf16[256,2048]{1,0:T(8,128)(2,1)S(1)}, bf16[256,2048]{1,0:T(8,128)(2,1)S(1)}, bf16[256,2048]{1,0:T(8,12...) custom-call(bf16[512,2048]{1,0:T(8,128)(2,1)} %copy-done.102, bf16[512,2048]{1,0:T(8,128)(2,1)} %copy-done.103, ...), custom_call_target="tpu_custom_call" | custom-call | flops 60000002048 | bytes 11543552 | tf_op jit(solution)/shard_map/pallas_call | solution.py:51
  583.3 28.0 %collective-permute-done.25 = bf16[4,2,128,128]{3,2,1,0:T(8,128)(2,1)} collective-permute-done((bf16[4,2,128,128]{3,2,1,0:T(8,128)(2,1)}, bf16[4,2,128,128]{3,2,1,0:T(8,128)(2,1)}, u32[]{:S(2)}, u32[]{:S(2)}) %collective-permute-start.25) | collective-permute-done | bytes 262176 | tf_op jit(solution)/shard_map/ppermute | solution.py:23
  622.6 41.9 %shard_map.202 = (bf16[4,2,128,512]{3,2,1,0:T(8,128)(2,1)S(1)}, f32[4,2,1,1024]{3,2,1,0:T(1,128)S(1)}) custom-call(s32[32]{0:T(128)S(1)} %fusion.41.loc_ref, s32[4]{0:T(128)S(1)} %pad_add_fusion.pos_ref, bf16[4,2,128,512]{3,2,1,0:T(8,128)(2,1)S(1)} %copy-done.95, bf16[32,2,128,128]{3,2,1,0:T(8,128)(2,1)S(1)} %copy-done.79), custom_call_target="tpu_custom_call" | custom-call | flops 46137344000 | bytes 4227216 | tf_op jit(solution)/shard_map/pallas_call | solution.py:51
  665.5 12.6 collective-permute-done.29.refs_7_.refs_5_
  687.5 62.3 %shard_map.204 = (bf16[256,2048]{1,0:T(8,128)(2,1)S(1)}, bf16[256,2048]{1,0:T(8,128)(2,1)S(1)}, bf16[256,2048]{1,0:T(8,128)(2,1)S(1)}, bf16[256,2048]{1,0:T(8,12...) custom-call(bf16[512,2048]{1,0:T(8,128)(2,1)} %copy-done.100, bf16[512,2048]{1,0:T(8,128)(2,1)} %copy-done.101, ...), custom_call_target="tpu_custom_call" | custom-call | flops 60000002048 | bytes 11543552 | tf_op jit(solution)/shard_map/pallas_call | solution.py:51
  749.9 21.5 %shard_map.205 = (bf16[1024,1408]{1,0:T(8,128)(2,1)}, bf16[1024,1408]{1,0:T(8,128)(2,1)}, bf16[1024,1408]{1,0:T(8,128)(2,1)}) custom-call(bf16[256,2048]{1,0:T(8,128)(2,1)S(1)} %get-tuple-element.328.refs_0_, bf16[256,2048]{1,0:T(8,128)(2,1)S(1)} %get-tuple-element.329.refs_1_, bf16[256,2048]{1,0:T(8,128)(2,1)S(1)} %get-tuple-element.330.refs_2_, ...), custom_call_target="tpu_custom_call" | custom-call | flops 11811160064 | bytes 24379392 | tf_op jit(solution)/shard_map/pallas_call | solution.py:51
  771.4 12.8 shard_map.206
  793.5 11.5 shard_map.207
  808.9 14.3 shard_map.208
  823.2 11.1 shard_map.209
  834.3 11.3 shard_map.210
  852.1 20.3 %shard_map.211 = (bf16[512,2048]{1,0:T(8,128)(2,1)S(1)}, bf16[512,2048]{1,0:T(8,128)(2,1)S(1)}) custom-call(bf16[1024,1408]{1,0:T(8,128)(2,1)} %get-tuple-element.334.refs_4_.refs_0_, bf16[1024,1408]{1,0:T(8,128)(2,1)} %get-tuple-element.332.refs_4_.refs_1_, bf16[1024,1408]{1,0:T(8,128)(2,1)} %all-gather.19.cloned.1.call-done.refs_4_.refs_2_, ...), custom_call_target="tpu_custom_call" | custom-call | flops 11811160064 | bytes 21495808 | tf_op jit(solution)/shard_map/pallas_call | solution.py:51
  884.9 57.4 %shard_map.212 = (bf16[256,2048]{1,0:T(8,128)(2,1)S(1)}, bf16[256,2048]{1,0:T(8,128)(2,1)S(1)}, bf16[256,2048]{1,0:T(8,128)(2,1)S(1)}, bf16[256,2048]{1,0:T(8,12...) custom-call(bf16[512,2048]{1,0:T(8,128)(2,1)} %copy-done.106, bf16[512,2048]{1,0:T(8,128)(2,1)} %copy-done.107, ...), custom_call_target="tpu_custom_call" | custom-call | flops 7500000256 | bytes 1706112 | tf_op jit(solution)/shard_map/pallas_call | solution.py:51
  962.1 35.9 %shard_map.214 = (bf16[4,2,128,512]{3,2,1,0:T(8,128)(2,1)S(1)}, bf16[16,128,128]{2,1,0:T(8,128)(2,1)S(1)}, bf16[16,128,128]{2,1,0:T(8,128)(2,1)S(1)}) custom-call(s32[32]{0:T(128)S(1)} %fusion.41.loc_ref, s32[4]{0:T(128)S(1)} %pad_add_fusion.pos_ref, bf16[4,2,128,512]{3,2,1,0:T(8,128)(2,1)S(1)} %copy-done.96, bf16[4,2,128,512]{3,2,1,0:T(8,128)(2,1)S(1)} %bitcast.222, ...), custom_call_target="tpu_custom_call" | custom-call | flops 4823449600 | bytes 1118226 | tf_op jit(solution)/shard_map/pallas_call | solution.py:51
  1006.4 35.7 %shard_map.215 = (bf16[4,2,128,512]{3,2,1,0:T(8,128)(2,1)S(1)}, bf16[16,128,128]{2,1,0:T(8,128)(2,1)S(1)}, bf16[16,128,128]{2,1,0:T(8,128)(2,1)S(1)}) custom-call(s32[32]{0:T(128)S(1)} %fusion.41.loc_ref, s32[4]{0:T(128)S(1)} %pad_add_fusion.pos_ref, bf16[4,2,128,512]{3,2,1,0:T(8,128)(2,1)S(1)} %copy-done.96, ...), custom_call_target="tpu_custom_call", output_to_operand_aliasing={{0}: (9, {})} | custom-call | flops 4823449600 | bytes 1118226 | tf_op jit(solution)/shard_map/pallas_call | solution.py:51
  1085.0 11.4 collective-permute-done.48
  1114.1 78.6 %shard_map.219 = (bf16[256,2048]{1,0:T(8,128)(2,1)S(1)}, bf16[256,2048]{1,0:T(8,128)(2,1)S(1)}, bf16[256,2048]{1,0:T(8,128)(2,1)S(1)}, bf16[256,2048]{1,0:T(8,12...) custom-call(bf16[512,2048]{1,0:T(8,128)(2,1)} %copy-done.85, bf16[512,2048]{1,0:T(8,128)(2,1)} %copy-done.86, ...), custom_call_target="tpu_custom_call" | custom-call | flops 7500000256 | bytes 1444992 | tf_op jit(solution)/shard_map/pallas_call | solution.py:51
  1206.0 11.5 shard_map.220
  1218.2 13.6 shard_map.221
  1231.9 11.2 shard_map.222
  1243.1 11.3 shard_map.223
  1254.4 20.3 %shard_map.224 = (bf16[512,2048]{1,0:T(8,128)(2,1)S(1)}, bf16[512,2048]{1,0:T(8,128)(2,1)S(1)}) custom-call(bf16[1024,1408]{1,0:T(8,128)(2,1)} %get-tuple-element.412.refs_4_.refs_0_, bf16[1024,1408]{1,0:T(8,128)(2,1)} %get-tuple-element.410.refs_4_.refs_1_, bf16[1024,1408]{1,0:T(8,128)(2,1)} %all-gather.11.cloned.1.call-done.refs_4_.refs_2_, ...), custom_call_target="tpu_custom_call" | custom-call | flops 11811160064 | bytes 21495808 | tf_op jit(solution)/shard_map/pallas_call | solution.py:51
  1287.1 57.7 %shard_map.225 = (bf16[256,2048]{1,0:T(8,128)(2,1)S(1)}, bf16[256,2048]{1,0:T(8,128)(2,1)S(1)}, bf16[256,2048]{1,0:T(8,128)(2,1)S(1)}, bf16[256,2048]{1,0:T(8,12...) custom-call(bf16[512,2048]{1,0:T(8,128)(2,1)} %copy-done.104, bf16[512,2048]{1,0:T(8,128)(2,1)} %copy-done.105, ...), custom_call_target="tpu_custom_call" | custom-call | flops 7500000256 | bytes 1706112 | tf_op jit(solution)/shard_map/pallas_call | solution.py:51
  1363.2 36.0 %shard_map.227 = (bf16[4,2,128,512]{3,2,1,0:T(8,128)(2,1)S(1)}, bf16[16,128,128]{2,1,0:T(8,128)(2,1)S(1)}, bf16[16,128,128]{2,1,0:T(8,128)(2,1)S(1)}) custom-call(s32[32]{0:T(128)S(1)} %fusion.41.loc_ref, s32[4]{0:T(128)S(1)} %pad_add_fusion.pos_ref, bf16[4,2,128,512]{3,2,1,0:T(8,128)(2,1)S(1)} %copy-done.90, bf16[4,2,128,512]{3,2,1,0:T(8,128)(2,1)S(1)} %bitcast.220, ...), custom_call_target="tpu_custom_call" | custom-call | flops 4823449600 | bytes 1118226 | tf_op jit(solution)/shard_map/pallas_call | solution.py:51
  1417.1 36.5 %shard_map.228 = (bf16[4,2,128,512]{3,2,1,0:T(8,128)(2,1)S(1)}, bf16[16,128,128]{2,1,0:T(8,128)(2,1)}, bf16[16,128,128]{2,1,0:T(8,128)(2,1)S(1)}) custom-call(s32[32]{0:T(128)S(1)} %fusion.41.loc_ref, s32[4]{0:T(128)S(1)} %pad_add_fusion.pos_ref, bf16[4,2,128,512]{3,2,1,0:T(8,128)(2,1)S(1)} %copy-done.90, ...), custom_call_target="tpu_custom_call", output_to_operand_aliasing={{0}: (9, {})} | custom-call | flops 4823449600 | bytes 1118226 | tf_op jit(solution)/shard_map/pallas_call | solution.py:51
  1502.7 9.9 collective-permute-start.74
  1516.8 23.6 %collective-permute-done.74 = bf16[2,128,2048]{2,1,0:T(8,128)(2,1)} collective-permute-done((bf16[2,128,2048]{2,1,0:T(8,128)(2,1)S(1)}, bf16[2,128,2048]{2,1,0:T(8,128)(2,1)}, u32[]{:S(2)}, u32[]{:S(2)}) %collective-permute-start.74) | collective-permute-done | bytes 1048608 | tf_op jit(solution)/shard_map/ppermute | solution.py:116
  1556.3 35.2 %shard_map.232 = (bf16[256,2048]{1,0:T(8,128)(2,1)S(1)}, f32[1,2048]{1,0:T(1,128)}, f32[1,2048]{1,0:T(1,128)S(1)}, bf16[4,256,640]{2,1,0:T(8,128)(2,1)S(1)}) custom-call(bf16[512,2048]{1,0:T(8,128)(2,1)S(1)} %copy-done.83, bf16[512,2048]{1,0:T(8,128)(2,1)} %copy-done.84, f32[256,2048]{1,0:T(8,128)} %get-tuple-element.477.refs_2_, f32[1,2048]{1,0:T(1,128)S(1)} %copy-done.75, ...), custom_call_target="tpu_custom_call" | custom-call | flops 7500000256 | bytes 1510528 | tf_op jit(solution)/shard_map/pallas_call | solution.py:51
  1610.5 18.6 %collective-permute-start.79 = (f32[4,256]{1,0:T(4,128)S(1)}, f32[4,256]{1,0:T(4,128)S(1)}, u32[]{:S(2)}, u32[]{:S(2)}) collective-permute-start(f32[4,256]{1,0:T(4,128)S(1)} %bitcast.253), channel_id=1, source_target_pairs={{0,4},{2,6},{4,0},{6,2},{8,12},{10,14},{12,8},{14,10},{1,5},{3,7},... | collective-permute-start | bytes 12296 | tf_op jit(solution)/shard_map/ppermute | solution.py:23
  1643.8 9.4 collective-permute-done.71
  1653.3 14.8 collective-permute-done.70
  1691.8 12.8 collective-permute-done.84
  (667 shorter events, 473.4 us)
Async XLA Ops:
  7.2 138.5 %all-gather.9.cloned.1.call-start = ((), (), s32[]{:S(2)}) async-start(), calls=%async_computation.8 | async-start | bytes 5308416 | tf_op jit(solution)/shard_map/all_gather | solution.py:983
  31.6 187.5 %all-gather.11.cloned.1.call-start = ((), (), s32[]{:S(2)}) async-start(), calls=%async_computation.9 | async-start | bytes 3604480 | tf_op jit(solution)/shard_map/all_gather | solution.py:77
  53.0 237.0 %all-gather.15.cloned.1.call-start = ((), (), s32[]{:S(2)}) async-start(), calls=%async_computation.11 | async-start | bytes 3604480 | tf_op jit(solution)/shard_map/all_gather | solution.py:77
  125.9 198.2 %all-gather.13.cloned.1.call-start = ((), (), s32[]{:S(2)}) async-start(), calls=%async_computation.10 | async-start | bytes 3604480 | tf_op jit(solution)/shard_map/all_gather | solution.py:77
  157.0 273.1 %all-gather.17.cloned.1.call-start = ((), (), s32[]{:S(2)}) async-start(), calls=%async_computation.12 | async-start | bytes 5308416 | tf_op jit(solution)/shard_map/all_gather | solution.py:983
  157.6 328.0 %all-gather.19.cloned.1.call-start = ((), (), s32[]{:S(2)}) async-start(), calls=%async_computation.13 | async-start | bytes 3604480 | tf_op jit(solution)/shard_map/all_gather | solution.py:77
  157.7 36.4 %collective-permute-start.7 = (bf16[4,2,128,128]{3,2,1,0:T(8,128)(2,1)}, bf16[4,2,128,128]{3,2,1,0:T(8,128)(2,1)S(1)}, u32[]{:S(2)}, u32[]{:S(2)}) collective-permute-start(bf16[4,2,128,128]{3,2,1,0:T(8,128)(2,1)} %copy-done.71), channel_id=1, source_target_pairs={{0,4},{2,6},{4,0},{6,2},{8,12},{10,14},{12,8},{14,10},{1,5},{3,7},... | collective-permute-start | bytes 786440 | tf_op jit(solution)/shard_map/ppermute | solution.py:23
  175.9 35.4 %collective-permute-start.6 = (bf16[4,2,128,128]{3,2,1,0:T(8,128)(2,1)}, bf16[4,2,128,128]{3,2,1,0:T(8,128)(2,1)S(1)}, u32[]{:S(2)}, u32[]{:S(2)}) collective-permute-start(bf16[4,2,128,128]{3,2,1,0:T(8,128)(2,1)} %copy-done.71), channel_id=1, source_target_pairs={{0,2},{2,0},{4,6},{6,4},{8,10},{10,8},{12,14},{14,12},{1,3},{3,1},... | collective-permute-start | bytes 786440 | tf_op jit(solution)/shard_map/ppermute | solution.py:23
  219.2 63.1 %collective-permute-start.14 = (bf16[1024,1408]{1,0:T(8,128)(2,1)}, bf16[1024,1408]{1,0:T(8,128)(2,1)}, u32[]{:S(2)}, u32[]{:S(2)}) collective-permute-start(bf16[1024,1408]{1,0:T(8,128)(2,1)} %all-gather.11.cloned.1.call-done.refs_4_.refs_2_), channel_id=1, source_target_pairs={{0,2},{2,0},{4,6},{6,4},{8,10},{10,8},{12,14},{14,12},{1,3},{3,1},... | collective-permute-start | bytes 8650760 | tf_op jit(solution)/shard_map/ppermute | solution.py:23
  265.1 354.4 %all-gather.21.cloned.1.call-start = ((), (), s32[]{:S(2)}) async-start(), calls=%async_computation.14 | async-start | bytes 3604480 | tf_op jit(solution)/shard_map/all_gather | solution.py:77
  290.0 93.1 %collective-permute-start.18 = (bf16[1024,1408]{1,0:T(8,128)(2,1)}, bf16[1024,1408]{1,0:T(8,128)(2,1)}, u32[]{:S(2)}, u32[]{:S(2)}) collective-permute-start(bf16[1024,1408]{1,0:T(8,128)(2,1)} %all-gather.15.cloned.1.call-done.refs_6_.refs_4_), channel_id=1, source_target_pairs={{0,2},{2,0},{4,6},{6,4},{8,10},{10,8},{12,14},{14,12},{1,3},{3,1},... | collective-permute-start | bytes 8650760 | tf_op jit(solution)/shard_map/ppermute | solution.py:23
  383.1 102.5 %collective-permute-start.20 = (bf16[1024,1408]{1,0:T(8,128)(2,1)}, bf16[1024,1408]{1,0:T(8,128)(2,1)}, u32[]{:S(2)}, u32[]{:S(2)}) collective-permute-start(bf16[1024,1408]{1,0:T(8,128)(2,1)} %all-gather.13.cloned.1.call-done.refs_1_.refs_4_), channel_id=1, source_target_pairs={{0,2},{2,0},{4,6},{6,4},{8,10},{10,8},{12,14},{14,12},{1,3},{3,1},... | collective-permute-start | bytes 8650760 | tf_op jit(solution)/shard_map/ppermute | solution.py:23
  387.8 277.8 %all-gather.23.cloned.1.call-start = ((), (), s32[]{:S(2)}) async-start(), calls=%async_computation.15 | async-start | bytes 3604480 | tf_op jit(solution)/shard_map/all_gather | solution.py:77
  485.6 73.6 %collective-permute-start.21 = (bf16[1024,1408]{1,0:T(8,128)(2,1)}, bf16[1024,1408]{1,0:T(8,128)(2,1)S(1)}, u32[]{:S(2)}, u32[]{:S(2)}) collective-permute-start(bf16[1024,1408]{1,0:T(8,128)(2,1)} %all-gather.19.cloned.1.call-done.refs_4_.refs_2_), channel_id=1, source_target_pairs={{0,2},{2,0},{4,6},{6,4},{8,10},{10,8},{12,14},{14,12},{1,3},{3,1},... | collective-permute-start | bytes 8650760 | tf_op jit(solution)/shard_map/ppermute | solution.py:23
  570.7 40.5 %collective-permute-start.25 = (bf16[4,2,128,128]{3,2,1,0:T(8,128)(2,1)}, bf16[4,2,128,128]{3,2,1,0:T(8,128)(2,1)}, u32[]{:S(2)}, u32[]{:S(2)}) collective-permute-start(bf16[4,2,128,128]{3,2,1,0:T(8,128)(2,1)} %get-tuple-element.289), channel_id=1, source_target_pairs={{0,8},{2,10},{4,12},{6,14},{8,0},{10,2},{12,4},{14,6},{1,9},{3,11}... | collective-permute-start | bytes 786440 | tf_op jit(solution)/shard_map/ppermute | solution.py:23
  571.4 40.1 %collective-permute-start.22 = (bf16[4,2,128,128]{3,2,1,0:T(8,128)(2,1)}, bf16[4,2,128,128]{3,2,1,0:T(8,128)(2,1)}, u32[]{:S(2)}, u32[]{:S(2)}) collective-permute-start(bf16[4,2,128,128]{3,2,1,0:T(8,128)(2,1)} %get-tuple-element.289), channel_id=1, source_target_pairs={{0,2},{2,0},{4,6},{6,4},{8,10},{10,8},{12,14},{14,12},{1,3},{3,1},... | collective-permute-start | bytes 786440 | tf_op jit(solution)/shard_map/ppermute | solution.py:23
  571.6 376.0 %reduce-scatter.9.cloned.1.call-start = ((), (), s32[]{:S(2)}) async-start(), calls=%async_computation.16 | async-start | bytes 3604480 | tf_op jit(solution)/shard_map/reduce_scatter | solution.py:81
  576.8 36.7 %collective-permute-start.24 = (bf16[4,2,128,128]{3,2,1,0:T(8,128)(2,1)}, bf16[4,2,128,128]{3,2,1,0:T(8,128)(2,1)S(1)}, u32[]{:S(2)}, u32[]{:S(2)}) collective-permute-start(bf16[4,2,128,128]{3,2,1,0:T(8,128)(2,1)} %collective-permute-done.23), channel_id=1, source_target_pairs={{0,2},{2,0},{4,6},{6,4},{8,10},{10,8},{12,14},{14,12},{1,3},{3,1},... | collective-permute-start | bytes 786440 | tf_op jit(solution)/shard_map/ppermute | solution.py:23
  619.5 58.6 %collective-permute-start.29 = (bf16[1024,1408]{1,0:T(8,128)(2,1)}, bf16[1024,1408]{1,0:T(8,128)(2,1)}, u32[]{:S(2)}, u32[]{:S(2)}) collective-permute-start(bf16[1024,1408]{1,0:T(8,128)(2,1)} %all-gather.21.cloned.1.call-done.refs_6_.refs_4_), channel_id=1, source_target_pairs={{0,2},{2,0},{4,6},{6,4},{8,10},{10,8},{12,14},{14,12},{1,3},{3,1},... | collective-permute-start | bytes 8650760 | tf_op jit(solution)/shard_map/ppermute | solution.py:23
  687.2 62.6 %collective-permute-start.30 = (bf16[1024,1408]{1,0:T(8,128)(2,1)S(1)}, bf16[1024,1408]{1,0:T(8,128)(2,1)S(1)}, u32[]{:S(2)}, u32[]{:S(2)}) collective-permute-start(bf16[1024,1408]{1,0:T(8,128)(2,1)S(1)} %copy-done.121), channel_id=1, source_target_pairs={{0,2},{2,0},{4,6},{6,4},{8,10},{10,8},{12,14},{14,12},{1,3},{3,1},... | collective-permute-start | bytes 8650760 | tf_op jit(solution)/shard_map/ppermute | solution.py:23
  787.0 58.7 %collective-permute-start.36 = (bf16[2,128,2048]{2,1,0:T(8,128)(2,1)S(1)}, bf16[2,128,2048]{2,1,0:T(8,128)(2,1)}, u32[]{:S(2)}, u32[]{:S(2)}) collective-permute-start(bf16[2,128,2048]{2,1,0:T(8,128)(2,1)S(1)} %bitcast.229), channel_id=1, source_target_pairs={{16,0},{17,15},{18,2},{19,13},{20,4},{21,11},{22,6},{23,9},{24,8},... | collective-permute-start | bytes 3145736 | tf_op jit(solution)/shard_map/ppermute | solution.py:116
  788.3 57.4 %collective-permute-start.35 = (bf16[2,128,2048]{2,1,0:T(8,128)(2,1)S(1)}, bf16[2,128,2048]{2,1,0:T(8,128)(2,1)}, u32[]{:S(2)}, u32[]{:S(2)}) collective-permute-start(bf16[2,128,2048]{2,1,0:T(8,128)(2,1)S(1)} %bitcast.230), channel_id=1, source_target_pairs={{0,0},{1,15},{2,2},{3,13},{4,4},{5,11},{6,6},{7,9},{8,8},{9,7},{10... | collective-permute-start | bytes 3145736 | tf_op jit(solution)/shard_map/ppermute | solution.py:116
  805.0 74.6 %collective-permute-start.37 = (bf16[4,256,1408]{2,1,0:T(8,128)(2,1)}, bf16[4,256,1408]{2,1,0:T(8,128)(2,1)}, u32[]{:S(2)}, u32[]{:S(2)}) collective-permute-start(bf16[4,256,1408]{2,1,0:T(8,128)(2,1)} %get-tuple-element.313), channel_id=1, source_target_pairs={{0,2},{2,0},{4,6},{6,4},{8,10},{10,8},{12,14},{14,12},{1,3},{3,1},... | collective-permute-start | bytes 8650760 | tf_op jit(solution)/shard_map/ppermute | solution.py:23
  806.9 42.1 %collective-permute-start.34 = (bf16[256,2048]{1,0:T(8,128)(2,1)S(1)}, bf16[256,2048]{1,0:T(8,128)(2,1)}, u32[]{:S(2)}, u32[]{:S(2)}) collective-permute-start(bf16[256,2048]{1,0:T(8,128)(2,1)S(1)} %add_convert_fusion.10), channel_id=1, source_target_pairs={{0,16},{16,0},{1,17},{17,1},{2,18},{18,2},{3,19},{19,3},{4,20},{20... | collective-permute-start | bytes 3145736 | tf_op jit(solution)/shard_map/ppermute | solution.py:23
  883.7 161.9 %reduce-scatter.11.cloned.1.call-start = ((), (), s32[]{:S(2)}) async-start(), calls=%async_computation.17 | async-start | bytes 3604480 | tf_op jit(solution)/shard_map/reduce_scatter | solution.py:81
  883.7 64.0 %collective-permute-start.38 = (bf16[4,256,1408]{2,1,0:T(8,128)(2,1)}, bf16[4,256,1408]{2,1,0:T(8,128)(2,1)}, u32[]{:S(2)}, u32[]{:S(2)}) collective-permute-start(bf16[4,256,1408]{2,1,0:T(8,128)(2,1)} %get-tuple-element.343), channel_id=1, source_target_pairs={{0,2},{2,0},{4,6},{6,4},{8,10},{10,8},{12,14},{14,12},{1,3},{3,1},... | collective-permute-start | bytes 8650760 | tf_op jit(solution)/shard_map/ppermute | solution.py:23
  952.6 244.1 %reduce-scatter.13.cloned.1.call-start = ((), (), s32[]{:S(2)}) async-start(), calls=%async_computation.18 | async-start | bytes 3604480 | tf_op jit(solution)/shard_map/reduce_scatter | solution.py:81
  952.7 92.9 %collective-permute-start.39 = (bf16[4,256,1408]{2,1,0:T(8,128)(2,1)}, bf16[4,256,1408]{2,1,0:T(8,128)(2,1)}, u32[]{:S(2)}, u32[]{:S(2)}) collective-permute-start(bf16[4,256,1408]{2,1,0:T(8,128)(2,1)} %get-tuple-element.348), channel_id=1, source_target_pairs={{0,2},{2,0},{4,6},{6,4},{8,10},{10,8},{12,14},{14,12},{1,3},{3,1},... | collective-permute-start | bytes 8650760 | tf_op jit(solution)/shard_map/ppermute | solution.py:23
  998.0 46.7 %collective-permute-start.40 = (bf16[4,4,128,128]{3,2,1,0:T(8,128)(2,1)S(1)}, bf16[4,4,128,128]{3,2,1,0:T(8,128)(2,1)S(1)}, u32[]{:S(2)}, u32[]{:S(2)}) collective-permute-start(bf16[4,4,128,128]{3,2,1,0:T(8,128)(2,1)S(1)} %bitcast.235), channel_id=1, source_target_pairs={{0,2},{2,0},{4,6},{6,4},{8,10},{10,8},{12,14},{14,12},{1,3},{3,1},... | collective-permute-start | bytes 1572872 | tf_op jit(solution)/shard_map/ppermute | solution.py:23
  999.4 59.2 %collective-permute-start.42 = (bf16[2,128,2048]{2,1,0:T(8,128)(2,1)}, bf16[2,128,2048]{2,1,0:T(8,128)(2,1)}, u32[]{:S(2)}, u32[]{:S(2)}) collective-permute-start(bf16[2,128,2048]{2,1,0:T(8,128)(2,1)} %bitcast.38), channel_id=1, source_target_pairs={{16,16},{17,31},{18,18},{19,29},{20,20},{21,27},{22,22},{23,25},{2... | collective-permute-start | bytes 3145736 | tf_op jit(solution)/shard_map/ppermute | solution.py:116
  1001.0 58.5 %collective-permute-start.41 = (bf16[2,128,2048]{2,1,0:T(8,128)(2,1)}, bf16[2,128,2048]{2,1,0:T(8,128)(2,1)}, u32[]{:S(2)}, u32[]{:S(2)}) collective-permute-start(bf16[2,128,2048]{2,1,0:T(8,128)(2,1)} %bitcast.38), channel_id=1, source_target_pairs={{0,16},{1,31},{2,18},{3,29},{4,20},{5,27},{6,22},{7,25},{8,24},{9,... | collective-permute-start | bytes 3145736 | tf_op jit(solution)/shard_map/ppermute | solution.py:116
  1053.1 231.9 %reduce-scatter.15.cloned.1.call-start = ((), (), s32[]{:S(2)}) async-start(), calls=%async_computation.19 | async-start | bytes 2949120 | tf_op jit(solution)/shard_map/reduce_scatter | solution.py:81
  1114.0 82.7 %collective-permute-start.50 = (bf16[4,256,1152]{2,1,0:T(8,128)(2,1)S(1)}, bf16[4,256,1152]{2,1,0:T(8,128)(2,1)}, u32[]{:S(2)}, u32[]{:S(2)}) collective-permute-start(bf16[4,256,1152]{2,1,0:T(8,128)(2,1)S(1)} %pad_maximum_fusion), channel_id=1, source_target_pairs={{0,2},{2,0},{4,6},{6,4},{8,10},{10,8},{12,14},{14,12},{1,3},{3,1},... | collective-permute-start | bytes 7077896 | tf_op jit(solution)/shard_map/ppermute | solution.py:23
  1201.0 146.4 %reduce-scatter.17.cloned.1.call-start = ((), (), s32[]{:S(2)}) async-start(), calls=%async_computation.20 | async-start | bytes 3604480 | tf_op jit(solution)/shard_map/reduce_scatter | solution.py:81
  1217.5 64.1 %collective-permute-start.51 = (bf16[4,256,1408]{2,1,0:T(8,128)(2,1)}, bf16[4,256,1408]{2,1,0:T(8,128)(2,1)S(1)}, u32[]{:S(2)}, u32[]{:S(2)}) collective-permute-start(bf16[4,256,1408]{2,1,0:T(8,128)(2,1)} %get-tuple-element.397), channel_id=1, source_target_pairs={{0,2},{2,0},{4,6},{6,4},{8,10},{10,8},{12,14},{14,12},{1,3},{3,1},... | collective-permute-start | bytes 8650760 | tf_op jit(solution)/shard_map/ppermute | solution.py:23
  1283.9 173.6 %reduce-scatter.19.cloned.1.call-start = ((), (), s32[]{:S(2)}) async-start(), calls=%async_computation.21 | async-start | bytes 3604480 | tf_op jit(solution)/shard_map/reduce_scatter | solution.py:81
  1284.0 63.4 %collective-permute-start.52 = (bf16[4,256,1408]{2,1,0:T(8,128)(2,1)}, bf16[4,256,1408]{2,1,0:T(8,128)(2,1)}, u32[]{:S(2)}, u32[]{:S(2)}) collective-permute-start(bf16[4,256,1408]{2,1,0:T(8,128)(2,1)} %get-tuple-element.424), channel_id=1, source_target_pairs={{0,2},{2,0},{4,6},{6,4},{8,10},{10,8},{12,14},{14,12},{1,3},{3,1},... | collective-permute-start | bytes 8650760 | tf_op jit(solution)/shard_map/ppermute | solution.py:23
  1352.4 327.3 %reduce-scatter.21.cloned.1.call-start = ((), (), s32[]{:S(2)}) async-start(), calls=%async_computation.22 | async-start | bytes 1310720 | tf_op jit(solution)/shard_map/reduce_scatter | solution.py:81
  1352.4 105.1 %collective-permute-start.54 = (bf16[4,256,1408]{2,1,0:T(8,128)(2,1)}, bf16[4,256,1408]{2,1,0:T(8,128)(2,1)}, u32[]{:S(2)}, u32[]{:S(2)}) collective-permute-start(bf16[4,256,1408]{2,1,0:T(8,128)(2,1)} %get-tuple-element.439), channel_id=1, source_target_pairs={{0,2},{2,0},{4,6},{6,4},{8,10},{10,8},{12,14},{14,12},{1,3},{3,1},... | collective-permute-start | bytes 8650760 | tf_op jit(solution)/shard_map/ppermute | solution.py:23
  1360.1 46.0 %collective-permute-start.63 = (bf16[256,1152]{1,0:T(8,128)(2,1)S(1)}, bf16[256,1152]{1,0:T(8,128)(2,1)S(1)}, u32[]{:S(2)}, u32[]{:S(2)}) collective-permute-start(bf16[256,1152]{1,0:T(8,128)(2,1)S(1)} %copy-done.145), channel_id=1, source_target_pairs={{0,16},{1,17},{2,18},{3,19},{4,20},{5,21},{6,22},{7,23},{8,24},{9,... | collective-permute-start | bytes 1769480 | tf_op jit(solution)/shard_map/ppermute | solution.py:27
  1400.6 54.7 %collective-permute-start.64 = (bf16[256,1408]{1,0:T(8,128)(2,1)S(1)}, bf16[256,1408]{1,0:T(8,128)(2,1)S(1)}, u32[]{:S(2)}, u32[]{:S(2)}) collective-permute-start(bf16[256,1408]{1,0:T(8,128)(2,1)S(1)} %copy-done.136), channel_id=1, source_target_pairs={{0,16},{1,17},{2,18},{3,19},{4,20},{5,21},{6,22},{7,23},{8,24},{9,... | collective-permute-start | bytes 2162696 | tf_op jit(solution)/shard_map/ppermute | solution.py:27
  1404.7 50.6 %collective-permute-start.65 = (bf16[256,1408]{1,0:T(8,128)(2,1)S(1)}, bf16[256,1408]{1,0:T(8,128)(2,1)S(1)}, u32[]{:S(2)}, u32[]{:S(2)}) collective-permute-start(bf16[256,1408]{1,0:T(8,128)(2,1)S(1)} %copy-done.138), channel_id=1, source_target_pairs={{0,16},{1,17},{2,18},{3,19},{4,20},{5,21},{6,22},{7,23},{8,24},{9,... | collective-permute-start | bytes 2162696 | tf_op jit(solution)/shard_map/ppermute | solution.py:27
  1406.1 49.2 %collective-permute-start.66 = (bf16[256,1408]{1,0:T(8,128)(2,1)S(1)}, bf16[256,1408]{1,0:T(8,128)(2,1)S(1)}, u32[]{:S(2)}, u32[]{:S(2)}) collective-permute-start(bf16[256,1408]{1,0:T(8,128)(2,1)S(1)} %copy-done.128), channel_id=1, source_target_pairs={{0,16},{1,17},{2,18},{3,19},{4,20},{5,21},{6,22},{7,23},{8,24},{9,... | collective-permute-start | bytes 2162696 | tf_op jit(solution)/shard_map/ppermute | solution.py:27
  1416.7 38.7 %collective-permute-start.55 = (bf16[4,4,128,128]{3,2,1,0:T(8,128)(2,1)S(1)}, bf16[4,4,128,128]{3,2,1,0:T(8,128)(2,1)S(1)}, u32[]{:S(2)}, u32[]{:S(2)}) collective-permute-start(bf16[4,4,128,128]{3,2,1,0:T(8,128)(2,1)S(1)} %bitcast.234), channel_id=1, source_target_pairs={{0,2},{2,0},{4,6},{6,4},{8,10},{10,8},{12,14},{14,12},{1,3},{3,1},... | collective-permute-start | bytes 1572872 | tf_op jit(solution)/shard_map/ppermute | solution.py:23
  1501.9 179.1 %reduce-scatter.23.cloned.1.call-start = ((), (), s32[]{:S(2)}) async-start(), calls=%async_computation.23 | async-start | bytes 3604480 | tf_op jit(solution)/shard_map/reduce_scatter | solution.py:81
  1502.7 37.6 %collective-permute-start.74 = (bf16[2,128,2048]{2,1,0:T(8,128)(2,1)S(1)}, bf16[2,128,2048]{2,1,0:T(8,128)(2,1)}, u32[]{:S(2)}, u32[]{:S(2)}) collective-permute-start(bf16[2,128,2048]{2,1,0:T(8,128)(2,1)S(1)} %bitcast.211), channel_id=1, source_target_pairs={{0,16},{1,31},{2,18},{3,29},{4,20},{5,27},{6,22},{7,25},{8,24},{9,... | collective-permute-start | bytes 3145736 | tf_op jit(solution)/shard_map/ppermute | solution.py:116
  1600.1 68.1 %collective-permute-start.73 = (bf16[2,128,2048]{2,1,0:T(8,128)(2,1)S(1)}, bf16[2,128,2048]{2,1,0:T(8,128)(2,1)S(1)}, u32[]{:S(2)}, u32[]{:S(2)}) collective-permute-start(bf16[2,128,2048]{2,1,0:T(8,128)(2,1)S(1)} %bitcast.231), channel_id=1, source_target_pairs={{16,0},{17,15},{18,2},{19,13},{20,4},{21,11},{22,6},{23,9},{24,8},... | collective-permute-start | bytes 3145736 | tf_op jit(solution)/shard_map/ppermute | solution.py:116
  1601.4 66.8 %collective-permute-start.72 = (bf16[2,128,2048]{2,1,0:T(8,128)(2,1)S(1)}, bf16[2,128,2048]{2,1,0:T(8,128)(2,1)}, u32[]{:S(2)}, u32[]{:S(2)}) collective-permute-start(bf16[2,128,2048]{2,1,0:T(8,128)(2,1)S(1)} %bitcast.232), channel_id=1, source_target_pairs={{0,0},{1,15},{2,2},{3,13},{4,4},{5,11},{6,6},{7,9},{8,8},{9,7},{10... | collective-permute-start | bytes 3145736 | tf_op jit(solution)/shard_map/ppermute | solution.py:116
  (218 other events, 2554.7 us)
Sparse Core Ops, SparseCore 0:
  31.8 97.0 all-gather.8
  130.9 65.8 all-gather.10
  199.0 65.7 all-gather.14
  266.2 57.8 all-gather.12
  326.1 94.2 all-gather.16
  421.8 63.7 all-gather.18
  487.2 57.8 all-gather.20
  571.8 70.1 all-gather.22
  883.8 54.0 reduce-scatter.8
  952.7 54.9 reduce-scatter.10
  1053.2 72.1 reduce-scatter.12
  1201.1 47.0 reduce-scatter.14
  1284.0 55.6 reduce-scatter.16
  1352.5 56.6 reduce-scatter.18
  1502.1 42.4 reduce-scatter.20
  1547.4 67.2 reduce-scatter.22

commit v3 on v2

--- a/solution.py
+++ b/solution.py
@@ -640,7 +640,7 @@
 
 
 def attend_kernel(
-    block, loc_ref, pos_ref, q_ref, kv_ref, o_ref, lse_ref, k_ref, vt_ref, m_ref, acc_ref
+    block, loc_ref, pos_ref, q_ref, kv_ref, o_ref, lse_ref, k_ref, vt_ref, m_ref, acc_ref, s_ref
 ):
     piece = pl.program_id(1)
     rows = q_ref.shape[2]
@@ -663,15 +663,15 @@
     m_ref[...] = jnp.full(m_ref.shape, -1e30, F32)
     acc_ref[...] = jnp.zeros(acc_ref.shape, F32)
 
-    def step(j, masked):
+    def scores_of(j):
         first = j * per_block
         keys = jnp.concatenate([k_ref[first + i] for i in range(per_block)], axis=0)
-        values = jnp.concatenate([vt_ref[first + i] for i in range(per_block)], axis=1)
-        scores = product(keys, queries)
-        if masked:
-            row = lax.broadcasted_iota(jnp.int32, scores.shape, 0)
-            column = lax.broadcasted_iota(jnp.int32, scores.shape, 1) % rows
-            scores = jnp.where(row + j * block <= column + pos, scores, -1e30)
+        return product(keys, queries)
+
+    def absorb(j, scores):
+        first = j * per_block
+        used = scores.shape[0] // rows
+        values = jnp.concatenate([vt_ref[first + i] for i in range(used)], axis=1)
         before = m_ref[...]
         now = jnp.maximum(before, jnp.max(scores, axis=0, keepdims=True))
         terms = jnp.exp(scores - now)
@@ -680,13 +680,33 @@
         m_ref[...] = now
 
     full = pos // block
+    s_ref[0] = scores_of(0)
 
     def loop(j, _):
-        step(j, False)
+        slot = j % 2
+        following = scores_of(j + 1)
+        absorb(j, s_ref[slot])
+        s_ref[1 - slot] = following
         return 0
 
     lax.fori_loop(0, full, loop, 0)
-    step(full, True)
+
+    def diagonal(size):
+        scores = s_ref[full % 2, :size]
+        row = lax.broadcasted_iota(jnp.int32, scores.shape, 0)
+        column = lax.broadcasted_iota(jnp.int32, scores.shape, 1) % rows
+        absorb(full, jnp.where(row + full * block <= column + pos, scores, -1e30))
+
+    half = pos - full * block < block // 2
+
+    @pl.when(half)
+    def _():
+        diagonal(block // 2)
+
+    @pl.when(jnp.logical_not(half))
+    def _():
+        diagonal(block)
+
     total = acc_ref[HD : HD + 1]
     out = acc_ref[:HD] / total
     lse_ref[0, 0] = m_ref[...] + jnp.log(total)
@@ -724,6 +744,7 @@
                 pltpu.VMEM((count, HD + GAIN_ROWS, rows), BF),
                 pltpu.VMEM((1, stacked), F32),
                 pltpu.VMEM((HD + GAIN_ROWS, stacked), F32),
+                pltpu.VMEM((2, block, stacked), F32),
             ],
         ),
     )
@@ -780,11 +801,11 @@
     logs = lse_ref[0, 0]
     dq_acc[...] = jnp.zeros(dq_acc.shape, F32)
 
-    def step(j, masked):
+    def step(j, masked, used=per_block):
         first = j * per_block
-        keys = jnp.concatenate([k_ref[first + i] for i in range(per_block)], axis=0)
-        values = jnp.concatenate([v_ref[first + i] for i in range(per_block)], axis=0)
-        keys_t = jnp.concatenate([kt_ref[first + i] for i in range(per_block)], axis=1)
+        keys = jnp.concatenate([k_ref[first + i] for i in range(used)], axis=0)
+        values = jnp.concatenate([v_ref[first + i] for i in range(used)], axis=0)
+        keys_t = jnp.concatenate([kt_ref[first + i] for i in range(used)], axis=1)
         scores = product(keys, queries_t)
         probs = jnp.exp(scores - logs)
         if masked:
@@ -796,7 +817,7 @@
         dv = product(probs.astype(BF), grads)
         dk = product(grad_low, queries)
         dq_acc[...] += product(keys_t, grad_low)
-        for i in range(per_block):
+        for i in range(used):
             dk_acc[first + i] += dk[i * rows : (i + 1) * rows]
             dv_acc[first + i] += dv[i * rows : (i + 1) * rows]
 
@@ -807,7 +828,15 @@
         return 0
 
     lax.fori_loop(0, full, loop, 0)
-    step(full, True)
+    half = pos - full * block < block // 2
+
+    @pl.when(half)
+    def _():
+        step(full, True, per_block // 2)
+
+    @pl.when(jnp.logical_not(half))
+    def _():
+        step(full, True)
 
     first = lax.broadcasted_iota(jnp.int32, (rows, PAIR), 1) % HD < HD // 2
     for g in range(q_ref.shape[3] // PAIR):
@@ -989,9 +1018,10 @@
     down_0 = gather_line(after(down_l[0], q0))
     kv0 = jnp.concatenate(gather_blocks(kv_own), axis=0)
     attn_1 = gather_all(after(attn_l[1], q0))
-    attended0, lse0 = attend(q0, after(kv0, gate_0), loc, pos)
-    gate_0 = (gate_0, near(gate_0, kv0))
-    gate_1 = gather_line(after(gate_l[1], attended0))
+    kv0, gate_0 = lax.optimization_barrier((kv0, gate_0))
+    attended0, lse0 = attend(q0, kv0, loc, pos)
+    gate_0 = (gate_0, near(gate_0))
+    gate_1 = gather_line(after(gate_l[1], kv0))
     own, send = contract(
         [after(attended0, gate_0[1]).reshape(-1, s.heads)],
         [(attn_0,)],
@@ -1002,23 +1032,27 @@
     up_0 = (up_0, near(up_0, gate_0[1], own))
     upstream = take(after(out_grad, own))
     normed_ffn0, middle0, second_scale0, _ = exchange(
-        after(own, down_0), send, u, gains_l[0][1], ident=0
+        own, send, u, gains_l[0][1], ident=0
     )
     up_1 = gather_line(after(up_l[1], middle0))
+    line_down0 = down_0
     down_0 = (down_0, near(down_0, up_0[1], middle0))
     gate0, up0, hidden0 = gate_up(
-        [after(normed_ffn0[0], up_0[1], upstream), *normed_ffn0[1:]], (gate_0), up_0, s.depth
+        [after(normed_ffn0[0], up_0[1], upstream, line_down0), *normed_ffn0[1:]],
+        gate_0,
+        up_0,
+        s.depth,
     )
     upstream_other = after(partner(after(upstream, up_0[1]), "section", 1), hidden0)
     down_1 = gather_line(after(down_l[1], hidden0))
     gate_1 = (gate_1, near(gate_1, down_0[1]))
     own, send = contract(
-        [after(hidden0, upstream_other, attn_1)], [down_0], (None,), s.depth, s.width
+        [after(hidden0, upstream_other)], [down_0], (None,), s.depth, s.width
     )
     kept0 = (u, first_scale, normed, q0, kv0, attended0, lse0, middle0, second_scale0)
     kept0 += (normed_ffn0, gate0, up0, hidden0)
     normed, u, first_scale, _ = exchange(
-        after(own, gate_1[0]), send, middle0, gains_l[1][0], keep_f32=False, ident=1
+        own, send, middle0, gains_l[1][0], keep_f32=False, ident=1
     )
     out0 = u
     q1, kv_own = qkv_project(
@@ -1173,7 +1207,6 @@
                 ident=3,
             )
             grads[1] = upstream = grad2[0]
-            grads_out = give(upstream, 1)
             pack_got, d_up = after((pack_got, d_up), grad2[0])
             pack_near = near_sum(jnp.concatenate([qkv_keep, out_keep], axis=2), pack_got)
             d_attn = reduce_line(after(pack_near, d_up))
@@ -1194,6 +1227,7 @@
             )
             grads[0] = grads[0][0]
             qkv_near = near_sum(qkv_keep, got[0])
+            grads_out = give(after(grads[1], grads[0]), 1)
             blocks = qkv_near.reshape(count // 2, s.depth, -1)
             d_qkv = blocks[wide // 2].astype(F32)
             for j in range(1, count // 2):

time: 1730 us -> 1710 us (0.988)
  starting transfers between devices: 149 us -> 129 us
    ppermute x66, waiting for transfers between devices: 252 us -> 329 us  [partner(): return lax.ppermute(x, axis, [(i, i ^ bit) for i in range(peers)])]
    all_gather x6, waiting for transfers between devices: 88.5 us -> 13.8 us  [gather_line(): lax.all_gather(shard, 'wide', axis=0, tiled=True, axis_index_groups=lines())]
    unnamed x350 -> x362, local copies, waits for them, and re-layouts: 84 us -> 96.5 us
  transfers between devices with their start and end apart: 101 -> 101, of which waited for: 43 -> 40; matrix products, arithmetic and copies ran while one was open for 5% -> 5% of each run, Pallas kernels for 51% -> 51%
where the time goes in v3:
time: 1710 us; the launch traced here: 1700 us
  Pallas kernels  911 us (53%)
  waiting for transfers between devices  401 us (23%)
  starting transfers between devices  129 us (8%)
  local copies, waits for them, and re-layouts  120 us (7%)
  other arithmetic  93.5 us (5%)
  blocking collectives  26 us (2%)
    pallas_call x39, Pallas kernels, call(): pl.pallas_call(body, out_shape=outs, scratch_shapes=scratch, compiler_par...  911 us
    ppermute x66, waiting for transfers between devices, partner(): return lax.ppermute(x, axis, [(i, i ^ bit) for i in range(peers)])  329 us
    unnamed x362, local copies, waits for them, and re-layouts  96.5 us
    ppermute x66, starting transfers between devices, partner(): return lax.ppermute(x, axis, [(i, i ^ bit) for i in range(peers)])  76.2 us
    ppermute x10, starting transfers between devices, mirror(): return lax.ppermute(x, ('section', 'wide', 'tp'), pairs)  35.3 us
    ppermute x10, waiting for transfers between devices, mirror(): return lax.ppermute(x, ('section', 'wide', 'tp'), pairs)  34.4 us
  transfers between devices with their start and end apart: 101, of which 40 were waited for; matrix products, arithmetic and copies ran while one was open for 5% of the time, Pallas kernels for 51%

profile of v3, /device:TPU:1, one launch (start us, length us, event | category | flops | bytes accessed | tf_op | source)
XLA Modules:
  0.0 1697.2 jit_solution(10391137505915033528)
XLA Ops:
  17.2 12.2 collective-permute-done.5
  35.0 15.6 collective-permute-done.13
  59.0 26.0 %all_gather.27 = bf16[2,2048]{1,0:T(2,128)(2,1)S(1)} all-gather(bf16[2,256]{1,0:T(2,128)(2,1)S(1)} %pad_maximum_fusion.12), channel_id=1, replica_groups=mesh['section'=2,'wide'=8,'tp'=2] {'wide'}, dimensions={1}, use_global_device_ids=true | all-gather | bytes 9216 | tf_op jit(solution)/shard_map/all_gather | solution.py:999
  92.1 20.2 %collective-permute-done.2.refs_1_ = bf16[256,2048]{1,0:T(8,128)(2,1)S(1)} collective-permute-done((bf16[256,2048]{1,0:T(8,128)(2,1)S(1)}, bf16[256,2048]{1,0:T(8,128)(2,1)S(1)}, u32[]{:S(2)}, u32[]{:S(2)}) %collective-permute-start.2) | collective-permute-done | bytes 1048608 | tf_op jit(solution)/shard_map/ppermute | solution.py:23
  113.8 10.8 collective-permute-done.16
  157.1 16.5 collective-permute-start.7
  175.8 18.6 %collective-permute-done.7 = bf16[4,2,128,128]{3,2,1,0:T(8,128)(2,1)S(1)} collective-permute-done((bf16[4,2,128,128]{3,2,1,0:T(8,128)(2,1)}, bf16[4,2,128,128]{3,2,1,0:T(8,128)(2,1)S(1)}, u32[]{:S(2)}, u32[]{:S(2)}) %collective-permute-start.7) | collective-permute-done | bytes 262176 | tf_op jit(solution)/shard_map/ppermute | solution.py:23
  199.6 10.6 collective-permute-done.9
  223.9 35.3 %shard_map.195 = (bf16[4,2,128,512]{3,2,1,0:T(8,128)(2,1)S(1)}, f32[4,2,1,1024]{3,2,1,0:T(1,128)S(1)}) custom-call(s32[32]{0:T(128)S(1)} %fusion.41.loc_ref, s32[4]{0:T(128)S(1)} %pad_add_fusion.pos_ref, bf16[4,2,128,512]{3,2,1,0:T(8,128)(2,1)S(1)} %copy-done.92, bf16[32,2,128,128]{3,2,1,0:T(8,128)(2,1)S(1)} %copy-done.80), custom_call_target="tpu_custom_call" | custom-call | flops 46137344000 | bytes 4227216 | tf_op jit(solution)/shard_map/pallas_call | solution.py:51
  259.2 23.9 %collective-permute-done.14.refs_5_.refs_3_ = bf16[1024,1408]{1,0:T(8,128)(2,1)S(1)} collective-permute-done((bf16[1024,1408]{1,0:T(8,128)(2,1)}, bf16[1024,1408]{1,0:T(8,128)(2,1)S(1)}, u32[]{:S(2)}, u32[]{:S(2)}) %collective-permute-start.14) | collective-permute-done | bytes 2883616 | tf_op jit(solution)/shard_map/ppermute | solution.py:23
  293.4 58.6 %shard_map.197 = (bf16[256,2048]{1,0:T(8,128)(2,1)S(1)}, bf16[256,2048]{1,0:T(8,128)(2,1)S(1)}, bf16[256,2048]{1,0:T(8,128)(2,1)S(1)}, bf16[256,2048]{1,0:T(8,12...) custom-call(bf16[512,2048]{1,0:T(8,128)(2,1)} %copy-done.101, bf16[512,2048]{1,0:T(8,128)(2,1)} %copy-done.102, ...), custom_call_target="tpu_custom_call" | custom-call | flops 60000002048 | bytes 12592128 | tf_op jit(solution)/shard_map/pallas_call | solution.py:51
  361.1 34.4 %collective-permute-done.15 = bf16[2,128,2048]{2,1,0:T(8,128)(2,1)} collective-permute-done((bf16[2,128,2048]{2,1,0:T(8,128)(2,1)}, bf16[2,128,2048]{2,1,0:T(8,128)(2,1)}, u32[]{:S(2)}, u32[]{:S(2)}) %collective-permute-start.15) | collective-permute-done | bytes 1048608 | tf_op jit(solution)/shard_map/ppermute | solution.py:116
  399.1 20.5 %shard_map.198 = (bf16[1024,1408]{1,0:T(8,128)(2,1)}, bf16[1024,1408]{1,0:T(8,128)(2,1)}, bf16[1024,1408]{1,0:T(8,128)(2,1)}) custom-call(bf16[256,2048]{1,0:T(8,128)(2,1)S(1)} %get-tuple-element.403.refs_0_, bf16[256,2048]{1,0:T(8,128)(2,1)S(1)} %get-tuple-element.404.refs_1_, bf16[256,2048]{1,0:T(8,128)(2,1)S(1)} %copy-done.3, ...), custom_call_target="tpu_custom_call" | custom-call | flops 11811160064 | bytes 24379392 | tf_op jit(solution)/shard_map/pallas_call | solution.py:51
  419.6 13.9 collective-permute-done.20.refs_2_.refs_5_
  434.3 20.2 %shard_map.199 = (bf16[512,2048]{1,0:T(8,128)(2,1)S(1)}, bf16[512,2048]{1,0:T(8,128)(2,1)S(1)}) custom-call(bf16[1024,1408]{1,0:T(8,128)(2,1)} %get-tuple-element.272.refs_0_.refs_4_, bf16[1024,1408]{1,0:T(8,128)(2,1)} %all-gather.15.cloned.1.call-done.refs_1_.refs_4_, bf16[1024,1408]{1,0:T(8,128)(2,1)} %collective-permute-done.20.refs_2_.refs_5_), custom_call_target="tpu_custom_call" | custom-call | flops 5905580032 | bytes 12845056 | tf_op jit(solution)/shard_map/pallas_call | solution.py:51
  457.2 59.6 %shard_map.200 = (bf16[256,2048]{1,0:T(8,128)(2,1)S(1)}, bf16[256,2048]{1,0:T(8,128)(2,1)S(1)}, bf16[256,2048]{1,0:T(8,128)(2,1)S(1)}, bf16[256,2048]{1,0:T(8,12...) custom-call(bf16[512,2048]{1,0:T(8,128)(2,1)} %copy-done.105, bf16[512,2048]{1,0:T(8,128)(2,1)} %copy-done.106, ...), custom_call_target="tpu_custom_call" | custom-call | flops 60000002048 | bytes 11543552 | tf_op jit(solution)/shard_map/pallas_call | solution.py:51
  540.2 22.6 %collective-permute-done.23 = bf16[4,2,128,128]{3,2,1,0:T(8,128)(2,1)} collective-permute-done((bf16[4,2,128,128]{3,2,1,0:T(8,128)(2,1)}, bf16[4,2,128,128]{3,2,1,0:T(8,128)(2,1)}, u32[]{:S(2)}, u32[]{:S(2)}) %collective-permute-start.23) | collective-permute-done | bytes 262176 | tf_op jit(solution)/shard_map/ppermute | solution.py:23
  565.4 22.5 %collective-permute-done.25 = bf16[4,2,128,128]{3,2,1,0:T(8,128)(2,1)} collective-permute-done((bf16[4,2,128,128]{3,2,1,0:T(8,128)(2,1)}, bf16[4,2,128,128]{3,2,1,0:T(8,128)(2,1)}, u32[]{:S(2)}, u32[]{:S(2)}) %collective-permute-start.25) | collective-permute-done | bytes 262176 | tf_op jit(solution)/shard_map/ppermute | solution.py:23
  599.4 35.3 %shard_map.202 = (bf16[4,2,128,512]{3,2,1,0:T(8,128)(2,1)S(1)}, f32[4,2,1,1024]{3,2,1,0:T(1,128)S(1)}) custom-call(s32[32]{0:T(128)S(1)} %fusion.41.loc_ref, s32[4]{0:T(128)S(1)} %pad_add_fusion.pos_ref, bf16[4,2,128,512]{3,2,1,0:T(8,128)(2,1)S(1)} %copy-done.98, bf16[32,2,128,128]{3,2,1,0:T(8,128)(2,1)S(1)} %copy-done.82), custom_call_target="tpu_custom_call" | custom-call | flops 46137344000 | bytes 4227216 | tf_op jit(solution)/shard_map/pallas_call | solution.py:51
  635.6 13.8 all-gather.23.cloned.1.call-done.refs_1_.refs_4_
  666.8 59.7 %shard_map.204 = (bf16[256,2048]{1,0:T(8,128)(2,1)S(1)}, bf16[256,2048]{1,0:T(8,128)(2,1)S(1)}, bf16[256,2048]{1,0:T(8,128)(2,1)S(1)}, bf16[256,2048]{1,0:T(8,12...) custom-call(bf16[512,2048]{1,0:T(8,128)(2,1)} %copy-done.103, bf16[512,2048]{1,0:T(8,128)(2,1)} %copy-done.104, ...), custom_call_target="tpu_custom_call" | custom-call | flops 60000002048 | bytes 11543552 | tf_op jit(solution)/shard_map/pallas_call | solution.py:51
  726.9 21.5 %shard_map.205 = (bf16[1024,1408]{1,0:T(8,128)(2,1)}, bf16[1024,1408]{1,0:T(8,128)(2,1)}, bf16[1024,1408]{1,0:T(8,128)(2,1)}) custom-call(bf16[256,2048]{1,0:T(8,128)(2,1)S(1)} %get-tuple-element.325.refs_0_, bf16[256,2048]{1,0:T(8,128)(2,1)S(1)} %get-tuple-element.326.refs_1_, bf16[256,2048]{1,0:T(8,128)(2,1)S(1)} %get-tuple-element.327.refs_2_, ...), custom_call_target="tpu_custom_call" | custom-call | flops 11811160064 | bytes 24379392 | tf_op jit(solution)/shard_map/pallas_call | solution.py:51
  748.4 12.8 shard_map.206
  773.0 11.3 shard_map.207
  788.0 14.2 shard_map.208
  802.2 11.1 shard_map.209
  813.3 11.3 shard_map.210
  831.1 20.3 %shard_map.211 = (bf16[512,2048]{1,0:T(8,128)(2,1)S(1)}, bf16[512,2048]{1,0:T(8,128)(2,1)S(1)}) custom-call(bf16[1024,1408]{1,0:T(8,128)(2,1)} %get-tuple-element.331.refs_4_.refs_0_, bf16[1024,1408]{1,0:T(8,128)(2,1)} %get-tuple-element.329.refs_4_.refs_1_, bf16[1024,1408]{1,0:T(8,128)(2,1)} %all-gather.17.cloned.1.call-done.refs_4_.refs_2_, ...), custom_call_target="tpu_custom_call" | custom-call | flops 11811160064 | bytes 21495808 | tf_op jit(solution)/shard_map/pallas_call | solution.py:51
  864.3 57.7 %shard_map.212 = (bf16[256,2048]{1,0:T(8,128)(2,1)S(1)}, bf16[256,2048]{1,0:T(8,128)(2,1)S(1)}, bf16[256,2048]{1,0:T(8,128)(2,1)S(1)}, bf16[256,2048]{1,0:T(8,12...) custom-call(bf16[512,2048]{1,0:T(8,128)(2,1)} %copy-done.109, bf16[512,2048]{1,0:T(8,128)(2,1)} %copy-done.110, ...), custom_call_target="tpu_custom_call" | custom-call | flops 7500000256 | bytes 1706112 | tf_op jit(solution)/shard_map/pallas_call | solution.py:51
  941.7 34.6 %shard_map.214 = (bf16[4,2,128,512]{3,2,1,0:T(8,128)(2,1)S(1)}, bf16[16,128,128]{2,1,0:T(8,128)(2,1)S(1)}, bf16[16,128,128]{2,1,0:T(8,128)(2,1)S(1)}) custom-call(s32[32]{0:T(128)S(1)} %fusion.41.loc_ref, s32[4]{0:T(128)S(1)} %pad_add_fusion.pos_ref, bf16[4,2,128,512]{3,2,1,0:T(8,128)(2,1)S(1)} %copy-done.99, bf16[4,2,128,512]{3,2,1,0:T(8,128)(2,1)S(1)} %bitcast.222, ...), custom_call_target="tpu_custom_call" | custom-call | flops 4823449600 | bytes 1118226 | tf_op jit(solution)/shard_map/pallas_call | solution.py:51
  985.1 34.2 %shard_map.215 = (bf16[4,2,128,512]{3,2,1,0:T(8,128)(2,1)S(1)}, bf16[16,128,128]{2,1,0:T(8,128)(2,1)S(1)}, bf16[16,128,128]{2,1,0:T(8,128)(2,1)S(1)}) custom-call(s32[32]{0:T(128)S(1)} %fusion.41.loc_ref, s32[4]{0:T(128)S(1)} %pad_add_fusion.pos_ref, bf16[4,2,128,512]{3,2,1,0:T(8,128)(2,1)S(1)} %copy-done.99, ...), custom_call_target="tpu_custom_call", output_to_operand_aliasing={{0}: (9, {})} | custom-call | flops 4823449600 | bytes 1118226 | tf_op jit(solution)/shard_map/pallas_call | solution.py:51
  1050.5 9.8 collective-permute-done.47
  1060.3 12.4 collective-permute-done.48
  1091.4 85.8 %shard_map.219 = (bf16[256,2048]{1,0:T(8,128)(2,1)S(1)}, bf16[256,2048]{1,0:T(8,128)(2,1)S(1)}, bf16[256,2048]{1,0:T(8,128)(2,1)S(1)}, bf16[256,2048]{1,0:T(8,12...) custom-call(bf16[512,2048]{1,0:T(8,128)(2,1)} %copy-done.88, bf16[512,2048]{1,0:T(8,128)(2,1)} %copy-done.89, ...), custom_call_target="tpu_custom_call" | custom-call | flops 7500000256 | bytes 1444992 | tf_op jit(solution)/shard_map/pallas_call | solution.py:51
  1190.7 11.3 shard_map.220
  1201.9 13.6 shard_map.221
  1215.6 11.1 shard_map.222
  1226.7 11.5 shard_map.223
  1238.2 20.3 %shard_map.224 = (bf16[512,2048]{1,0:T(8,128)(2,1)S(1)}, bf16[512,2048]{1,0:T(8,128)(2,1)S(1)}) custom-call(bf16[1024,1408]{1,0:T(8,128)(2,1)} %get-tuple-element.409.refs_4_.refs_0_, bf16[1024,1408]{1,0:T(8,128)(2,1)} %get-tuple-element.407.refs_4_.refs_1_, bf16[1024,1408]{1,0:T(8,128)(2,1)} %all-gather.11.cloned.1.call-done.refs_4_.refs_2_, ...), custom_call_target="tpu_custom_call" | custom-call | flops 11811160064 | bytes 21495808 | tf_op jit(solution)/shard_map/pallas_call | solution.py:51
  1271.2 57.6 %shard_map.225 = (bf16[256,2048]{1,0:T(8,128)(2,1)S(1)}, bf16[256,2048]{1,0:T(8,128)(2,1)S(1)}, bf16[256,2048]{1,0:T(8,128)(2,1)S(1)}, bf16[256,2048]{1,0:T(8,12...) custom-call(bf16[512,2048]{1,0:T(8,128)(2,1)} %copy-done.107, bf16[512,2048]{1,0:T(8,128)(2,1)} %copy-done.108, ...), custom_call_target="tpu_custom_call" | custom-call | flops 7500000256 | bytes 1706112 | tf_op jit(solution)/shard_map/pallas_call | solution.py:51
  1347.2 34.5 %shard_map.227 = (bf16[4,2,128,512]{3,2,1,0:T(8,128)(2,1)S(1)}, bf16[16,128,128]{2,1,0:T(8,128)(2,1)S(1)}, bf16[16,128,128]{2,1,0:T(8,128)(2,1)S(1)}) custom-call(s32[32]{0:T(128)S(1)} %fusion.41.loc_ref, s32[4]{0:T(128)S(1)} %pad_add_fusion.pos_ref, bf16[4,2,128,512]{3,2,1,0:T(8,128)(2,1)S(1)} %copy-done.93, bf16[4,2,128,512]{3,2,1,0:T(8,128)(2,1)S(1)} %bitcast.220, ...), custom_call_target="tpu_custom_call" | custom-call | flops 4823449600 | bytes 1118226 | tf_op jit(solution)/shard_map/pallas_call | solution.py:51
  1389.9 9.0 collective-permute-done.53
  1399.7 35.0 %shard_map.228 = (bf16[4,2,128,512]{3,2,1,0:T(8,128)(2,1)S(1)}, bf16[16,128,128]{2,1,0:T(8,128)(2,1)}, bf16[16,128,128]{2,1,0:T(8,128)(2,1)S(1)}) custom-call(s32[32]{0:T(128)S(1)} %fusion.41.loc_ref, s32[4]{0:T(128)S(1)} %pad_add_fusion.pos_ref, bf16[4,2,128,512]{3,2,1,0:T(8,128)(2,1)S(1)} %copy-done.93, ...), custom_call_target="tpu_custom_call", output_to_operand_aliasing={{0}: (9, {})} | custom-call | flops 4823449600 | bytes 1118226 | tf_op jit(solution)/shard_map/pallas_call | solution.py:51
  1485.3 9.1 shard_map.231
  1495.8 39.8 %shard_map.232 = (bf16[256,2048]{1,0:T(8,128)(2,1)S(1)}, f32[1,2048]{1,0:T(1,128)}, f32[1,2048]{1,0:T(1,128)S(1)}, bf16[4,256,640]{2,1,0:T(8,128)(2,1)S(1)}) custom-call(bf16[512,2048]{1,0:T(8,128)(2,1)S(1)} %copy-done.86, bf16[512,2048]{1,0:T(8,128)(2,1)} %copy-done.87, f32[256,2048]{1,0:T(8,128)} %get-tuple-element.474.refs_2_, f32[1,2048]{1,0:T(1,128)S(1)} %copy-done.78, ...), custom_call_target="tpu_custom_call" | custom-call | flops 7500000256 | bytes 1510528 | tf_op jit(solution)/shard_map/pallas_call | solution.py:51
  1557.7 31.2 %collective-permute-done.79 = f32[4,256]{1,0:T(4,128)S(1)} collective-permute-done((f32[4,256]{1,0:T(4,128)S(1)}, f32[4,256]{1,0:T(4,128)S(1)}, u32[]{:S(2)}, u32[]{:S(2)}) %collective-permute-start.79) | collective-permute-done | bytes 4128 | tf_op jit(solution)/shard_map/ppermute | solution.py:23
  1592.3 21.1 %collective-permute-done.80 = f32[4,256]{1,0:T(4,128)S(1)} collective-permute-done((f32[4,256]{1,0:T(4,128)S(1)}, f32[4,256]{1,0:T(4,128)S(1)}, u32[]{:S(2)}, u32[]{:S(2)}) %collective-permute-start.80) | collective-permute-done | bytes 4128 | tf_op jit(solution)/shard_map/ppermute | solution.py:23
  1626.8 29.9 %collective-permute-done.70 = bf16[256,640]{1,0:T(8,128)(2,1)S(1)} collective-permute-done((bf16[256,640]{1,0:T(8,128)(2,1)S(1)}, bf16[256,640]{1,0:T(8,128)(2,1)S(1)}, u32[]{:S(2)}, u32[]{:S(2)}) %collective-permute-start.70) | collective-permute-done | bytes 327712 | tf_op jit(solution)/shard_map/ppermute | solution.py:23
  (679 shorter events, 458.1 us)
Async XLA Ops:
  7.2 138.5 %all-gather.9.cloned.1.call-start = ((), (), s32[]{:S(2)}) async-start(), calls=%async_computation.8 | async-start | bytes 5308416 | tf_op jit(solution)/shard_map/all_gather | solution.py:1012
  31.6 187.4 %all-gather.11.cloned.1.call-start = ((), (), s32[]{:S(2)}) async-start(), calls=%async_computation.9 | async-start | bytes 3604480 | tf_op jit(solution)/shard_map/all_gather | solution.py:77
  53.0 239.4 %all-gather.13.cloned.1.call-start = ((), (), s32[]{:S(2)}) async-start(), calls=%async_computation.10 | async-start | bytes 3604480 | tf_op jit(solution)/shard_map/all_gather | solution.py:77
  125.9 228.7 %all-gather.15.cloned.1.call-start = ((), (), s32[]{:S(2)}) async-start(), calls=%async_computation.11 | async-start | bytes 3604480 | tf_op jit(solution)/shard_map/all_gather | solution.py:77
  157.0 262.6 %all-gather.17.cloned.1.call-start = ((), (), s32[]{:S(2)}) async-start(), calls=%async_computation.12 | async-start | bytes 3604480 | tf_op jit(solution)/shard_map/all_gather | solution.py:77
  219.1 303.2 %all-gather.19.cloned.1.call-start = ((), (), s32[]{:S(2)}) async-start(), calls=%async_computation.13 | async-start | bytes 5308416 | tf_op jit(solution)/shard_map/all_gather | solution.py:1012
  219.7 376.7 %all-gather.21.cloned.1.call-start = ((), (), s32[]{:S(2)}) async-start(), calls=%async_computation.14 | async-start | bytes 3604480 | tf_op jit(solution)/shard_map/all_gather | solution.py:77
  220.0 63.1 %collective-permute-start.14 = (bf16[1024,1408]{1,0:T(8,128)(2,1)}, bf16[1024,1408]{1,0:T(8,128)(2,1)S(1)}, u32[]{:S(2)}, u32[]{:S(2)}) collective-permute-start(bf16[1024,1408]{1,0:T(8,128)(2,1)} %all-gather.11.cloned.1.call-done.refs_4_.refs_2_), channel_id=1, source_target_pairs={{0,2},{2,0},{4,6},{6,4},{8,10},{10,8},{12,14},{14,12},{1,3},{3,1},... | collective-permute-start | bytes 8650760 | tf_op jit(solution)/shard_map/ppermute | solution.py:23
  292.4 62.2 %collective-permute-start.17 = (bf16[1024,1408]{1,0:T(8,128)(2,1)}, bf16[1024,1408]{1,0:T(8,128)(2,1)}, u32[]{:S(2)}, u32[]{:S(2)}) collective-permute-start(bf16[1024,1408]{1,0:T(8,128)(2,1)} %all-gather.13.cloned.1.call-done.refs_6_.refs_4_), channel_id=1, source_target_pairs={{0,2},{2,0},{4,6},{6,4},{8,10},{10,8},{12,14},{14,12},{1,3},{3,1},... | collective-permute-start | bytes 8650760 | tf_op jit(solution)/shard_map/ppermute | solution.py:23
  354.6 78.8 %collective-permute-start.20 = (bf16[1024,1408]{1,0:T(8,128)(2,1)}, bf16[1024,1408]{1,0:T(8,128)(2,1)}, u32[]{:S(2)}, u32[]{:S(2)}) collective-permute-start(bf16[1024,1408]{1,0:T(8,128)(2,1)} %all-gather.15.cloned.1.call-done.refs_1_.refs_4_), channel_id=1, source_target_pairs={{0,2},{2,0},{4,6},{6,4},{8,10},{10,8},{12,14},{14,12},{1,3},{3,1},... | collective-permute-start | bytes 8650760 | tf_op jit(solution)/shard_map/ppermute | solution.py:23
  361.1 288.3 %all-gather.23.cloned.1.call-start = ((), (), s32[]{:S(2)}) async-start(), calls=%async_computation.15 | async-start | bytes 3604480 | tf_op jit(solution)/shard_map/all_gather | solution.py:77
  433.5 88.9 %collective-permute-start.21 = (bf16[1024,1408]{1,0:T(8,128)(2,1)}, bf16[1024,1408]{1,0:T(8,128)(2,1)}, u32[]{:S(2)}, u32[]{:S(2)}) collective-permute-start(bf16[1024,1408]{1,0:T(8,128)(2,1)} %all-gather.17.cloned.1.call-done.refs_4_.refs_2_), channel_id=1, source_target_pairs={{0,2},{2,0},{4,6},{6,4},{8,10},{10,8},{12,14},{14,12},{1,3},{3,1},... | collective-permute-start | bytes 8650760 | tf_op jit(solution)/shard_map/ppermute | solution.py:23
  538.1 49.8 %collective-permute-start.25 = (bf16[4,2,128,128]{3,2,1,0:T(8,128)(2,1)}, bf16[4,2,128,128]{3,2,1,0:T(8,128)(2,1)}, u32[]{:S(2)}, u32[]{:S(2)}) collective-permute-start(bf16[4,2,128,128]{3,2,1,0:T(8,128)(2,1)} %get-tuple-element.286), channel_id=1, source_target_pairs={{0,8},{2,10},{4,12},{6,14},{8,0},{10,2},{12,4},{14,6},{1,9},{3,11}... | collective-permute-start | bytes 786440 | tf_op jit(solution)/shard_map/ppermute | solution.py:23
  539.7 48.3 %collective-permute-start.22 = (bf16[4,2,128,128]{3,2,1,0:T(8,128)(2,1)}, bf16[4,2,128,128]{3,2,1,0:T(8,128)(2,1)}, u32[]{:S(2)}, u32[]{:S(2)}) collective-permute-start(bf16[4,2,128,128]{3,2,1,0:T(8,128)(2,1)} %get-tuple-element.286), channel_id=1, source_target_pairs={{0,2},{2,0},{4,6},{6,4},{8,10},{10,8},{12,14},{14,12},{1,3},{3,1},... | collective-permute-start | bytes 786440 | tf_op jit(solution)/shard_map/ppermute | solution.py:23
  540.2 387.1 %reduce-scatter.9.cloned.1.call-start = ((), (), s32[]{:S(2)}) async-start(), calls=%async_computation.16 | async-start | bytes 3604480 | tf_op jit(solution)/shard_map/reduce_scatter | solution.py:81
  596.4 61.4 %collective-permute-start.29 = (bf16[1024,1408]{1,0:T(8,128)(2,1)}, bf16[1024,1408]{1,0:T(8,128)(2,1)}, u32[]{:S(2)}, u32[]{:S(2)}) collective-permute-start(bf16[1024,1408]{1,0:T(8,128)(2,1)} %all-gather.21.cloned.1.call-done.refs_6_.refs_4_), channel_id=1, source_target_pairs={{0,2},{2,0},{4,6},{6,4},{8,10},{10,8},{12,14},{14,12},{1,3},{3,1},... | collective-permute-start | bytes 8650760 | tf_op jit(solution)/shard_map/ppermute | solution.py:23
  666.8 60.1 %collective-permute-start.30 = (bf16[1024,1408]{1,0:T(8,128)(2,1)S(1)}, bf16[1024,1408]{1,0:T(8,128)(2,1)S(1)}, u32[]{:S(2)}, u32[]{:S(2)}) collective-permute-start(bf16[1024,1408]{1,0:T(8,128)(2,1)S(1)} %copy-done.128), channel_id=1, source_target_pairs={{0,2},{2,0},{4,6},{6,4},{8,10},{10,8},{12,14},{14,12},{1,3},{3,1},... | collective-permute-start | bytes 8650760 | tf_op jit(solution)/shard_map/ppermute | solution.py:23
  766.6 58.0 %collective-permute-start.36 = (bf16[2,128,2048]{2,1,0:T(8,128)(2,1)S(1)}, bf16[2,128,2048]{2,1,0:T(8,128)(2,1)}, u32[]{:S(2)}, u32[]{:S(2)}) collective-permute-start(bf16[2,128,2048]{2,1,0:T(8,128)(2,1)S(1)} %bitcast.229), channel_id=1, source_target_pairs={{16,0},{17,15},{18,2},{19,13},{20,4},{21,11},{22,6},{23,9},{24,8},... | collective-permute-start | bytes 3145736 | tf_op jit(solution)/shard_map/ppermute | solution.py:116
  767.8 56.8 %collective-permute-start.35 = (bf16[2,128,2048]{2,1,0:T(8,128)(2,1)S(1)}, bf16[2,128,2048]{2,1,0:T(8,128)(2,1)}, u32[]{:S(2)}, u32[]{:S(2)}) collective-permute-start(bf16[2,128,2048]{2,1,0:T(8,128)(2,1)S(1)} %bitcast.230), channel_id=1, source_target_pairs={{0,0},{1,15},{2,2},{3,13},{4,4},{5,11},{6,6},{7,9},{8,8},{9,7},{10... | collective-permute-start | bytes 3145736 | tf_op jit(solution)/shard_map/ppermute | solution.py:116
  784.3 74.8 %collective-permute-start.37 = (bf16[4,256,1408]{2,1,0:T(8,128)(2,1)}, bf16[4,256,1408]{2,1,0:T(8,128)(2,1)}, u32[]{:S(2)}, u32[]{:S(2)}) collective-permute-start(bf16[4,256,1408]{2,1,0:T(8,128)(2,1)} %get-tuple-element.310), channel_id=1, source_target_pairs={{0,2},{2,0},{4,6},{6,4},{8,10},{10,8},{12,14},{14,12},{1,3},{3,1},... | collective-permute-start | bytes 8650760 | tf_op jit(solution)/shard_map/ppermute | solution.py:23
  786.0 41.9 %collective-permute-start.34 = (bf16[256,2048]{1,0:T(8,128)(2,1)S(1)}, bf16[256,2048]{1,0:T(8,128)(2,1)}, u32[]{:S(2)}, u32[]{:S(2)}) collective-permute-start(bf16[256,2048]{1,0:T(8,128)(2,1)S(1)} %add_convert_fusion.10), channel_id=1, source_target_pairs={{0,16},{16,0},{1,17},{17,1},{2,18},{18,2},{3,19},{19,3},{4,20},{20... | collective-permute-start | bytes 3145736 | tf_op jit(solution)/shard_map/ppermute | solution.py:23
  863.2 159.7 %reduce-scatter.11.cloned.1.call-start = ((), (), s32[]{:S(2)}) async-start(), calls=%async_computation.17 | async-start | bytes 3604480 | tf_op jit(solution)/shard_map/reduce_scatter | solution.py:81
  863.3 64.0 %collective-permute-start.38 = (bf16[4,256,1408]{2,1,0:T(8,128)(2,1)}, bf16[4,256,1408]{2,1,0:T(8,128)(2,1)}, u32[]{:S(2)}, u32[]{:S(2)}) collective-permute-start(bf16[4,256,1408]{2,1,0:T(8,128)(2,1)} %get-tuple-element.340), channel_id=1, source_target_pairs={{0,2},{2,0},{4,6},{6,4},{8,10},{10,8},{12,14},{14,12},{1,3},{3,1},... | collective-permute-start | bytes 8650760 | tf_op jit(solution)/shard_map/ppermute | solution.py:23
  932.2 249.0 %reduce-scatter.13.cloned.1.call-start = ((), (), s32[]{:S(2)}) async-start(), calls=%async_computation.18 | async-start | bytes 3604480 | tf_op jit(solution)/shard_map/reduce_scatter | solution.py:81
  932.2 90.7 %collective-permute-start.39 = (bf16[4,256,1408]{2,1,0:T(8,128)(2,1)}, bf16[4,256,1408]{2,1,0:T(8,128)(2,1)}, u32[]{:S(2)}, u32[]{:S(2)}) collective-permute-start(bf16[4,256,1408]{2,1,0:T(8,128)(2,1)} %get-tuple-element.345), channel_id=1, source_target_pairs={{0,2},{2,0},{4,6},{6,4},{8,10},{10,8},{12,14},{14,12},{1,3},{3,1},... | collective-permute-start | bytes 8650760 | tf_op jit(solution)/shard_map/ppermute | solution.py:23
  976.3 45.8 %collective-permute-start.40 = (bf16[4,4,128,128]{3,2,1,0:T(8,128)(2,1)S(1)}, bf16[4,4,128,128]{3,2,1,0:T(8,128)(2,1)S(1)}, u32[]{:S(2)}, u32[]{:S(2)}) collective-permute-start(bf16[4,4,128,128]{3,2,1,0:T(8,128)(2,1)S(1)} %bitcast.235), channel_id=1, source_target_pairs={{0,2},{2,0},{4,6},{6,4},{8,10},{10,8},{12,14},{14,12},{1,3},{3,1},... | collective-permute-start | bytes 1572872 | tf_op jit(solution)/shard_map/ppermute | solution.py:23
  977.6 58.4 %collective-permute-start.42 = (bf16[2,128,2048]{2,1,0:T(8,128)(2,1)}, bf16[2,128,2048]{2,1,0:T(8,128)(2,1)}, u32[]{:S(2)}, u32[]{:S(2)}) collective-permute-start(bf16[2,128,2048]{2,1,0:T(8,128)(2,1)} %bitcast.38), channel_id=1, source_target_pairs={{16,16},{17,31},{18,18},{19,29},{20,20},{21,27},{22,22},{23,25},{2... | collective-permute-start | bytes 3145736 | tf_op jit(solution)/shard_map/ppermute | solution.py:116
  979.2 58.0 %collective-permute-start.41 = (bf16[2,128,2048]{2,1,0:T(8,128)(2,1)}, bf16[2,128,2048]{2,1,0:T(8,128)(2,1)}, u32[]{:S(2)}, u32[]{:S(2)}) collective-permute-start(bf16[2,128,2048]{2,1,0:T(8,128)(2,1)} %bitcast.38), channel_id=1, source_target_pairs={{0,16},{1,31},{2,18},{3,29},{4,20},{5,27},{6,22},{7,25},{8,24},{9,... | collective-permute-start | bytes 3145736 | tf_op jit(solution)/shard_map/ppermute | solution.py:116
  1030.4 238.1 %reduce-scatter.15.cloned.1.call-start = ((), (), s32[]{:S(2)}) async-start(), calls=%async_computation.19 | async-start | bytes 2949120 | tf_op jit(solution)/shard_map/reduce_scatter | solution.py:81
  1090.3 90.8 %collective-permute-start.50 = (bf16[4,256,1152]{2,1,0:T(8,128)(2,1)S(1)}, bf16[4,256,1152]{2,1,0:T(8,128)(2,1)}, u32[]{:S(2)}, u32[]{:S(2)}) collective-permute-start(bf16[4,256,1152]{2,1,0:T(8,128)(2,1)S(1)} %pad_maximum_fusion), channel_id=1, source_target_pairs={{0,2},{2,0},{4,6},{6,4},{8,10},{10,8},{12,14},{14,12},{1,3},{3,1},... | collective-permute-start | bytes 7077896 | tf_op jit(solution)/shard_map/ppermute | solution.py:23
  1185.5 146.3 %reduce-scatter.17.cloned.1.call-start = ((), (), s32[]{:S(2)}) async-start(), calls=%async_computation.20 | async-start | bytes 3604480 | tf_op jit(solution)/shard_map/reduce_scatter | solution.py:81
  1201.9 64.1 %collective-permute-start.51 = (bf16[4,256,1408]{2,1,0:T(8,128)(2,1)}, bf16[4,256,1408]{2,1,0:T(8,128)(2,1)S(1)}, u32[]{:S(2)}, u32[]{:S(2)}) collective-permute-start(bf16[4,256,1408]{2,1,0:T(8,128)(2,1)} %get-tuple-element.394), channel_id=1, source_target_pairs={{0,2},{2,0},{4,6},{6,4},{8,10},{10,8},{12,14},{14,12},{1,3},{3,1},... | collective-permute-start | bytes 8650760 | tf_op jit(solution)/shard_map/ppermute | solution.py:23
  1268.4 170.3 %reduce-scatter.19.cloned.1.call-start = ((), (), s32[]{:S(2)}) async-start(), calls=%async_computation.21 | async-start | bytes 3604480 | tf_op jit(solution)/shard_map/reduce_scatter | solution.py:81
  1268.4 63.4 %collective-permute-start.52 = (bf16[4,256,1408]{2,1,0:T(8,128)(2,1)}, bf16[4,256,1408]{2,1,0:T(8,128)(2,1)}, u32[]{:S(2)}, u32[]{:S(2)}) collective-permute-start(bf16[4,256,1408]{2,1,0:T(8,128)(2,1)} %get-tuple-element.421), channel_id=1, source_target_pairs={{0,2},{2,0},{4,6},{6,4},{8,10},{10,8},{12,14},{14,12},{1,3},{3,1},... | collective-permute-start | bytes 8650760 | tf_op jit(solution)/shard_map/ppermute | solution.py:23
  1336.8 331.3 %reduce-scatter.21.cloned.1.call-start = ((), (), s32[]{:S(2)}) async-start(), calls=%async_computation.22 | async-start | bytes 1310720 | tf_op jit(solution)/shard_map/reduce_scatter | solution.py:81
  1336.8 101.9 %collective-permute-start.54 = (bf16[4,256,1408]{2,1,0:T(8,128)(2,1)}, bf16[4,256,1408]{2,1,0:T(8,128)(2,1)}, u32[]{:S(2)}, u32[]{:S(2)}) collective-permute-start(bf16[4,256,1408]{2,1,0:T(8,128)(2,1)} %get-tuple-element.436), channel_id=1, source_target_pairs={{0,2},{2,0},{4,6},{6,4},{8,10},{10,8},{12,14},{14,12},{1,3},{3,1},... | collective-permute-start | bytes 8650760 | tf_op jit(solution)/shard_map/ppermute | solution.py:23
  1343.6 44.9 %collective-permute-start.63 = (bf16[256,1152]{1,0:T(8,128)(2,1)S(1)}, bf16[256,1152]{1,0:T(8,128)(2,1)S(1)}, u32[]{:S(2)}, u32[]{:S(2)}) collective-permute-start(bf16[256,1152]{1,0:T(8,128)(2,1)S(1)} %copy-done.152), channel_id=1, source_target_pairs={{0,16},{1,17},{2,18},{3,19},{4,20},{5,21},{6,22},{7,23},{8,24},{9,... | collective-permute-start | bytes 1769480 | tf_op jit(solution)/shard_map/ppermute | solution.py:27
  1383.1 53.5 %collective-permute-start.64 = (bf16[256,1408]{1,0:T(8,128)(2,1)S(1)}, bf16[256,1408]{1,0:T(8,128)(2,1)S(1)}, u32[]{:S(2)}, u32[]{:S(2)}) collective-permute-start(bf16[256,1408]{1,0:T(8,128)(2,1)S(1)} %copy-done.143), channel_id=1, source_target_pairs={{0,16},{1,17},{2,18},{3,19},{4,20},{5,21},{6,22},{7,23},{8,24},{9,... | collective-permute-start | bytes 2162696 | tf_op jit(solution)/shard_map/ppermute | solution.py:27
  1387.1 49.4 %collective-permute-start.65 = (bf16[256,1408]{1,0:T(8,128)(2,1)S(1)}, bf16[256,1408]{1,0:T(8,128)(2,1)S(1)}, u32[]{:S(2)}, u32[]{:S(2)}) collective-permute-start(bf16[256,1408]{1,0:T(8,128)(2,1)S(1)} %copy-done.145), channel_id=1, source_target_pairs={{0,16},{1,17},{2,18},{3,19},{4,20},{5,21},{6,22},{7,23},{8,24},{9,... | collective-permute-start | bytes 2162696 | tf_op jit(solution)/shard_map/ppermute | solution.py:27
  1388.5 48.0 %collective-permute-start.66 = (bf16[256,1408]{1,0:T(8,128)(2,1)S(1)}, bf16[256,1408]{1,0:T(8,128)(2,1)S(1)}, u32[]{:S(2)}, u32[]{:S(2)}) collective-permute-start(bf16[256,1408]{1,0:T(8,128)(2,1)S(1)} %copy-done.135), channel_id=1, source_target_pairs={{0,16},{1,17},{2,18},{3,19},{4,20},{5,21},{6,22},{7,23},{8,24},{9,... | collective-permute-start | bytes 2162696 | tf_op jit(solution)/shard_map/ppermute | solution.py:27
  1398.8 37.8 %collective-permute-start.55 = (bf16[4,4,128,128]{3,2,1,0:T(8,128)(2,1)S(1)}, bf16[4,4,128,128]{3,2,1,0:T(8,128)(2,1)S(1)}, u32[]{:S(2)}, u32[]{:S(2)}) collective-permute-start(bf16[4,4,128,128]{3,2,1,0:T(8,128)(2,1)S(1)} %bitcast.234), channel_id=1, source_target_pairs={{0,2},{2,0},{4,6},{6,4},{8,10},{10,8},{12,14},{14,12},{1,3},{3,1},... | collective-permute-start | bytes 1572872 | tf_op jit(solution)/shard_map/ppermute | solution.py:23
  1482.5 186.9 %reduce-scatter.23.cloned.1.call-start = ((), (), s32[]{:S(2)}) async-start(), calls=%async_computation.23 | async-start | bytes 3604480 | tf_op jit(solution)/shard_map/reduce_scatter | solution.py:81
  1542.7 115.2 %collective-permute-start.75 = (bf16[2,128,2048]{2,1,0:T(8,128)(2,1)S(1)}, bf16[2,128,2048]{2,1,0:T(8,128)(2,1)}, u32[]{:S(2)}, u32[]{:S(2)}) collective-permute-start(bf16[2,128,2048]{2,1,0:T(8,128)(2,1)S(1)} %bitcast.210), channel_id=1, source_target_pairs={{16,16},{17,31},{18,18},{19,29},{20,20},{21,27},{22,22},{23,25},{2... | collective-permute-start | bytes 3145736 | tf_op jit(solution)/shard_map/ppermute | solution.py:116
  1544.3 113.6 %collective-permute-start.74 = (bf16[2,128,2048]{2,1,0:T(8,128)(2,1)S(1)}, bf16[2,128,2048]{2,1,0:T(8,128)(2,1)}, u32[]{:S(2)}, u32[]{:S(2)}) collective-permute-start(bf16[2,128,2048]{2,1,0:T(8,128)(2,1)S(1)} %bitcast.211), channel_id=1, source_target_pairs={{0,16},{1,31},{2,18},{3,29},{4,20},{5,27},{6,22},{7,25},{8,24},{9,... | collective-permute-start | bytes 3145736 | tf_op jit(solution)/shard_map/ppermute | solution.py:116
  1554.8 58.5 %collective-permute-start.80 = (f32[4,256]{1,0:T(4,128)S(1)}, f32[4,256]{1,0:T(4,128)S(1)}, u32[]{:S(2)}, u32[]{:S(2)}) collective-permute-start(f32[4,256]{1,0:T(4,128)S(1)} %bitcast.251), channel_id=1, source_target_pairs={{0,8},{2,10},{4,12},{6,14},{8,0},{10,2},{12,4},{14,6},{1,9},{3,11}... | collective-permute-start | bytes 12296 | tf_op jit(solution)/shard_map/ppermute | solution.py:23
  1557.7 63.3 %collective-permute-start.69 = (bf16[256,640]{1,0:T(8,128)(2,1)}, bf16[256,640]{1,0:T(8,128)(2,1)S(1)}, u32[]{:S(2)}, u32[]{:S(2)}) collective-permute-start(bf16[256,640]{1,0:T(8,128)(2,1)} %get-tuple-element.533), channel_id=1, source_target_pairs={{0,4},{2,6},{4,0},{6,2},{8,12},{10,14},{12,8},{14,10},{1,5},{3,7},... | collective-permute-start | bytes 983048 | tf_op jit(solution)/shard_map/ppermute | solution.py:23
  1619.7 39.9 %collective-permute-start.73 = (bf16[2,128,2048]{2,1,0:T(8,128)(2,1)S(1)}, bf16[2,128,2048]{2,1,0:T(8,128)(2,1)S(1)}, u32[]{:S(2)}, u32[]{:S(2)}) collective-permute-start(bf16[2,128,2048]{2,1,0:T(8,128)(2,1)S(1)} %bitcast.231), channel_id=1, source_target_pairs={{16,0},{17,15},{18,2},{19,13},{20,4},{21,11},{22,6},{23,9},{24,8},... | collective-permute-start | bytes 3145736 | tf_op jit(solution)/shard_map/ppermute | solution.py:116
  1621.0 38.6 %collective-permute-start.72 = (bf16[2,128,2048]{2,1,0:T(8,128)(2,1)S(1)}, bf16[2,128,2048]{2,1,0:T(8,128)(2,1)S(1)}, u32[]{:S(2)}, u32[]{:S(2)}) collective-permute-start(bf16[2,128,2048]{2,1,0:T(8,128)(2,1)S(1)} %bitcast.232), channel_id=1, source_target_pairs={{0,0},{1,15},{2,2},{3,13},{4,4},{5,11},{6,6},{7,9},{8,8},{9,7},{10... | collective-permute-start | bytes 3145736 | tf_op jit(solution)/shard_map/ppermute | solution.py:116
  (224 other events, 2461.4 us)
Sparse Core Ops, SparseCore 0:
  31.8 97.0 all-gather.8
  130.9 66.5 all-gather.10
  199.1 65.3 all-gather.12
  265.9 57.8 all-gather.14
  325.2 74.2 all-gather.16
  401.6 106.8 all-gather.18
  510.1 79.8 all-gather.20
  591.5 57.8 all-gather.22
  863.4 52.3 reduce-scatter.8
  932.3 53.2 reduce-scatter.10
  1030.6 71.9 reduce-scatter.12
  1185.6 45.5 reduce-scatter.14
  1268.5 54.6 reduce-scatter.16
  1336.9 55.6 reduce-scatter.18
  1482.7 33.4 reduce-scatter.20
  1519.0 76.1 reduce-scatter.22

commit v4 on v3

--- a/solution.py
+++ b/solution.py
@@ -1250,6 +1250,7 @@
     gain_total = gain_total + partner(gain_total, "section", 1)
     gain_total = gain_total.reshape(4, count // 2, 2, s.depth)
     gain_total = gain_total[:, :, side()] + partner(gain_total[:, :, 1 - side()], "wide", 1)
+    gain_total = after(gain_total, *given)
     total = gain_total[:, wide // 2]
     for j in range(1, count // 2):
         total = total + partner(gain_total[:, (wide // 2) ^ j], "wide", 2 * j)

time: 1710 us -> 1720 us (level)
  starting transfers between devices: 129 us -> 162 us
  waiting for transfers between devices: 401 us -> 378 us
    ppermute x66, starting transfers between devices: 76.2 us -> 108 us  [partner(): return lax.ppermute(x, axis, [(i, i ^ bit) for i in range(peers)])]
    ppermute x66, waiting for transfers between devices: 329 us -> 305 us  [partner(): return lax.ppermute(x, axis, [(i, i ^ bit) for i in range(peers)])]
    unnamed x362 -> x346, local copies, waits for them, and re-layouts: 96.5 us -> 97.4 us
  transfers between devices with their start and end apart: 101 -> 101, of which waited for: 40 -> 43; matrix products, arithmetic and copies ran while one was open for 5% -> 5% of each run, Pallas kernels for 51% -> 51%
where the time goes in v4:
time: 1720 us; the launch traced here: 1710 us
  Pallas kernels  911 us (53%)
  waiting for transfers between devices  378 us (22%)
  starting transfers between devices  162 us (9%)
  local copies, waits for them, and re-layouts  121 us (7%)
  other arithmetic  95.5 us (6%)
  blocking collectives  26 us (2%)
    pallas_call x39, Pallas kernels, call(): pl.pallas_call(body, out_shape=outs, scratch_shapes=scratch, compiler_par...  911 us
    ppermute x66, waiting for transfers between devices, partner(): return lax.ppermute(x, axis, [(i, i ^ bit) for i in range(peers)])  305 us
    ppermute x66, starting transfers between devices, partner(): return lax.ppermute(x, axis, [(i, i ^ bit) for i in range(peers)])  108 us
    unnamed x346, local copies, waits for them, and re-layouts  97.4 us
    ppermute x10, starting transfers between devices, mirror(): return lax.ppermute(x, ('section', 'wide', 'tp'), pairs)  36.7 us
  transfers between devices with their start and end apart: 101, of which 43 were waited for; matrix products, arithmetic and copies ran while one was open for 5% of the time, Pallas kernels for 51%

profile of v4, /device:TPU:1, one launch (start us, length us, event | category | flops | bytes accessed | tf_op | source)
XLA Modules:
  0.0 1710.3 jit_solution(5745006950409951923)
XLA Ops:
  17.2 12.2 collective-permute-done.5
  35.0 15.6 collective-permute-done.13
  59.0 26.0 %all_gather.27 = bf16[2,2048]{1,0:T(2,128)(2,1)S(1)} all-gather(bf16[2,256]{1,0:T(2,128)(2,1)S(1)} %pad_maximum_fusion.12), channel_id=1, replica_groups=mesh['section'=2,'wide'=8,'tp'=2] {'wide'}, dimensions={1}, use_global_device_ids=true | all-gather | bytes 9216 | tf_op jit(solution)/shard_map/all_gather | solution.py:999
  92.1 20.2 %collective-permute-done.2.refs_1_ = bf16[256,2048]{1,0:T(8,128)(2,1)S(1)} collective-permute-done((bf16[256,2048]{1,0:T(8,128)(2,1)S(1)}, bf16[256,2048]{1,0:T(8,128)(2,1)S(1)}, u32[]{:S(2)}, u32[]{:S(2)}) %collective-permute-start.2) | collective-permute-done | bytes 1048608 | tf_op jit(solution)/shard_map/ppermute | solution.py:23
  113.8 10.8 collective-permute-done.16
  157.0 16.7 collective-permute-start.7
  176.0 18.4 %collective-permute-done.7 = bf16[4,2,128,128]{3,2,1,0:T(8,128)(2,1)S(1)} collective-permute-done((bf16[4,2,128,128]{3,2,1,0:T(8,128)(2,1)}, bf16[4,2,128,128]{3,2,1,0:T(8,128)(2,1)S(1)}, u32[]{:S(2)}, u32[]{:S(2)}) %collective-permute-start.7) | collective-permute-done | bytes 262176 | tf_op jit(solution)/shard_map/ppermute | solution.py:23
  199.7 10.4 collective-permute-done.9
  223.9 35.3 %shard_map.195 = (bf16[4,2,128,512]{3,2,1,0:T(8,128)(2,1)S(1)}, f32[4,2,1,1024]{3,2,1,0:T(1,128)S(1)}) custom-call(s32[32]{0:T(128)S(1)} %fusion.41.loc_ref, s32[4]{0:T(128)S(1)} %pad_add_fusion.pos_ref, bf16[4,2,128,512]{3,2,1,0:T(8,128)(2,1)S(1)} %copy-done.92, bf16[32,2,128,128]{3,2,1,0:T(8,128)(2,1)S(1)} %copy-done.80), custom_call_target="tpu_custom_call" | custom-call | flops 46137344000 | bytes 4227216 | tf_op jit(solution)/shard_map/pallas_call | solution.py:51
  259.2 23.9 %collective-permute-done.14.refs_5_.refs_3_ = bf16[1024,1408]{1,0:T(8,128)(2,1)S(1)} collective-permute-done((bf16[1024,1408]{1,0:T(8,128)(2,1)}, bf16[1024,1408]{1,0:T(8,128)(2,1)S(1)}, u32[]{:S(2)}, u32[]{:S(2)}) %collective-permute-start.14) | collective-permute-done | bytes 2883616 | tf_op jit(solution)/shard_map/ppermute | solution.py:23
  293.4 58.6 %shard_map.197 = (bf16[256,2048]{1,0:T(8,128)(2,1)S(1)}, bf16[256,2048]{1,0:T(8,128)(2,1)S(1)}, bf16[256,2048]{1,0:T(8,128)(2,1)S(1)}, bf16[256,2048]{1,0:T(8,12...) custom-call(bf16[512,2048]{1,0:T(8,128)(2,1)} %copy-done.101, bf16[512,2048]{1,0:T(8,128)(2,1)} %copy-done.102, ...), custom_call_target="tpu_custom_call" | custom-call | flops 60000002048 | bytes 12592128 | tf_op jit(solution)/shard_map/pallas_call | solution.py:51
  361.1 34.3 %collective-permute-done.15 = bf16[2,128,2048]{2,1,0:T(8,128)(2,1)} collective-permute-done((bf16[2,128,2048]{2,1,0:T(8,128)(2,1)}, bf16[2,128,2048]{2,1,0:T(8,128)(2,1)}, u32[]{:S(2)}, u32[]{:S(2)}) %collective-permute-start.15) | collective-permute-done | bytes 1048608 | tf_op jit(solution)/shard_map/ppermute | solution.py:116
  399.0 20.4 %shard_map.198 = (bf16[1024,1408]{1,0:T(8,128)(2,1)}, bf16[1024,1408]{1,0:T(8,128)(2,1)}, bf16[1024,1408]{1,0:T(8,128)(2,1)}) custom-call(bf16[256,2048]{1,0:T(8,128)(2,1)S(1)} %get-tuple-element.404.refs_0_, bf16[256,2048]{1,0:T(8,128)(2,1)S(1)} %get-tuple-element.405.refs_1_, bf16[256,2048]{1,0:T(8,128)(2,1)S(1)} %copy-done.3, ...), custom_call_target="tpu_custom_call" | custom-call | flops 11811160064 | bytes 24379392 | tf_op jit(solution)/shard_map/pallas_call | solution.py:51
  419.5 14.1 collective-permute-done.20.refs_2_.refs_5_
  434.3 20.2 %shard_map.199 = (bf16[512,2048]{1,0:T(8,128)(2,1)S(1)}, bf16[512,2048]{1,0:T(8,128)(2,1)S(1)}) custom-call(bf16[1024,1408]{1,0:T(8,128)(2,1)} %get-tuple-element.273.refs_0_.refs_4_, bf16[1024,1408]{1,0:T(8,128)(2,1)} %all-gather.15.cloned.1.call-done.refs_1_.refs_4_, bf16[1024,1408]{1,0:T(8,128)(2,1)} %collective-permute-done.20.refs_2_.refs_5_), custom_call_target="tpu_custom_call" | custom-call | flops 5905580032 | bytes 12845056 | tf_op jit(solution)/shard_map/pallas_call | solution.py:51
  457.2 59.6 %shard_map.200 = (bf16[256,2048]{1,0:T(8,128)(2,1)S(1)}, bf16[256,2048]{1,0:T(8,128)(2,1)S(1)}, bf16[256,2048]{1,0:T(8,128)(2,1)S(1)}, bf16[256,2048]{1,0:T(8,12...) custom-call(bf16[512,2048]{1,0:T(8,128)(2,1)} %copy-done.105, bf16[512,2048]{1,0:T(8,128)(2,1)} %copy-done.106, ...), custom_call_target="tpu_custom_call" | custom-call | flops 60000002048 | bytes 11543552 | tf_op jit(solution)/shard_map/pallas_call | solution.py:51
  540.3 22.4 %collective-permute-done.23 = bf16[4,2,128,128]{3,2,1,0:T(8,128)(2,1)} collective-permute-done((bf16[4,2,128,128]{3,2,1,0:T(8,128)(2,1)}, bf16[4,2,128,128]{3,2,1,0:T(8,128)(2,1)}, u32[]{:S(2)}, u32[]{:S(2)}) %collective-permute-start.23) | collective-permute-done | bytes 262176 | tf_op jit(solution)/shard_map/ppermute | solution.py:23
  565.3 22.7 %collective-permute-done.25 = bf16[4,2,128,128]{3,2,1,0:T(8,128)(2,1)} collective-permute-done((bf16[4,2,128,128]{3,2,1,0:T(8,128)(2,1)}, bf16[4,2,128,128]{3,2,1,0:T(8,128)(2,1)}, u32[]{:S(2)}, u32[]{:S(2)}) %collective-permute-start.25) | collective-permute-done | bytes 262176 | tf_op jit(solution)/shard_map/ppermute | solution.py:23
  599.5 35.3 %shard_map.202 = (bf16[4,2,128,512]{3,2,1,0:T(8,128)(2,1)S(1)}, f32[4,2,1,1024]{3,2,1,0:T(1,128)S(1)}) custom-call(s32[32]{0:T(128)S(1)} %fusion.41.loc_ref, s32[4]{0:T(128)S(1)} %pad_add_fusion.pos_ref, bf16[4,2,128,512]{3,2,1,0:T(8,128)(2,1)S(1)} %copy-done.98, bf16[32,2,128,128]{3,2,1,0:T(8,128)(2,1)S(1)} %copy-done.82), custom_call_target="tpu_custom_call" | custom-call | flops 46137344000 | bytes 4227216 | tf_op jit(solution)/shard_map/pallas_call | solution.py:51
  635.8 13.5 all-gather.23.cloned.1.call-done.refs_1_.refs_4_
  667.1 59.6 %shard_map.204 = (bf16[256,2048]{1,0:T(8,128)(2,1)S(1)}, bf16[256,2048]{1,0:T(8,128)(2,1)S(1)}, bf16[256,2048]{1,0:T(8,128)(2,1)S(1)}, bf16[256,2048]{1,0:T(8,12...) custom-call(bf16[512,2048]{1,0:T(8,128)(2,1)} %copy-done.103, bf16[512,2048]{1,0:T(8,128)(2,1)} %copy-done.104, ...), custom_call_target="tpu_custom_call" | custom-call | flops 60000002048 | bytes 11543552 | tf_op jit(solution)/shard_map/pallas_call | solution.py:51
  727.3 21.4 %shard_map.205 = (bf16[1024,1408]{1,0:T(8,128)(2,1)}, bf16[1024,1408]{1,0:T(8,128)(2,1)}, bf16[1024,1408]{1,0:T(8,128)(2,1)}) custom-call(bf16[256,2048]{1,0:T(8,128)(2,1)S(1)} %get-tuple-element.326.refs_0_, bf16[256,2048]{1,0:T(8,128)(2,1)S(1)} %get-tuple-element.327.refs_1_, bf16[256,2048]{1,0:T(8,128)(2,1)S(1)} %get-tuple-element.328.refs_2_, ...), custom_call_target="tpu_custom_call" | custom-call | flops 11811160064 | bytes 24379392 | tf_op jit(solution)/shard_map/pallas_call | solution.py:51
  748.7 12.8 shard_map.206
  773.3 11.3 shard_map.207
  788.1 14.3 shard_map.208
  802.4 11.1 shard_map.209
  813.5 11.3 shard_map.210
  831.4 20.3 %shard_map.211 = (bf16[512,2048]{1,0:T(8,128)(2,1)S(1)}, bf16[512,2048]{1,0:T(8,128)(2,1)S(1)}) custom-call(bf16[1024,1408]{1,0:T(8,128)(2,1)} %get-tuple-element.332.refs_4_.refs_0_, bf16[1024,1408]{1,0:T(8,128)(2,1)} %get-tuple-element.330.refs_4_.refs_1_, bf16[1024,1408]{1,0:T(8,128)(2,1)} %all-gather.17.cloned.1.call-done.refs_4_.refs_2_, ...), custom_call_target="tpu_custom_call" | custom-call | flops 11811160064 | bytes 21495808 | tf_op jit(solution)/shard_map/pallas_call | solution.py:51
  864.5 57.6 %shard_map.212 = (bf16[256,2048]{1,0:T(8,128)(2,1)S(1)}, bf16[256,2048]{1,0:T(8,128)(2,1)S(1)}, bf16[256,2048]{1,0:T(8,128)(2,1)S(1)}, bf16[256,2048]{1,0:T(8,12...) custom-call(bf16[512,2048]{1,0:T(8,128)(2,1)} %copy-done.109, bf16[512,2048]{1,0:T(8,128)(2,1)} %copy-done.110, ...), custom_call_target="tpu_custom_call" | custom-call | flops 7500000256 | bytes 1706112 | tf_op jit(solution)/shard_map/pallas_call | solution.py:51
  942.0 34.6 %shard_map.214 = (bf16[4,2,128,512]{3,2,1,0:T(8,128)(2,1)S(1)}, bf16[16,128,128]{2,1,0:T(8,128)(2,1)S(1)}, bf16[16,128,128]{2,1,0:T(8,128)(2,1)S(1)}) custom-call(s32[32]{0:T(128)S(1)} %fusion.41.loc_ref, s32[4]{0:T(128)S(1)} %pad_add_fusion.pos_ref, bf16[4,2,128,512]{3,2,1,0:T(8,128)(2,1)S(1)} %copy-done.99, bf16[4,2,128,512]{3,2,1,0:T(8,128)(2,1)S(1)} %bitcast.222, ...), custom_call_target="tpu_custom_call" | custom-call | flops 4823449600 | bytes 1118226 | tf_op jit(solution)/shard_map/pallas_call | solution.py:51
  985.5 34.2 %shard_map.215 = (bf16[4,2,128,512]{3,2,1,0:T(8,128)(2,1)S(1)}, bf16[16,128,128]{2,1,0:T(8,128)(2,1)S(1)}, bf16[16,128,128]{2,1,0:T(8,128)(2,1)S(1)}) custom-call(s32[32]{0:T(128)S(1)} %fusion.41.loc_ref, s32[4]{0:T(128)S(1)} %pad_add_fusion.pos_ref, bf16[4,2,128,512]{3,2,1,0:T(8,128)(2,1)S(1)} %copy-done.99, ...), custom_call_target="tpu_custom_call", output_to_operand_aliasing={{0}: (9, {})} | custom-call | flops 4823449600 | bytes 1118226 | tf_op jit(solution)/shard_map/pallas_call | solution.py:51
  1050.8 9.6 collective-permute-done.47
  1060.3 12.5 collective-permute-done.48
  1091.7 85.7 %shard_map.219 = (bf16[256,2048]{1,0:T(8,128)(2,1)S(1)}, bf16[256,2048]{1,0:T(8,128)(2,1)S(1)}, bf16[256,2048]{1,0:T(8,128)(2,1)S(1)}, bf16[256,2048]{1,0:T(8,12...) custom-call(bf16[512,2048]{1,0:T(8,128)(2,1)} %copy-done.88, bf16[512,2048]{1,0:T(8,128)(2,1)} %copy-done.89, ...), custom_call_target="tpu_custom_call" | custom-call | flops 7500000256 | bytes 1444992 | tf_op jit(solution)/shard_map/pallas_call | solution.py:51
  1190.9 11.3 shard_map.220
  1202.2 13.6 shard_map.221
  1215.9 11.1 shard_map.222
  1227.0 11.5 shard_map.223
  1238.5 20.3 %shard_map.224 = (bf16[512,2048]{1,0:T(8,128)(2,1)S(1)}, bf16[512,2048]{1,0:T(8,128)(2,1)S(1)}) custom-call(bf16[1024,1408]{1,0:T(8,128)(2,1)} %get-tuple-element.410.refs_4_.refs_0_, bf16[1024,1408]{1,0:T(8,128)(2,1)} %get-tuple-element.408.refs_4_.refs_1_, bf16[1024,1408]{1,0:T(8,128)(2,1)} %all-gather.11.cloned.1.call-done.refs_4_.refs_2_, ...), custom_call_target="tpu_custom_call" | custom-call | flops 11811160064 | bytes 21495808 | tf_op jit(solution)/shard_map/pallas_call | solution.py:51
  1271.4 57.6 %shard_map.225 = (bf16[256,2048]{1,0:T(8,128)(2,1)S(1)}, bf16[256,2048]{1,0:T(8,128)(2,1)S(1)}, bf16[256,2048]{1,0:T(8,128)(2,1)S(1)}, bf16[256,2048]{1,0:T(8,12...) custom-call(bf16[512,2048]{1,0:T(8,128)(2,1)} %copy-done.107, bf16[512,2048]{1,0:T(8,128)(2,1)} %copy-done.108, ...), custom_call_target="tpu_custom_call" | custom-call | flops 7500000256 | bytes 1706112 | tf_op jit(solution)/shard_map/pallas_call | solution.py:51
  1347.8 34.5 %shard_map.227 = (bf16[4,2,128,512]{3,2,1,0:T(8,128)(2,1)S(1)}, bf16[16,128,128]{2,1,0:T(8,128)(2,1)S(1)}, bf16[16,128,128]{2,1,0:T(8,128)(2,1)S(1)}) custom-call(s32[32]{0:T(128)S(1)} %fusion.41.loc_ref, s32[4]{0:T(128)S(1)} %pad_add_fusion.pos_ref, bf16[4,2,128,512]{3,2,1,0:T(8,128)(2,1)S(1)} %copy-done.93, bf16[4,2,128,512]{3,2,1,0:T(8,128)(2,1)S(1)} %bitcast.220, ...), custom_call_target="tpu_custom_call" | custom-call | flops 4823449600 | bytes 1118226 | tf_op jit(solution)/shard_map/pallas_call | solution.py:51
  1390.4 9.0 collective-permute-done.53
  1400.0 35.0 %shard_map.228 = (bf16[4,2,128,512]{3,2,1,0:T(8,128)(2,1)S(1)}, bf16[16,128,128]{2,1,0:T(8,128)(2,1)}, bf16[16,128,128]{2,1,0:T(8,128)(2,1)S(1)}) custom-call(s32[32]{0:T(128)S(1)} %fusion.41.loc_ref, s32[4]{0:T(128)S(1)} %pad_add_fusion.pos_ref, bf16[4,2,128,512]{3,2,1,0:T(8,128)(2,1)S(1)} %copy-done.93, ...), custom_call_target="tpu_custom_call", output_to_operand_aliasing={{0}: (9, {})} | custom-call | flops 4823449600 | bytes 1118226 | tf_op jit(solution)/shard_map/pallas_call | solution.py:51
  1489.8 9.1 shard_map.231
  1500.3 39.8 %shard_map.232 = (bf16[256,2048]{1,0:T(8,128)(2,1)S(1)}, f32[1,2048]{1,0:T(1,128)}, f32[1,2048]{1,0:T(1,128)S(1)}, bf16[4,256,640]{2,1,0:T(8,128)(2,1)S(1)}) custom-call(bf16[512,2048]{1,0:T(8,128)(2,1)S(1)} %copy-done.86, bf16[512,2048]{1,0:T(8,128)(2,1)} %copy-done.87, f32[256,2048]{1,0:T(8,128)} %get-tuple-element.475.refs_2_, f32[1,2048]{1,0:T(1,128)S(1)} %copy-done.78, ...), custom_call_target="tpu_custom_call" | custom-call | flops 7500000256 | bytes 1510528 | tf_op jit(solution)/shard_map/pallas_call | solution.py:51
  1559.8 33.7 %collective-permute-done.69 = bf16[256,640]{1,0:T(8,128)(2,1)} collective-permute-done((bf16[256,640]{1,0:T(8,128)(2,1)}, bf16[256,640]{1,0:T(8,128)(2,1)}, u32[]{:S(2)}, u32[]{:S(2)}) %collective-permute-start.69) | collective-permute-done | bytes 327712 | tf_op jit(solution)/shard_map/ppermute | solution.py:23
  1600.9 36.2 %collective-permute-start.70 = (bf16[256,640]{1,0:T(8,128)(2,1)}, bf16[256,640]{1,0:T(8,128)(2,1)}, u32[]{:S(2)}, u32[]{:S(2)}) collective-permute-start(bf16[256,640]{1,0:T(8,128)(2,1)} %get-tuple-element.537), channel_id=1, source_target_pairs={{0,8},{2,10},{4,12},{6,14},{8,0},{10,2},{12,4},{14,6},{1,9},{3,11}... | collective-permute-start | bytes 983048 | tf_op jit(solution)/shard_map/ppermute | solution.py:23
  1642.3 20.8 %collective-permute-done.70 = bf16[256,640]{1,0:T(8,128)(2,1)} collective-permute-done((bf16[256,640]{1,0:T(8,128)(2,1)}, bf16[256,640]{1,0:T(8,128)(2,1)}, u32[]{:S(2)}, u32[]{:S(2)}) %collective-permute-start.70) | collective-permute-done | bytes 327712 | tf_op jit(solution)/shard_map/ppermute | solution.py:23
  (663 shorter events, 463.2 us)
Async XLA Ops:
  7.2 138.5 %all-gather.9.cloned.1.call-start = ((), (), s32[]{:S(2)}) async-start(), calls=%async_computation.8 | async-start | bytes 5308416 | tf_op jit(solution)/shard_map/all_gather | solution.py:1012
  31.6 187.5 %all-gather.11.cloned.1.call-start = ((), (), s32[]{:S(2)}) async-start(), calls=%async_computation.9 | async-start | bytes 3604480 | tf_op jit(solution)/shard_map/all_gather | solution.py:77
  53.0 239.5 %all-gather.13.cloned.1.call-start = ((), (), s32[]{:S(2)}) async-start(), calls=%async_computation.10 | async-start | bytes 3604480 | tf_op jit(solution)/shard_map/all_gather | solution.py:77
  125.9 228.7 %all-gather.15.cloned.1.call-start = ((), (), s32[]{:S(2)}) async-start(), calls=%async_computation.11 | async-start | bytes 3604480 | tf_op jit(solution)/shard_map/all_gather | solution.py:77
  157.0 262.5 %all-gather.17.cloned.1.call-start = ((), (), s32[]{:S(2)}) async-start(), calls=%async_computation.12 | async-start | bytes 3604480 | tf_op jit(solution)/shard_map/all_gather | solution.py:77
  219.1 303.3 %all-gather.19.cloned.1.call-start = ((), (), s32[]{:S(2)}) async-start(), calls=%async_computation.13 | async-start | bytes 5308416 | tf_op jit(solution)/shard_map/all_gather | solution.py:1012
  219.7 376.8 %all-gather.21.cloned.1.call-start = ((), (), s32[]{:S(2)}) async-start(), calls=%async_computation.14 | async-start | bytes 3604480 | tf_op jit(solution)/shard_map/all_gather | solution.py:77
  220.0 63.1 %collective-permute-start.14 = (bf16[1024,1408]{1,0:T(8,128)(2,1)}, bf16[1024,1408]{1,0:T(8,128)(2,1)S(1)}, u32[]{:S(2)}, u32[]{:S(2)}) collective-permute-start(bf16[1024,1408]{1,0:T(8,128)(2,1)} %all-gather.11.cloned.1.call-done.refs_4_.refs_2_), channel_id=1, source_target_pairs={{0,2},{2,0},{4,6},{6,4},{8,10},{10,8},{12,14},{14,12},{1,3},{3,1},... | collective-permute-start | bytes 8650760 | tf_op jit(solution)/shard_map/ppermute | solution.py:23
  292.5 62.2 %collective-permute-start.17 = (bf16[1024,1408]{1,0:T(8,128)(2,1)}, bf16[1024,1408]{1,0:T(8,128)(2,1)}, u32[]{:S(2)}, u32[]{:S(2)}) collective-permute-start(bf16[1024,1408]{1,0:T(8,128)(2,1)} %all-gather.13.cloned.1.call-done.refs_6_.refs_4_), channel_id=1, source_target_pairs={{0,2},{2,0},{4,6},{6,4},{8,10},{10,8},{12,14},{14,12},{1,3},{3,1},... | collective-permute-start | bytes 8650760 | tf_op jit(solution)/shard_map/ppermute | solution.py:23
  354.7 78.9 %collective-permute-start.20 = (bf16[1024,1408]{1,0:T(8,128)(2,1)}, bf16[1024,1408]{1,0:T(8,128)(2,1)}, u32[]{:S(2)}, u32[]{:S(2)}) collective-permute-start(bf16[1024,1408]{1,0:T(8,128)(2,1)} %all-gather.15.cloned.1.call-done.refs_1_.refs_4_), channel_id=1, source_target_pairs={{0,2},{2,0},{4,6},{6,4},{8,10},{10,8},{12,14},{14,12},{1,3},{3,1},... | collective-permute-start | bytes 8650760 | tf_op jit(solution)/shard_map/ppermute | solution.py:23
  361.0 288.2 %all-gather.23.cloned.1.call-start = ((), (), s32[]{:S(2)}) async-start(), calls=%async_computation.15 | async-start | bytes 3604480 | tf_op jit(solution)/shard_map/all_gather | solution.py:77
  433.6 88.8 %collective-permute-start.21 = (bf16[1024,1408]{1,0:T(8,128)(2,1)}, bf16[1024,1408]{1,0:T(8,128)(2,1)}, u32[]{:S(2)}, u32[]{:S(2)}) collective-permute-start(bf16[1024,1408]{1,0:T(8,128)(2,1)} %all-gather.17.cloned.1.call-done.refs_4_.refs_2_), channel_id=1, source_target_pairs={{0,2},{2,0},{4,6},{6,4},{8,10},{10,8},{12,14},{14,12},{1,3},{3,1},... | collective-permute-start | bytes 8650760 | tf_op jit(solution)/shard_map/ppermute | solution.py:23
  538.1 49.9 %collective-permute-start.25 = (bf16[4,2,128,128]{3,2,1,0:T(8,128)(2,1)}, bf16[4,2,128,128]{3,2,1,0:T(8,128)(2,1)}, u32[]{:S(2)}, u32[]{:S(2)}) collective-permute-start(bf16[4,2,128,128]{3,2,1,0:T(8,128)(2,1)} %get-tuple-element.287), channel_id=1, source_target_pairs={{0,8},{2,10},{4,12},{6,14},{8,0},{10,2},{12,4},{14,6},{1,9},{3,11}... | collective-permute-start | bytes 786440 | tf_op jit(solution)/shard_map/ppermute | solution.py:23
  539.8 48.4 %collective-permute-start.22 = (bf16[4,2,128,128]{3,2,1,0:T(8,128)(2,1)}, bf16[4,2,128,128]{3,2,1,0:T(8,128)(2,1)}, u32[]{:S(2)}, u32[]{:S(2)}) collective-permute-start(bf16[4,2,128,128]{3,2,1,0:T(8,128)(2,1)} %get-tuple-element.287), channel_id=1, source_target_pairs={{0,2},{2,0},{4,6},{6,4},{8,10},{10,8},{12,14},{14,12},{1,3},{3,1},... | collective-permute-start | bytes 786440 | tf_op jit(solution)/shard_map/ppermute | solution.py:23
  540.3 387.2 %reduce-scatter.9.cloned.1.call-start = ((), (), s32[]{:S(2)}) async-start(), calls=%async_computation.16 | async-start | bytes 3604480 | tf_op jit(solution)/shard_map/reduce_scatter | solution.py:81
  596.5 61.4 %collective-permute-start.29 = (bf16[1024,1408]{1,0:T(8,128)(2,1)}, bf16[1024,1408]{1,0:T(8,128)(2,1)}, u32[]{:S(2)}, u32[]{:S(2)}) collective-permute-start(bf16[1024,1408]{1,0:T(8,128)(2,1)} %all-gather.21.cloned.1.call-done.refs_6_.refs_4_), channel_id=1, source_target_pairs={{0,2},{2,0},{4,6},{6,4},{8,10},{10,8},{12,14},{14,12},{1,3},{3,1},... | collective-permute-start | bytes 8650760 | tf_op jit(solution)/shard_map/ppermute | solution.py:23
  667.1 60.2 %collective-permute-start.30 = (bf16[1024,1408]{1,0:T(8,128)(2,1)S(1)}, bf16[1024,1408]{1,0:T(8,128)(2,1)S(1)}, u32[]{:S(2)}, u32[]{:S(2)}) collective-permute-start(bf16[1024,1408]{1,0:T(8,128)(2,1)S(1)} %copy-done.123), channel_id=1, source_target_pairs={{0,2},{2,0},{4,6},{6,4},{8,10},{10,8},{12,14},{14,12},{1,3},{3,1},... | collective-permute-start | bytes 8650760 | tf_op jit(solution)/shard_map/ppermute | solution.py:23
  766.8 58.1 %collective-permute-start.36 = (bf16[2,128,2048]{2,1,0:T(8,128)(2,1)S(1)}, bf16[2,128,2048]{2,1,0:T(8,128)(2,1)}, u32[]{:S(2)}, u32[]{:S(2)}) collective-permute-start(bf16[2,128,2048]{2,1,0:T(8,128)(2,1)S(1)} %bitcast.229), channel_id=1, source_target_pairs={{16,0},{17,15},{18,2},{19,13},{20,4},{21,11},{22,6},{23,9},{24,8},... | collective-permute-start | bytes 3145736 | tf_op jit(solution)/shard_map/ppermute | solution.py:116
  768.1 56.8 %collective-permute-start.35 = (bf16[2,128,2048]{2,1,0:T(8,128)(2,1)S(1)}, bf16[2,128,2048]{2,1,0:T(8,128)(2,1)}, u32[]{:S(2)}, u32[]{:S(2)}) collective-permute-start(bf16[2,128,2048]{2,1,0:T(8,128)(2,1)S(1)} %bitcast.230), channel_id=1, source_target_pairs={{0,0},{1,15},{2,2},{3,13},{4,4},{5,11},{6,6},{7,9},{8,8},{9,7},{10... | collective-permute-start | bytes 3145736 | tf_op jit(solution)/shard_map/ppermute | solution.py:116
  784.6 74.8 %collective-permute-start.37 = (bf16[4,256,1408]{2,1,0:T(8,128)(2,1)}, bf16[4,256,1408]{2,1,0:T(8,128)(2,1)}, u32[]{:S(2)}, u32[]{:S(2)}) collective-permute-start(bf16[4,256,1408]{2,1,0:T(8,128)(2,1)} %get-tuple-element.311), channel_id=1, source_target_pairs={{0,2},{2,0},{4,6},{6,4},{8,10},{10,8},{12,14},{14,12},{1,3},{3,1},... | collective-permute-start | bytes 8650760 | tf_op jit(solution)/shard_map/ppermute | solution.py:23
  786.2 42.0 %collective-permute-start.34 = (bf16[256,2048]{1,0:T(8,128)(2,1)S(1)}, bf16[256,2048]{1,0:T(8,128)(2,1)}, u32[]{:S(2)}, u32[]{:S(2)}) collective-permute-start(bf16[256,2048]{1,0:T(8,128)(2,1)S(1)} %add_convert_fusion.10), channel_id=1, source_target_pairs={{0,16},{16,0},{1,17},{17,1},{2,18},{18,2},{3,19},{19,3},{4,20},{20... | collective-permute-start | bytes 3145736 | tf_op jit(solution)/shard_map/ppermute | solution.py:23
  863.5 159.7 %reduce-scatter.11.cloned.1.call-start = ((), (), s32[]{:S(2)}) async-start(), calls=%async_computation.17 | async-start | bytes 3604480 | tf_op jit(solution)/shard_map/reduce_scatter | solution.py:81
  863.5 64.0 %collective-permute-start.38 = (bf16[4,256,1408]{2,1,0:T(8,128)(2,1)}, bf16[4,256,1408]{2,1,0:T(8,128)(2,1)}, u32[]{:S(2)}, u32[]{:S(2)}) collective-permute-start(bf16[4,256,1408]{2,1,0:T(8,128)(2,1)} %get-tuple-element.341), channel_id=1, source_target_pairs={{0,2},{2,0},{4,6},{6,4},{8,10},{10,8},{12,14},{14,12},{1,3},{3,1},... | collective-permute-start | bytes 8650760 | tf_op jit(solution)/shard_map/ppermute | solution.py:23
  932.4 248.9 %reduce-scatter.13.cloned.1.call-start = ((), (), s32[]{:S(2)}) async-start(), calls=%async_computation.18 | async-start | bytes 3604480 | tf_op jit(solution)/shard_map/reduce_scatter | solution.py:81
  932.5 90.7 %collective-permute-start.39 = (bf16[4,256,1408]{2,1,0:T(8,128)(2,1)}, bf16[4,256,1408]{2,1,0:T(8,128)(2,1)}, u32[]{:S(2)}, u32[]{:S(2)}) collective-permute-start(bf16[4,256,1408]{2,1,0:T(8,128)(2,1)} %get-tuple-element.346), channel_id=1, source_target_pairs={{0,2},{2,0},{4,6},{6,4},{8,10},{10,8},{12,14},{14,12},{1,3},{3,1},... | collective-permute-start | bytes 8650760 | tf_op jit(solution)/shard_map/ppermute | solution.py:23
  976.6 45.7 %collective-permute-start.40 = (bf16[4,4,128,128]{3,2,1,0:T(8,128)(2,1)S(1)}, bf16[4,4,128,128]{3,2,1,0:T(8,128)(2,1)S(1)}, u32[]{:S(2)}, u32[]{:S(2)}) collective-permute-start(bf16[4,4,128,128]{3,2,1,0:T(8,128)(2,1)S(1)} %bitcast.235), channel_id=1, source_target_pairs={{0,2},{2,0},{4,6},{6,4},{8,10},{10,8},{12,14},{14,12},{1,3},{3,1},... | collective-permute-start | bytes 1572872 | tf_op jit(solution)/shard_map/ppermute | solution.py:23
  978.0 58.2 %collective-permute-start.42 = (bf16[2,128,2048]{2,1,0:T(8,128)(2,1)}, bf16[2,128,2048]{2,1,0:T(8,128)(2,1)}, u32[]{:S(2)}, u32[]{:S(2)}) collective-permute-start(bf16[2,128,2048]{2,1,0:T(8,128)(2,1)} %bitcast.38), channel_id=1, source_target_pairs={{16,16},{17,31},{18,18},{19,29},{20,20},{21,27},{22,22},{23,25},{2... | collective-permute-start | bytes 3145736 | tf_op jit(solution)/shard_map/ppermute | solution.py:116
  979.7 57.8 %collective-permute-start.41 = (bf16[2,128,2048]{2,1,0:T(8,128)(2,1)}, bf16[2,128,2048]{2,1,0:T(8,128)(2,1)}, u32[]{:S(2)}, u32[]{:S(2)}) collective-permute-start(bf16[2,128,2048]{2,1,0:T(8,128)(2,1)} %bitcast.38), channel_id=1, source_target_pairs={{0,16},{1,31},{2,18},{3,29},{4,20},{5,27},{6,22},{7,25},{8,24},{9,... | collective-permute-start | bytes 3145736 | tf_op jit(solution)/shard_map/ppermute | solution.py:116
  1030.7 238.1 %reduce-scatter.15.cloned.1.call-start = ((), (), s32[]{:S(2)}) async-start(), calls=%async_computation.19 | async-start | bytes 2949120 | tf_op jit(solution)/shard_map/reduce_scatter | solution.py:81
  1090.4 91.0 %collective-permute-start.50 = (bf16[4,256,1152]{2,1,0:T(8,128)(2,1)S(1)}, bf16[4,256,1152]{2,1,0:T(8,128)(2,1)}, u32[]{:S(2)}, u32[]{:S(2)}) collective-permute-start(bf16[4,256,1152]{2,1,0:T(8,128)(2,1)S(1)} %pad_maximum_fusion), channel_id=1, source_target_pairs={{0,2},{2,0},{4,6},{6,4},{8,10},{10,8},{12,14},{14,12},{1,3},{3,1},... | collective-permute-start | bytes 7077896 | tf_op jit(solution)/shard_map/ppermute | solution.py:23
  1185.7 146.4 %reduce-scatter.17.cloned.1.call-start = ((), (), s32[]{:S(2)}) async-start(), calls=%async_computation.20 | async-start | bytes 3604480 | tf_op jit(solution)/shard_map/reduce_scatter | solution.py:81
  1202.2 64.1 %collective-permute-start.51 = (bf16[4,256,1408]{2,1,0:T(8,128)(2,1)}, bf16[4,256,1408]{2,1,0:T(8,128)(2,1)S(1)}, u32[]{:S(2)}, u32[]{:S(2)}) collective-permute-start(bf16[4,256,1408]{2,1,0:T(8,128)(2,1)} %get-tuple-element.395), channel_id=1, source_target_pairs={{0,2},{2,0},{4,6},{6,4},{8,10},{10,8},{12,14},{14,12},{1,3},{3,1},... | collective-permute-start | bytes 8650760 | tf_op jit(solution)/shard_map/ppermute | solution.py:23
  1268.6 170.4 %reduce-scatter.19.cloned.1.call-start = ((), (), s32[]{:S(2)}) async-start(), calls=%async_computation.21 | async-start | bytes 3604480 | tf_op jit(solution)/shard_map/reduce_scatter | solution.py:81
  1268.7 63.4 %collective-permute-start.52 = (bf16[4,256,1408]{2,1,0:T(8,128)(2,1)}, bf16[4,256,1408]{2,1,0:T(8,128)(2,1)}, u32[]{:S(2)}, u32[]{:S(2)}) collective-permute-start(bf16[4,256,1408]{2,1,0:T(8,128)(2,1)} %get-tuple-element.422), channel_id=1, source_target_pairs={{0,2},{2,0},{4,6},{6,4},{8,10},{10,8},{12,14},{14,12},{1,3},{3,1},... | collective-permute-start | bytes 8650760 | tf_op jit(solution)/shard_map/ppermute | solution.py:23
  1337.1 344.1 %reduce-scatter.21.cloned.1.call-start = ((), (), s32[]{:S(2)}) async-start(), calls=%async_computation.22 | async-start | bytes 1310720 | tf_op jit(solution)/shard_map/reduce_scatter | solution.py:81
  1337.1 101.9 %collective-permute-start.54 = (bf16[4,256,1408]{2,1,0:T(8,128)(2,1)}, bf16[4,256,1408]{2,1,0:T(8,128)(2,1)}, u32[]{:S(2)}, u32[]{:S(2)}) collective-permute-start(bf16[4,256,1408]{2,1,0:T(8,128)(2,1)} %get-tuple-element.437), channel_id=1, source_target_pairs={{0,2},{2,0},{4,6},{6,4},{8,10},{10,8},{12,14},{14,12},{1,3},{3,1},... | collective-permute-start | bytes 8650760 | tf_op jit(solution)/shard_map/ppermute | solution.py:23
  1343.9 45.1 %collective-permute-start.63 = (bf16[256,1152]{1,0:T(8,128)(2,1)S(1)}, bf16[256,1152]{1,0:T(8,128)(2,1)S(1)}, u32[]{:S(2)}, u32[]{:S(2)}) collective-permute-start(bf16[256,1152]{1,0:T(8,128)(2,1)S(1)} %copy-done.144), channel_id=1, source_target_pairs={{0,16},{1,17},{2,18},{3,19},{4,20},{5,21},{6,22},{7,23},{8,24},{9,... | collective-permute-start | bytes 1769480 | tf_op jit(solution)/shard_map/ppermute | solution.py:27
  1383.6 53.2 %collective-permute-start.64 = (bf16[256,1408]{1,0:T(8,128)(2,1)S(1)}, bf16[256,1408]{1,0:T(8,128)(2,1)S(1)}, u32[]{:S(2)}, u32[]{:S(2)}) collective-permute-start(bf16[256,1408]{1,0:T(8,128)(2,1)S(1)} %copy-done.135), channel_id=1, source_target_pairs={{0,16},{1,17},{2,18},{3,19},{4,20},{5,21},{6,22},{7,23},{8,24},{9,... | collective-permute-start | bytes 2162696 | tf_op jit(solution)/shard_map/ppermute | solution.py:27
  1387.7 49.2 %collective-permute-start.65 = (bf16[256,1408]{1,0:T(8,128)(2,1)S(1)}, bf16[256,1408]{1,0:T(8,128)(2,1)S(1)}, u32[]{:S(2)}, u32[]{:S(2)}) collective-permute-start(bf16[256,1408]{1,0:T(8,128)(2,1)S(1)} %copy-done.137), channel_id=1, source_target_pairs={{0,16},{1,17},{2,18},{3,19},{4,20},{5,21},{6,22},{7,23},{8,24},{9,... | collective-permute-start | bytes 2162696 | tf_op jit(solution)/shard_map/ppermute | solution.py:27
  1389.0 47.8 %collective-permute-start.66 = (bf16[256,1408]{1,0:T(8,128)(2,1)S(1)}, bf16[256,1408]{1,0:T(8,128)(2,1)S(1)}, u32[]{:S(2)}, u32[]{:S(2)}) collective-permute-start(bf16[256,1408]{1,0:T(8,128)(2,1)S(1)} %copy-done.131), channel_id=1, source_target_pairs={{0,16},{1,17},{2,18},{3,19},{4,20},{5,21},{6,22},{7,23},{8,24},{9,... | collective-permute-start | bytes 2162696 | tf_op jit(solution)/shard_map/ppermute | solution.py:27
  1483.0 199.5 %reduce-scatter.23.cloned.1.call-start = ((), (), s32[]{:S(2)}) async-start(), calls=%async_computation.23 | async-start | bytes 3604480 | tf_op jit(solution)/shard_map/reduce_scatter | solution.py:81
  1540.1 124.3 %collective-permute-start.75 = (bf16[2,128,2048]{2,1,0:T(8,128)(2,1)S(1)}, bf16[2,128,2048]{2,1,0:T(8,128)(2,1)}, u32[]{:S(2)}, u32[]{:S(2)}) collective-permute-start(bf16[2,128,2048]{2,1,0:T(8,128)(2,1)S(1)} %bitcast.210), channel_id=1, source_target_pairs={{16,16},{17,31},{18,18},{19,29},{20,20},{21,27},{22,22},{23,25},{2... | collective-permute-start | bytes 3145736 | tf_op jit(solution)/shard_map/ppermute | solution.py:116
  1541.8 122.7 %collective-permute-start.74 = (bf16[2,128,2048]{2,1,0:T(8,128)(2,1)S(1)}, bf16[2,128,2048]{2,1,0:T(8,128)(2,1)}, u32[]{:S(2)}, u32[]{:S(2)}) collective-permute-start(bf16[2,128,2048]{2,1,0:T(8,128)(2,1)S(1)} %bitcast.211), channel_id=1, source_target_pairs={{0,16},{1,31},{2,18},{3,29},{4,20},{5,27},{6,22},{7,25},{8,24},{9,... | collective-permute-start | bytes 3145736 | tf_op jit(solution)/shard_map/ppermute | solution.py:116
  1553.1 40.4 %collective-permute-start.69 = (bf16[256,640]{1,0:T(8,128)(2,1)}, bf16[256,640]{1,0:T(8,128)(2,1)}, u32[]{:S(2)}, u32[]{:S(2)}) collective-permute-start(bf16[256,640]{1,0:T(8,128)(2,1)} %get-tuple-element.535), channel_id=1, source_target_pairs={{0,4},{2,6},{4,0},{6,2},{8,12},{10,14},{12,8},{14,10},{1,5},{3,7},... | collective-permute-start | bytes 983048 | tf_op jit(solution)/shard_map/ppermute | solution.py:23
  1553.1 47.8 %collective-permute-start.71 = (bf16[256,640]{1,0:T(8,128)(2,1)}, bf16[256,640]{1,0:T(8,128)(2,1)}, u32[]{:S(2)}, u32[]{:S(2)}) collective-permute-start(bf16[256,640]{1,0:T(8,128)(2,1)} %get-tuple-element.536), channel_id=1, source_target_pairs={{0,12},{2,14},{4,8},{6,10},{8,4},{10,6},{12,0},{14,2},{1,13},{3,15... | collective-permute-start | bytes 983048 | tf_op jit(solution)/shard_map/ppermute | solution.py:23
  1558.5 107.6 %collective-permute-start.73 = (bf16[2,128,2048]{2,1,0:T(8,128)(2,1)S(1)}, bf16[2,128,2048]{2,1,0:T(8,128)(2,1)}, u32[]{:S(2)}, u32[]{:S(2)}) collective-permute-start(bf16[2,128,2048]{2,1,0:T(8,128)(2,1)S(1)} %bitcast.231), channel_id=1, source_target_pairs={{16,0},{17,15},{18,2},{19,13},{20,4},{21,11},{22,6},{23,9},{24,8},... | collective-permute-start | bytes 3145736 | tf_op jit(solution)/shard_map/ppermute | solution.py:116
  1593.5 72.7 %collective-permute-start.72 = (bf16[2,128,2048]{2,1,0:T(8,128)(2,1)S(1)}, bf16[2,128,2048]{2,1,0:T(8,128)(2,1)}, u32[]{:S(2)}, u32[]{:S(2)}) collective-permute-start(bf16[2,128,2048]{2,1,0:T(8,128)(2,1)S(1)} %bitcast.232), channel_id=1, source_target_pairs={{0,0},{1,15},{2,2},{3,13},{4,4},{5,11},{6,6},{7,9},{8,8},{9,7},{10... | collective-permute-start | bytes 3145736 | tf_op jit(solution)/shard_map/ppermute | solution.py:116
  1600.9 62.2 %collective-permute-start.70 = (bf16[256,640]{1,0:T(8,128)(2,1)}, bf16[256,640]{1,0:T(8,128)(2,1)}, u32[]{:S(2)}, u32[]{:S(2)}) collective-permute-start(bf16[256,640]{1,0:T(8,128)(2,1)} %get-tuple-element.537), channel_id=1, source_target_pairs={{0,8},{2,10},{4,12},{6,14},{8,0},{10,2},{12,4},{14,6},{1,9},{3,11}... | collective-permute-start | bytes 983048 | tf_op jit(solution)/shard_map/ppermute | solution.py:23
  (216 other events, 2274.8 us)
Sparse Core Ops, SparseCore 0:
  31.8 97.0 all-gather.8
  130.9 66.3 all-gather.10
  198.9 65.4 all-gather.12
  265.8 57.8 all-gather.14
  325.1 74.2 all-gather.16
  401.5 106.8 all-gather.18
  510.0 79.7 all-gather.20
  591.4 57.7 all-gather.22
  863.6 51.8 reduce-scatter.8
  932.6 52.8 reduce-scatter.10
  1030.8 71.9 reduce-scatter.12
  1185.8 45.5 reduce-scatter.14
  1268.8 54.7 reduce-scatter.16
  1337.2 55.6 reduce-scatter.18
  1483.1 33.2 reduce-scatter.20
  1519.2 76.1 reduce-scatter.22
